TPU v7x, 256 devices: a whole 4x4x8 slice. The times are simulated.
256 devices in a mesh: dp: 16 (over x, y_lo, core), atom: 16 (over y_hi, z).
Axes of the slice: x: 4, y: 4 (y_hi: 2, y_lo: 2; y = y_hi * 2 + y_lo), z: 8, core: 2. Of those that a mesh axis runs over, the one named last changes fastest.
Arguments:
- node_feats: bfloat16 [16, 128, 2048], P('dp', None, 'atom'), may hold values from -6 to 6
- frac: float32 [16, 3, 2048], P('dp', None, 'atom'), may hold values from 0 to 1
- neighbours: int32 [16, 32, 2048], P('dp', None, 'atom'), may hold values from 0 to 2047, as said below
- images: int32 [16, 32, 2048], P('dp', None, 'atom'), may hold values from 0 to 26
- neighbour_count: int32 [16, 2048], P('dp', 'atom'), may hold values from 16 to 32, as said below
- atom_count: int32 [16], P('dp'), may hold values from 512 to 2048, as said below
- miller: int32 [3, 2048], replicated, may hold values from -6 to 6
- in_weight: bfloat16 [128, 128], replicated, may hold values from -0.5 to 0.5
- radial_weight: float32 [3, 8, 128], replicated, may hold values from -6 to 6
- out_weight: bfloat16 [384, 128], replicated, may hold values from -0.3125 to 0.3125
- filter_weight: float32 [2048, 128], replicated, may hold values from -6 to 6
- cotangent: bfloat16 [16, 128, 2048], P('dp', None, 'atom'), may hold values from -6 to 6
Outputs:
- updated: bfloat16 [16, 128, 2048], P('dp', None, 'atom')
- grad_filter: float32 [2048, 128], P('atom')
- grad_in: float32 [128, 128], replicated
- grad_out: float32 [384, 128], replicated
Inputs may be any that keep to these rules, and one draw needn't show every extreme that they name: `neighbours`: the neighbour in any slot of atom g is (g + o) mod 2048 with 1 <= |o| <= 32. `neighbour_count`: atom 0 of every structure uses all 32 slots. Atoms 0 to atom_count - 1 are real, the rest are padding; some structure is full.
All inputs are finite; a program needn't handle non-finite values.
Results may differ from a plain program's by a relative error of at most 0.02.
Values may be sent and summed in bfloat16 or wider, within the bound.
No kernel may reach another device: no remote copies, remote signals or barrier semaphores. Data moves between devices by JAX's collectives and lax.ppermute only.
A program may use at most 128 MiB of HBM per device.

v0:
```python
import math

import jax
import jax.numpy as jnp
from jax import lax
from jax.sharding import PartitionSpec as P

GHOST = 32


two_pi = 2.0 * math.pi
maximum_degree = lax.Precision.HIGHEST
contract_last = (((1,), (1,)), ((), ()))
contract_first = (((0,), (0,)), ((), ()))


def padded(cells, sides, width):
    for axis, dim in sides:
        count = lax.axis_size(axis)
        head = lax.slice_in_dim(cells, 0, width, axis=dim)
        tail = lax.slice_in_dim(cells, cells.shape[dim] - width, cells.shape[dim], axis=dim)
        cells = jnp.concatenate(
            [
                lax.ppermute(tail, axis, [(i, (i + 1) % count) for i in range(count)]),
                cells,
                lax.ppermute(head, axis, [((i + 1) % count, i) for i in range(count)]),
            ],
            axis=dim,
        )
    return cells


def harmonics(vector_feature):
    along_x, along_y, along_z = (vector_feature[0], vector_feature[1], vector_feature[2])
    square = along_x * along_x + along_y * along_y + along_z * along_z
    root_three = math.sqrt(3.0)
    root_fifteen = math.sqrt(15.0)
    root_five = math.sqrt(5.0)
    spherical_harmonic = jnp.stack(
        [
            jnp.ones_like(along_x),
            root_three * along_x,
            root_three * along_y,
            root_three * along_z,
            root_fifteen * along_x * along_y,
            root_fifteen * along_y * along_z,
            0.5 * root_five * (3.0 * along_z * along_z - square),
            root_fifteen * along_x * along_z,
            0.5 * root_fifteen * (along_x * along_x - along_y * along_y),
        ]
    )
    return (spherical_harmonic, square)


def edge_terms(frac_own, frac_ext, slot_index, image_codes, radial_weight):
    others = jnp.take(frac_ext, slot_index, axis=1)
    shifts = (
        jnp.stack([image_codes // 9, image_codes // 3 % 3, image_codes % 3]).astype(jnp.float32)
        - 1.0
    )
    vector_feature = 0.5 * (others - frac_own[:, None, :] + shifts)
    spherical_harmonic, square = harmonics(vector_feature)
    length = jnp.sqrt(square)
    basis_count = radial_weight.shape[1]
    spacing = 1.75 / (basis_count - 1)
    centres = jnp.arange(basis_count, dtype=jnp.float32) * spacing
    gauss_basis = jnp.exp(-jnp.square((length[None] - centres[:, None, None]) / spacing))
    radial = jnp.einsum("lnc,nea->lcea", radial_weight, gauss_basis, precision=maximum_degree)
    return (spherical_harmonic, radial)


def edge_sum(spherical_harmonic, radial, weighted):
    edge_message = radial * weighted[None]
    scalar_part = jnp.einsum(
        "ea,cea->ca", spherical_harmonic[0], edge_message[0], precision=maximum_degree
    )
    vector_component = jnp.einsum(
        "osf,xsf->oxf", spherical_harmonic[1:4], edge_message[1], precision=maximum_degree
    )
    tensor_component = jnp.einsum(
        "osf,xsf->oxf", spherical_harmonic[4:9], edge_message[2], precision=maximum_degree
    )
    return jnp.concatenate([scalar_part[None], vector_component, tensor_component], axis=0)


def spread_back(spherical_harmonic, radial, incoming_gradient):
    scalar_part = jnp.einsum(
        "ea,ca->cea", spherical_harmonic[0], incoming_gradient[0], precision=maximum_degree
    )
    vector_component = jnp.einsum(
        "ftl,fjl->jtl", spherical_harmonic[1:4], incoming_gradient[1:4], precision=maximum_degree
    )
    tensor_component = jnp.einsum(
        "ftl,fjl->jtl", spherical_harmonic[4:9], incoming_gradient[4:9], precision=maximum_degree
    )
    return radial[0] * scalar_part + radial[1] * vector_component + radial[2] * tensor_component


def invariants(features):
    squared = features * features
    return jnp.concatenate(
        [
            squared[0],
            squared[1] + squared[2] + squared[3],
            squared[4] + squared[5] + squared[6] + squared[7] + squared[8],
        ],
        axis=0,
    )


def widen_grad(inv_grad, features):
    channels = features.shape[1]
    repeated = jnp.concatenate(
        [inv_grad[:channels][None]]
        + [inv_grad[channels : 2 * channels][None]] * 3
        + [inv_grad[2 * channels :][None]] * 5,
        axis=0,
    )
    return 2.0 * features * repeated


def phases(miller, frac):
    factor = miller.astype(jnp.float32)
    argument = (
        factor[0][:, None] * frac[0][None]
        + factor[1][:, None] * frac[1][None]
        + factor[2][:, None] * frac[2][None]
    )
    angles = two_pi * argument
    return (jnp.cos(angles), jnp.sin(angles))


def spectrum(values, cos_table, sin_table):
    wide_values = values.astype(jnp.float32)
    real_part = lax.dot_general(wide_values, cos_table, contract_last, precision=maximum_degree)
    imag_part = lax.dot_general(wide_values, sin_table, contract_last, precision=maximum_degree)
    return (real_part, imag_part)


def project(real_coef, imag_coef, cos_table, sin_table):
    return jnp.dot(real_coef, cos_table, precision=maximum_degree) + jnp.dot(
        imag_coef, sin_table, precision=maximum_degree
    )


def shards(
    node_feats,
    frac,
    neighbours,
    images,
    neighbour_count,
    atom_count,
    miller,
    in_weight,
    radial_weight,
    out_weight,
    filter_weight,
    cotangent,
):
    own_feats = node_feats[0]
    own_frac = frac[0]
    slots_all = neighbours[0]
    codes_all = images[0]
    slot_count = neighbour_count[0]
    atoms_live = atom_count[0]
    cot_own = cotangent[0]
    channels, row_count = own_feats.shape
    slot_total = slots_all.shape[0]
    groups = lax.axis_size("atom")
    place_index = lax.axis_index("atom")
    total_atoms = row_count * groups
    first_row = place_index * row_count
    ext_feats, ext_frac = (
        padded(node_feats, (("atom", 2),), GHOST),
        padded(frac.astype(jnp.bfloat16), (("atom", 2),), GHOST).astype(frac.dtype),
    )
    ext_feats = ext_feats[0]
    ext_frac = ext_frac[0]
    ext_global = (
        first_row - GHOST + jnp.arange(row_count + 2 * GHOST, dtype=jnp.int32)
    ) % total_atoms
    live_ext = (ext_global < atoms_live).astype(jnp.float32)
    live_own = live_ext[GHOST : GHOST + row_count]
    hidden_ext = (
        lax.dot_general(in_weight, ext_feats, contract_first, preferred_element_type=jnp.float32)
        * live_ext[None]
    ).astype(jnp.bfloat16)
    hidden_own = hidden_ext[:, GHOST : GHOST + row_count]
    masked_cot = cot_own * live_own.astype(jnp.bfloat16)[None]
    kcount = filter_weight.shape[0]
    kshare = kcount // groups
    scale = 1.0 / math.sqrt(kcount * total_atoms)
    filt_t = filter_weight.T
    cos_table, sin_table = phases(miller, own_frac)
    s_real, s_imag = spectrum(hidden_own, cos_table, sin_table)
    g_real, g_imag = spectrum(masked_cot, cos_table, sin_table)
    s_real, s_imag, g_real, g_imag = lax.psum((s_real, s_imag, g_real, g_imag), "atom")
    full_grad = (scale * (s_real * g_real + s_imag * g_imag)).T
    grad_filter = lax.dynamic_slice_in_dim(full_grad, place_index * kshare, kshare, 0)
    ewald = project(scale * filt_t * s_real, scale * filt_t * s_imag, cos_table, sin_table)
    grad_ewald = project(scale * filt_t * g_real, scale * filt_t * g_imag, cos_table, sin_table)
    slot_local = (slots_all - first_row + GHOST) % total_atoms
    slot_ids = jnp.arange(slot_total, dtype=jnp.int32)[:, None]
    edge_weight = (
        (slot_ids < slot_count[None]).astype(jnp.float32) * live_own[None] * slot_total ** (-0.5)
    )
    hidden_float = hidden_ext.astype(jnp.float32)
    features = jnp.zeros((9, channels, row_count), jnp.float32)
    for offset in range(0, slot_total, 8):
        block_slots = slot_local[offset : offset + 8]
        spherical_harmonic, radial = edge_terms(
            own_frac, ext_frac, block_slots, codes_all[offset : offset + 8], radial_weight
        )
        weighted = (
            jnp.take(hidden_float, block_slots, axis=1) * edge_weight[offset : offset + 8][None]
        )
        features = features + edge_sum(spherical_harmonic, radial, weighted)
    inv_round = invariants(features).astype(jnp.bfloat16)
    local_out = lax.dot_general(
        out_weight, inv_round, contract_first, preferred_element_type=jnp.float32
    )
    updated = ((own_feats.astype(jnp.float32) + local_out + ewald) * live_own[None]).astype(
        jnp.bfloat16
    )
    inv_grad = jnp.dot(out_weight, masked_cot, preferred_element_type=jnp.float32)
    incoming_gradient = widen_grad(inv_grad, features)
    grad_hidden = jnp.zeros((channels, row_count + 2 * GHOST), jnp.float32)
    for offset in range(0, slot_total, 8):
        block_slots = slot_local[offset : offset + 8]
        spherical_harmonic, radial = edge_terms(
            own_frac, ext_frac, block_slots, codes_all[offset : offset + 8], radial_weight
        )
        pulled = (
            spread_back(spherical_harmonic, radial, incoming_gradient)
            * edge_weight[offset : offset + 8][None]
        )
        grad_hidden = grad_hidden.at[:, block_slots.reshape(-1)].add(pulled.reshape(channels, -1))
    grad_hidden = grad_hidden.at[:, GHOST : GHOST + row_count].add(grad_ewald)
    grad_hidden = grad_hidden * live_ext[None]
    grad_in = lax.dot_general(
        ext_feats.astype(jnp.float32), grad_hidden, contract_last, precision=maximum_degree
    )
    grad_out = lax.dot_general(
        inv_round, masked_cot, contract_last, preferred_element_type=jnp.float32
    )
    grad_in, grad_out = lax.psum((grad_in, grad_out), ("dp", "atom"))
    grad_filter = lax.psum(grad_filter, "dp")
    return (updated[None], grad_filter, grad_in, grad_out)


def solution(mesh):
    return jax.shard_map(
        shards,
        mesh=mesh,
        in_specs=(
            P("dp", None, "atom"),
            P("dp", None, "atom"),
            P("dp", None, "atom"),
            P("dp", None, "atom"),
            P("dp", "atom"),
            P("dp"),
            P(),
            P(),
            P(),
            P(),
            P(),
            P("dp", None, "atom"),
        ),
        out_specs=(P("dp", None, "atom"), P("atom", None), P(), P()),
        check_vma=False,
    )
```

profile of v0, /device:TPU:1, one launch (start us, length us, event | category | flops | bytes accessed | tf_op | source)
XLA Modules:
  0.0 687.0 jit_solution(3327787774463110607)
XLA Ops:
  10.5 6.6 collective-permute-start.1
  18.0 5.5 collective-permute-start.3
  29.5 6.9 %fusion.15 = f32[128,2048]{1,0:T(8,128)} fusion(f32[128]{0:T(128)S(1)} %get-tuple-element.125, f32[2048]{0:T(1024)S(1)} %bitcast.460, f32[128]{0:T(128)S(1)} %get-tuple-element.126, f32[2048]{0:T(1024)S(1)} %bitcast.468, f32[128]{0:T(128)S(1)} %get-tuple-element.124, f32[2048]{0:T(1024)S(1)} %bitcast.452, bf16[1,128,128]{2,1,0:T(8,128)(2,1)} %param.29, ...), kind=kOutput, calls=%fused_computation.44 | convolution fusion | flops 404242432 | bytes 1107712 | tf_op jit(solution)/shard_map/dot_general | solution.py:135
  36.4 6.1 fusion.21
  53.3 2.8 gather_fusion.6
  56.4 2.8 gather_fusion.4
  59.4 2.8 gather_fusion
  62.4 2.8 gather_fusion.2
  76.5 2.8 gather_fusion.5
  79.4 2.8 gather_fusion.3
  82.2 2.8 gather_fusion.1
  85.0 6.2 fusion.18
  91.3 6.2 fusion.24
  155.9 6.7 scatter_custom_fusion
  171.2 6.5 scatter_fusion
  177.8 6.1 scatter_fusion.1
  184.0 6.5 scatter_fusion.2
  191.7 98.8 %all-reduce.10.cloned.1.call-done = (f32[128,2048]{1,0:T(8,128)}, f32[128,2048]{1,0:T(8,128)}, f32[128,2048]{1,0:T(8,128)}, f32[128,2048]{1,0:T(8,128)}) async-done(((f32[128,2048]{1,0:T(8,128)}, f32[128,2048]{1,0:T(8,128)}, f32[128,2048]{1,0:T(8,128)}, f32[128,2048]{1,0:T(8,128)}), (f32[128,2048]{1,0:T(8,128)}, f32[128,2048]{1,0:T(8,128)}, f32[128,2048]{1,0:T(8,128)}, ...) | async-done | bytes 4194320 | tf_op jit(solution)/shard_map/psum | solution.py:197
  290.5 7.0 %fusion.10 = f32[128,128]{0,1:T(8,128)S(1)} fusion(f32[128,2048]{1,0:T(8,128)} %get-tuple-element.44, f32[2048,128]{0,1:T(8,128)S(1)} %copy-done.24, f32[128]{0:T(128)S(1)} %copy-done.69, f32[2048]{0:T(1024)S(1)} %bitcast.464, f32[128]{0:T(128)S(1)} %copy-done.71, f32[2048]{0:T(1024)S(1)} %bitcast.472, f32[128]{0:T(128)S(1)} %copy-done.67, ...), kind=kOutput, calls=%fused_computation.39 | convolution fusion | flops 404750336 | bytes 2188800 | tf_op jit(solution)/shard_map/dot_general | solution.py:141
  297.5 5.7 fusion.11
  305.0 7.6 %fusion.3 = f32[128,192]{0,1:T(8,128)S(1)} fusion(f32[128,192]{0,1:T(8,128)S(1)} %scatter_fusion.2, f32[128,128]{0,1:T(8,128)S(1)} %fusion.11, f32[128,2048]{1,0:T(8,128)} %get-tuple-element.46, f32[2048,128]{0,1:T(8,128)S(1)} %copy-done.24, f32[128]{0:T(128)S(1)} %copy-done.69, f32[2048]{0:T(1024)S(1)} %bitcast.466, f32[128]{0:T(128)S(1)} %copy-done.71, ...), kind=kOutput, calls=%fused_computation.26 | convolution fusion | flops 404799488 | bytes 2319873 | tf_op jit(solution)/shard_map/dot_general | solution.py:141
  313.7 5.7 fusion.9
  320.1 100.7 %all-reduce.6.cloned.1.call-done = f32[128,128]{0,1:T(8,128)} async-done(((f32[128,128]{0,1:T(8,128)}), f32[128,128]{0,1:T(8,128)}) %all-reduce.6.cloned.1.call-update) | async-done | bytes 65552 | tf_op jit(solution)/shard_map/psum | solution.py:247
  422.3 254.9 %all-reduce.8.cloned.1.call-done = (f32[128,128]{1,0:T(8,128)}, f32[384,128]{1,0:T(8,128)}) async-done(((f32[128,128]{1,0:T(8,128)}, f32[384,128]{1,0:T(8,128)}), (f32[128,128]{1,0:T(8,128)}, f32[384,128]{1,0:T(8,128)})) %all-reduce.8.cloned.1.call-update) | async-done | bytes 262160 | tf_op jit(solution)/shard_map/psum | solution.py:246
  (299 shorter events, 107.9 us)
Async XLA Ops:
  7.2 283.3 %all-reduce.10.cloned.1.call-start = ((), (), s32[]{:S(2)}) async-start(), calls=%async_computation.2 | async-start | bytes 8388608 | tf_op jit(solution)/shard_map/psum | solution.py:197
  8.0 45.0 %collective-permute-start = (bf16[1,3,32]{2,1,0:T(4,128)(2,1)S(1)}, bf16[1,3,32]{2,1,0:T(4,128)(2,1)S(1)}, u32[]{:S(2)}, u32[]{:S(2)}) collective-permute-start(bf16[1,3,32]{2,1,0:T(4,128)(2,1)S(1)} %get-tuple-element.127), channel_id=1, source_target_pairs={{0,1},{1,2},{2,3},{3,4},{4,5},{5,6},{6,7},{7,8},{8,9},{9,10},{10,1... | collective-permute-start | bytes 584 | tf_op jit(solution)/shard_map/ppermute | solution.py:24
  10.5 42.6 %collective-permute-start.1 = (bf16[1,3,32]{2,1,0:T(4,128)(2,1)S(1)}, bf16[1,3,32]{2,1,0:T(4,128)(2,1)S(1)}, u32[]{:S(2)}, u32[]{:S(2)}) collective-permute-start(bf16[1,3,32]{2,1,0:T(4,128)(2,1)S(1)} %get-tuple-element.128), channel_id=1, source_target_pairs={{1,0},{2,1},{3,2},{4,3},{5,4},{6,5},{7,6},{8,7},{9,8},{10,9},{11,1... | collective-permute-start | bytes 584 | tf_op jit(solution)/shard_map/ppermute | solution.py:26
  18.0 55.1 %collective-permute-start.2 = (bf16[1,128,32]{2,1,0:T(8,128)(2,1)S(1)}, bf16[1,128,32]{2,1,0:T(8,128)(2,1)S(1)}, u32[]{:S(2)}, u32[]{:S(2)}) collective-permute-start(bf16[1,128,32]{2,1,0:T(8,128)(2,1)S(1)} %get-tuple-element.74), channel_id=1, source_target_pairs={{0,1},{1,2},{2,3},{3,4},{4,5},{5,6},{6,7},{7,8},{8,9},{9,10},{10,1... | collective-permute-start | bytes 24584 | tf_op jit(solution)/shard_map/ppermute | solution.py:24
  18.0 55.1 %collective-permute-start.3 = (bf16[1,128,32]{2,1,0:T(8,128)(2,1)S(1)}, bf16[1,128,32]{2,1,0:T(8,128)(2,1)S(1)}, u32[]{:S(2)}, u32[]{:S(2)}) collective-permute-start(bf16[1,128,32]{2,1,0:T(8,128)(2,1)S(1)} %get-tuple-element.75), channel_id=1, source_target_pairs={{1,0},{2,1},{3,2},{4,3},{5,4},{6,5},{7,6},{8,7},{9,8},{10,9},{11,1... | collective-permute-start | bytes 24584 | tf_op jit(solution)/shard_map/ppermute | solution.py:26
  23.5 81.4 %copy-start.57 = (f32[8]{0:T(128)}, f32[8]{0:T(128)S(1)}, u32[]{:S(2)}) copy-start(f32[8]{0:T(128)S(1)} %iota_multiply_fusion) | copy-start | bytes 100
  25.7 65.5 %copy-start.66 = (f32[128]{0:T(128)}, f32[128]{0:T(128)S(1)}, u32[]{:S(2)}) copy-start(f32[128]{0:T(128)S(1)} %get-tuple-element.124) | copy-start | bytes 1540
  25.7 65.5 %copy-start.68 = (f32[128]{0:T(128)}, f32[128]{0:T(128)S(1)}, u32[]{:S(2)}) copy-start(f32[128]{0:T(128)S(1)} %get-tuple-element.125) | copy-start | bytes 1540
  25.7 65.5 %copy-start.70 = (f32[128]{0:T(128)}, f32[128]{0:T(128)S(1)}, u32[]{:S(2)}) copy-start(f32[128]{0:T(128)S(1)} %get-tuple-element.126) | copy-start | bytes 1540
  29.5 61.8 %copy-start.51 = (f32[1,2048]{1,0:T(1,128)}, f32[1,2048]{1,0:T(1,128)S(1)}, u32[]{:S(2)}) copy-start(f32[1,2048]{1,0:T(1,128)S(1)} %get-tuple-element.71) | copy-start | bytes 24580
  29.5 61.8 %copy-start.53 = (f32[1,2048]{1,0:T(1,128)}, f32[1,2048]{1,0:T(1,128)S(1)}, u32[]{:S(2)}) copy-start(f32[1,2048]{1,0:T(1,128)S(1)} %get-tuple-element.72) | copy-start | bytes 24580
  29.5 61.8 %copy-start.55 = (f32[1,2048]{1,0:T(1,128)}, f32[1,2048]{1,0:T(1,128)S(1)}, u32[]{:S(2)}) copy-start(f32[1,2048]{1,0:T(1,128)S(1)} %get-tuple-element.73) | copy-start | bytes 24580
  42.6 54.9 %copy-start.37 = (f32[8,128]{1,0:T(8,128)}, f32[8,128]{1,0:T(8,128)S(1)}, u32[]{:S(2)}) copy-start(f32[8,128]{1,0:T(8,128)S(1)} %get-tuple-element.82) | copy-start | bytes 12292
  42.6 61.6 %copy-start.39 = (f32[8,128]{1,0:T(8,128)}, f32[8,128]{1,0:T(8,128)S(1)}, u32[]{:S(2)}) copy-start(f32[8,128]{1,0:T(8,128)S(1)} %get-tuple-element.83) | copy-start | bytes 12292
  42.6 61.6 %copy-start.41 = (f32[8,128]{1,0:T(8,128)}, f32[8,128]{1,0:T(8,128)S(1)}, u32[]{:S(2)}) copy-start(f32[8,128]{1,0:T(8,128)S(1)} %get-tuple-element.80) | copy-start | bytes 12292
  128.5 292.2 %all-reduce.6.cloned.1.call-start = ((), (), s32[]{:S(2)}) async-start(), calls=%async_computation | async-start | bytes 131072 | tf_op jit(solution)/shard_map/psum | solution.py:247
  183.9 106.5 %copy-start.24 = (f32[2048,128]{0,1:T(8,128)S(1)}, f32[2048,128]{0,1:T(8,128)}, u32[]{:S(2)}) copy-start(f32[2048,128]{0,1:T(8,128)} %copy.356) | copy-start | bytes 3145732
  183.9 106.5 %copy-start.52 = (f32[1,2048]{1,0:T(1,128)S(1)}, f32[1,2048]{1,0:T(1,128)}, u32[]{:S(2)}) copy-start(f32[1,2048]{1,0:T(1,128)} %copy-done.51) | copy-start | bytes 24580
  183.9 106.5 %copy-start.54 = (f32[1,2048]{1,0:T(1,128)S(1)}, f32[1,2048]{1,0:T(1,128)}, u32[]{:S(2)}) copy-start(f32[1,2048]{1,0:T(1,128)} %copy-done.53) | copy-start | bytes 24580
  183.9 106.5 %copy-start.56 = (f32[1,2048]{1,0:T(1,128)S(1)}, f32[1,2048]{1,0:T(1,128)}, u32[]{:S(2)}) copy-start(f32[1,2048]{1,0:T(1,128)} %copy-done.55) | copy-start | bytes 24580
  184.0 106.5 %copy-start.67 = (f32[128]{0:T(128)S(1)}, f32[128]{0:T(128)}, u32[]{:S(2)}) copy-start(f32[128]{0:T(128)} %copy-done.66) | copy-start | bytes 1540
  184.0 106.5 %copy-start.69 = (f32[128]{0:T(128)S(1)}, f32[128]{0:T(128)}, u32[]{:S(2)}) copy-start(f32[128]{0:T(128)} %copy-done.68) | copy-start | bytes 1540
  184.0 106.5 %copy-start.71 = (f32[128]{0:T(128)S(1)}, f32[128]{0:T(128)}, u32[]{:S(2)}) copy-start(f32[128]{0:T(128)} %copy-done.70) | copy-start | bytes 1540
  305.0 372.2 %all-reduce.8.cloned.1.call-start = ((), (), s32[]{:S(2)}) async-start(), calls=%async_computation.1 | async-start | bytes 524288 | tf_op jit(solution)/shard_map/psum | solution.py:246
  (55 other events, 440.2 us)
Sparse Core Ops, SparseCore 0:
  128.7 161.7 all-reduce.9
  304.9 115.8 all-reduce.5
  427.9 249.2 all-reduce.7
where the time goes:
time: 692 us; the launch traced here: 687 us
  waiting for transfers between devices  454 us (66%)
  matrix products  90.6 us (13%)
  local copies, waits for them, and re-layouts  68.7 us (10%)
  other arithmetic  42.7 us (6%)
  between operations  15.9 us (2%)
  starting transfers between devices  14.7 us (2%)
    psum x1, waiting for transfers between devices, shards(): grad_in, grad_out = lax.psum((grad_in, grad_out), ('dp', 'atom'))  255 us
    psum x1, waiting for transfers between devices, shards(): grad_filter = lax.psum(grad_filter, 'dp')  101 us
    psum x1, waiting for transfers between devices, shards(): lax.psum((s_real, s_imag, g_real, g_imag), 'atom')  98.8 us
    scatter-add x4, other arithmetic, shards(): grad_hidden.at[:, block_slots.reshape(-1)].add(pulled.reshape(channels, -1))  25.7 us
    unnamed x161, local copies, waits for them, and re-layouts  16.2 us
  transfers between devices with their start and end apart: 7, of which 3 were waited for; matrix products, arithmetic and copies ran while one was open for 19% of the time, Pallas kernels for 0%

commit v1 on v0

v1 whole, which is shorter than its diff:
```python
import math

import jax
import jax.numpy as jnp
from jax import lax
from jax.experimental import pallas as pl
from jax.experimental.pallas import tpu as pltpu
from jax.sharding import PartitionSpec as P

F32 = jnp.float32
BF16 = jnp.bfloat16
I32 = jnp.int32

CH = 128
ROWS = 128
SLABS = 16
STRUCTS = 16
ATOMS = ROWS * SLABS
SLOTS = 32
EDGES = SLOTS * ROWS
GHOST = 32
KVEC = 2048
KSHARE = KVEC // SLABS
NB = 8
TOP = 6
SIDE = 2 * TOP + 1
PLANE = 176
HALF = (TOP + 1) * PLANE
FRAC_AT = CH
COT_AT = CH + 16
PAY = 2 * CH + 16

VMEM = pl.BlockSpec(memory_space=pltpu.VMEM)
SMEM = pl.BlockSpec(memory_space=pltpu.SMEM)

NN = (((1,), (0,)), ((), ()))
NT = (((1,), (1,)), ((), ()))
TN = (((0,), (0,)), ((), ()))


def dot(a, b, dims):
    return lax.dot_general(a, b, dims, preferred_element_type=F32)


def split(x):
    hi = x.astype(BF16)
    return hi, (x - hi.astype(F32)).astype(BF16)


def call(kernel, out, scratch, mib, flops, *args):
    smem = sum(1 for a in args if a.ndim == 1)
    specs = [SMEM if a.ndim == 1 else VMEM for a in args]
    del smem
    return pl.pallas_call(
        kernel,
        out_shape=out,
        in_specs=specs,
        out_specs=jax.tree.map(lambda _: VMEM, out),
        scratch_shapes=scratch,
        compiler_params=pltpu.CompilerParams(vmem_limit_bytes=mib * 2**20),
        cost_estimate=pl.CostEstimate(
            flops=flops, bytes_accessed=2**20, transcendentals=0
        ),
    )(*args)


def pack_kernel(place, feats, cot, frac, pay, pad):
    live = lax.broadcasted_iota(I32, (CH, ROWS), 1) < place[1]
    pay[0:CH] = jnp.where(live, feats[0].astype(F32), 0.0).astype(BF16)
    pay[COT_AT:PAY] = jnp.where(live, cot[0].astype(F32), 0.0).astype(BF16)
    pad[...] = jnp.zeros((8, ROWS), F32)
    pad[0:3, :] = frac[0]
    hi, lo = split(pad[...])
    pay[FRAC_AT:COT_AT] = jnp.concatenate(
        [hi.astype(F32), lo.astype(F32)], axis=0
    ).astype(BF16)


def joined_frac(block):
    wide = block.astype(F32)
    return wide[0:8] + wide[8:16]


ROOT3, ROOT5, ROOT15 = math.sqrt(3.0), math.sqrt(5.0), math.sqrt(15.0)
STEP = 1.75 / (NB - 1)
BAND = 16


def edge_kernel(
    place,
    own,
    left,
    right,
    neighbours,
    images,
    count,
    in_weight,
    radial_weight,
    out_weight,
    early,
    local,
    ext,
    hot,
    weights,
    basis,
    radial,
    moved,
    shape_w,
    length,
    feats9,
    up9,
    pulled,
    inv,
):
    first, live_here = place[0], place[1]
    lane = lax.broadcasted_iota(I32, (CH, ROWS), 1)
    ext[:, 0:ROWS] = own[0:CH]
    ext[:, ROWS : 2 * ROWS] = jnp.where(
        lane < GHOST, right[0:CH].astype(F32), left[0:CH].astype(F32)
    ).astype(BF16)
    hidden = dot(in_weight[...], ext[...], TN).astype(BF16)

    offset = (neighbours[0] - first) & (ATOMS - 1)
    column = jnp.where(offset < ROWS + GHOST, offset, offset - (ATOMS - 2 * ROWS))
    at = column & (ROWS - 1)
    in_slab = column < ROWS
    frac_own = joined_frac(own[FRAC_AT:COT_AT])
    frac_left = joined_frac(left[FRAC_AT:COT_AT])
    frac_right = joined_frac(right[FRAC_AT:COT_AT])
    lane8 = lax.broadcasted_iota(I32, (8, ROWS), 1)
    frac_far = jnp.where(lane8 < GHOST, frac_right, frac_left)

    code = images[0]
    ninth = (code * 57) >> 9
    third = (code * 171) >> 9
    shifts = (ninth, third - 3 * ninth, code - 3 * third)
    vector = []
    for d in range(3):
        near = jnp.broadcast_to(frac_own[d : d + 1], (SLOTS, ROWS))
        far = jnp.broadcast_to(frac_far[d : d + 1], (SLOTS, ROWS))
        other = jnp.where(
            in_slab,
            jnp.take_along_axis(near, at, axis=1),
            jnp.take_along_axis(far, at, axis=1),
        )
        vector.append(0.5 * (other - near + (shifts[d].astype(F32) - 1.0)))
    x, y, z = vector
    square = x * x + y * y + z * z
    slot = lax.broadcasted_iota(I32, (SLOTS, ROWS), 0)
    lane32 = lax.broadcasted_iota(I32, (SLOTS, ROWS), 1)
    used = (slot < count[...]) & (lane32 < live_here)
    weight = jnp.where(used, SLOTS**-0.5, 0.0)
    harmonics = (
        weight,
        weight * (ROOT3 * x),
        weight * (ROOT3 * y),
        weight * (ROOT3 * z),
        weight * (ROOT15 * x * y),
        weight * (ROOT15 * y * z),
        weight * (0.5 * ROOT5 * (3.0 * z * z - square)),
        weight * (ROOT15 * x * z),
        weight * (0.5 * ROOT15 * (x * x - y * y)),
    )
    for m in range(9):
        shape_w[m] = harmonics[m]
    length[...] = jnp.sqrt(square)

    rows256 = lax.broadcasted_iota(I32, (2 * ROWS, ROWS), 0)
    centre = lax.broadcasted_iota(I32, (NB, ROWS), 0).astype(F32) * STEP
    basis[24:32, :] = jnp.zeros((8, EDGES), F32)
    for e in range(SLOTS):
        here = slice(e * ROWS, (e + 1) * ROWS)
        hot[:, here] = jnp.where(rows256 == column[e : e + 1], 1.0, 0.0).astype(BF16)
        gap = (length[e : e + 1, :] - centre) * (1.0 / STEP)
        gauss = jnp.exp(-(gap * gap))
        hi, lo = split(gauss)
        basis[0:8, here] = hi.astype(F32)
        basis[8:16, here] = lo.astype(F32)
        basis[16:24, here] = hi.astype(F32)
    weights[...] = jnp.zeros((32, 3 * CH), F32)
    for l in range(3):
        hi, lo = split(radial_weight[l])
        part = slice(l * CH, (l + 1) * CH)
        weights[0:8, part] = hi.astype(F32)
        weights[8:16, part] = hi.astype(F32)
        weights[16:24, part] = lo.astype(F32)
    radial[...] = dot(weights[...].astype(BF16), basis[...].astype(BF16), TN)
    moved[...] = dot(hidden, hot[...], NN)

    def forward(step, carry):
        top = pl.multiple_of(step * BAND, BAND)
        total = [jnp.zeros((BAND, ROWS), F32) for _ in range(9)]
        for e in range(SLOTS):
            here = slice(e * ROWS, (e + 1) * ROWS)
            value = moved[pl.ds(top, BAND), here]
            parts = [
                radial[pl.ds(pl.multiple_of(l * CH + top, BAND), BAND), here] * value
                for l in range(3)
            ]
            for m in range(9):
                l = 0 if m == 0 else (1 if m < 4 else 2)
                total[m] = total[m] + shape_w[m, e : e + 1, :] * parts[l]
        for m in range(9):
            feats9[m, pl.ds(top, BAND), :] = total[m]
        squares = [t * t for t in total]
        inv[pl.ds(top, BAND), :] = squares[0].astype(BF16)
        inv[pl.ds(pl.multiple_of(CH + top, BAND), BAND), :] = (
            squares[1] + squares[2] + squares[3]
        ).astype(BF16)
        inv[pl.ds(pl.multiple_of(2 * CH + top, BAND), BAND), :] = (
            squares[4] + squares[5] + squares[6] + squares[7] + squares[8]
        ).astype(BF16)
        return carry

    lax.fori_loop(0, CH // BAND, forward, 0)

    masked = own[COT_AT:PAY]
    local[...] = dot(out_weight[...], inv[...], TN)
    up9[...] = 2.0 * dot(out_weight[...], masked, NN)
    early[CH : 4 * CH, :] = dot(inv[...], masked, NT)

    def backward(step, carry):
        top = pl.multiple_of(step * BAND, BAND)
        up = [
            up9[pl.ds(pl.multiple_of(l * CH + top, BAND), BAND), :] for l in range(3)
        ]
        upstream = []
        for m in range(9):
            l = 0 if m == 0 else (1 if m < 4 else 2)
            upstream.append(feats9[m, pl.ds(top, BAND), :] * up[l])
        for e in range(SLOTS):
            here = slice(e * ROWS, (e + 1) * ROWS)
            term = [shape_w[m, e : e + 1, :] * upstream[m] for m in range(9)]
            pull = (
                radial[pl.ds(top, BAND), here] * term[0]
                + radial[pl.ds(pl.multiple_of(CH + top, BAND), BAND), here]
                * (term[1] + term[2] + term[3])
                + radial[pl.ds(pl.multiple_of(2 * CH + top, BAND), BAND), here]
                * (term[4] + term[5] + term[6] + term[7] + term[8])
            )
            pulled[pl.ds(top, BAND), here] = pull.astype(BF16)
        return carry

    lax.fori_loop(0, CH // BAND, backward, 0)
    back = dot(pulled[...], hot[...], NT)
    early[0:CH, :] = dot(ext[...], back.astype(BF16), NT)


def half_row(miller):
    m0, m1, m2 = miller[0:1], miller[1:2], miller[2:3]
    sign = jnp.where(m0 < 0, -1, 1)
    return (sign * m0) * PLANE + (sign * m1 + TOP) * SIDE + (sign * m2 + TOP)


def turns(frac_row, first, count):
    width = frac_row.shape[1]
    m = (lax.broadcasted_iota(I32, (count, width), 0) + first).astype(F32)
    turn = m * frac_row
    turn = turn - jnp.floor(turn + 0.5)
    quarter = jnp.floor(turn * 4.0 + 0.5)
    arc = (turn - 0.25 * quarter) * (2.0 * math.pi)
    s2 = arc * arc
    sine = arc * (1.0 + s2 * (-1 / 6 + s2 * (1 / 120 + s2 * (-1 / 5040))))
    cosine = 1.0 + s2 * (-0.5 + s2 * (1 / 24 + s2 * (-1 / 720 + s2 * (1 / 40320))))
    odd = jnp.abs(quarter) == 1.0
    back = jnp.abs(quarter) == 2.0
    flip = jnp.where(quarter < 0.0, -1.0, 1.0)
    cos_out = jnp.where(odd, -flip * sine, jnp.where(back, -cosine, cosine))
    sin_out = jnp.where(odd, flip * cosine, jnp.where(back, -sine, sine))
    return cos_out, sin_out


def plane_tables(frac, cos_plane, sin_plane):
    c1, s1 = turns(frac[1:2], -TOP, 16)
    c2, s2 = turns(frac[2:3], -TOP, 16)
    for a in range(SIDE):
        ca, sa = c1[a : a + 1], s1[a : a + 1]
        rows = slice(a * SIDE, a * SIDE + 16 if a < SIDE - 1 else PLANE)
        many = 16 if a < SIDE - 1 else PLANE - a * SIDE
        if many <= 16:
            cos_plane[rows, :] = (ca * c2 - sa * s2)[0:many]
            sin_plane[rows, :] = (sa * c2 + ca * s2)[0:many]
        else:
            cos_plane[a * SIDE : a * SIDE + 16, :] = ca * c2 - sa * s2
            sin_plane[a * SIDE : a * SIDE + 16, :] = sa * c2 + ca * s2
            cos_plane[a * SIDE + 16 : PLANE, :] = jnp.zeros(
                (many - 16, ca.shape[1]), F32
            )
            sin_plane[a * SIDE + 16 : PLANE, :] = jnp.zeros(
                (many - 16, ca.shape[1]), F32
            )
    return turns(frac[0:1], 0, 8)


def lattice_kernel(miller, filter_weight, frac, folded, table, hot, cos_p, sin_p, pad):
    row = half_row(miller[...])
    hi, lo = split(filter_weight[...] * (1.0 / math.sqrt(KVEC * ATOMS)))
    point = lax.broadcasted_iota(I32, (HALF, 256), 0)
    for k in range(KVEC // 256):
        here = slice(k * 256, (k + 1) * 256)
        hot[:, here] = jnp.where(point == row[:, here], 1.0, 0.0).astype(BF16)
    both = dot(hot[...], jnp.concatenate([hi, lo], axis=1), NN)
    folded[...] = both[:, 0:CH] + both[:, CH : 2 * CH]
    pad[...] = jnp.zeros((8, ROWS), F32)
    pad[0:3, :] = frac[0]
    c0, s0 = plane_tables(pad[...], cos_p, sin_p)
    for m in range(TOP + 1):
        cm, sm = c0[m : m + 1], s0[m : m + 1]
        here = slice(m * PLANE, (m + 1) * PLANE)
        there = slice(HALF + m * PLANE, HALF + (m + 1) * PLANE)
        table[here, :] = (cm * cos_p[...] - sm * sin_p[...]).astype(BF16)
        table[there, :] = (sm * cos_p[...] + cm * sin_p[...]).astype(BF16)


def ewald_kernel(
    place,
    gathered,
    folded,
    table_own,
    miller_own,
    in_weight,
    feats,
    local,
    updated,
    parts,
    frac,
    values,
    cos_p,
    sin_p,
    table,
    factor,
    coef,
):
    for p in range(SLABS):
        here = slice(p * ROWS, (p + 1) * ROWS)
        values[0:CH, here] = gathered[p, 0:CH]
        values[CH : 2 * CH, here] = gathered[p, COT_AT:PAY]
        frac[:, here] = joined_frac(gathered[p, FRAC_AT:COT_AT])
    c0, s0 = plane_tables(frac[...], cos_p, sin_p)
    for m in range(TOP + 1):
        cm, sm = c0[m : m + 1], s0[m : m + 1]
        here = slice(m * PLANE, (m + 1) * PLANE)
        there = slice(HALF + m * PLANE, HALF + (m + 1) * PLANE)
        table[here, :] = (cm * cos_p[...] - sm * sin_p[...]).astype(BF16)
        table[there, :] = (sm * cos_p[...] + cm * sin_p[...]).astype(BF16)
    factor[...] = dot(table[...], values[...], NT)

    point = lax.broadcasted_iota(I32, (HALF, KSHARE), 0)
    hot = jnp.where(point == half_row(miller_own[...]), 1.0, 0.0).astype(BF16)
    feats_hi, feats_lo = split(factor[:, 0:CH])
    stacked = jnp.concatenate([in_weight[...], in_weight[...]], axis=0)
    s = dot(jnp.concatenate([feats_hi, feats_lo], axis=1), stacked, NN)
    g = factor[:, CH : 2 * CH]
    for k in range(2):
        here = slice(k * HALF, (k + 1) * HALF)
        coef[here, 0:CH] = (folded[...] * s[here]).astype(BF16)
        coef[here, CH : 2 * CH] = (folded[...] * g[here]).astype(BF16)
    scale = 1.0 / math.sqrt(KVEC * ATOMS)
    pair = scale * (s[0:HALF] * g[0:HALF] + s[HALF:] * g[HALF:])
    pair_hi, pair_lo = split(pair)
    both = dot(hot, jnp.concatenate([pair_hi, pair_lo], axis=1), TN)
    grad_filter = both[:, 0:CH] + both[:, CH : 2 * CH]
    ewald = dot(coef[:, 0:CH], table_own[...], TN)
    grad_in = dot(feats_hi, coef[:, CH : 2 * CH], TN)
    for d in range(STRUCTS):
        parts[d, 0:8, :] = grad_in[8 * d : 8 * d + 8]
        parts[d, 8:16, :] = grad_filter[8 * d : 8 * d + 8]
    live = lax.broadcasted_iota(I32, (CH, ROWS), 1) < place[1]
    updated[0] = jnp.where(
        live, feats[0].astype(F32) + local[...] + ewald, 0.0
    ).astype(BF16)


def exchange(x, axis):
    return lax.all_to_all(x, axis, 0, 0)


def to_all(x, axis, count):
    return exchange(jnp.broadcast_to(x[None], (count,) + x.shape), axis)


def shards(
    node_feats,
    frac,
    neighbours,
    images,
    neighbour_count,
    atom_count,
    miller,
    in_weight,
    radial_weight,
    out_weight,
    filter_weight,
    cotangent,
):
    slab = lax.axis_index("atom")
    first = slab * ROWS
    place = jnp.stack([first, atom_count[0] - first]).astype(I32)
    struct = jax.ShapeDtypeStruct

    pay = call(
        pack_kernel,
        struct((PAY, ROWS), BF16),
        [pltpu.VMEM((8, ROWS), F32)],
        16,
        10**6,
        place,
        node_feats,
        cotangent,
        frac,
    )
    halo = pay[0:COT_AT]
    ring = range(SLABS)
    left = lax.ppermute(halo, "atom", [(i, (i + 1) % SLABS) for i in ring])
    right = lax.ppermute(halo, "atom", [((i + 1) % SLABS, i) for i in ring])
    gathered = to_all(pay, "atom", SLABS)

    folded, table_own = call(
        lattice_kernel,
        (struct((HALF, CH), F32), struct((2 * HALF, ROWS), BF16)),
        [
            pltpu.VMEM((HALF, KVEC), BF16),
            pltpu.VMEM((PLANE, ROWS), F32),
            pltpu.VMEM((PLANE, ROWS), F32),
            pltpu.VMEM((8, ROWS), F32),
        ],
        40,
        3 * 10**9,
        miller,
        filter_weight,
        frac,
    )
    early, local = call(
        edge_kernel,
        (struct((4 * CH, CH), F32), struct((CH, ROWS), F32)),
        [
            pltpu.VMEM((CH, 2 * ROWS), BF16),
            pltpu.VMEM((2 * ROWS, EDGES), BF16),
            pltpu.VMEM((32, 3 * CH), F32),
            pltpu.VMEM((32, EDGES), F32),
            pltpu.VMEM((3 * CH, EDGES), F32),
            pltpu.VMEM((CH, EDGES), F32),
            pltpu.VMEM((9, SLOTS, ROWS), F32),
            pltpu.VMEM((SLOTS, ROWS), F32),
            pltpu.VMEM((9, CH, ROWS), F32),
            pltpu.VMEM((3 * CH, ROWS), F32),
            pltpu.VMEM((CH, EDGES), BF16),
            pltpu.VMEM((3 * CH, ROWS), BF16),
        ],
        40,
        3 * 10**9,
        place,
        pay,
        left,
        right,
        neighbours,
        images,
        neighbour_count,
        in_weight,
        radial_weight,
        out_weight,
    )
    chunk = exchange(early.reshape(STRUCTS, SLOTS, CH), "dp").sum(axis=0)
    chunk = to_all(chunk.astype(BF16), "atom", SLABS).astype(F32).sum(axis=0)

    miller_own = lax.dynamic_slice_in_dim(miller, slab * KSHARE, KSHARE, 1)
    updated, parts = call(
        ewald_kernel,
        (struct((1, CH, ROWS), BF16), struct((STRUCTS, 16, CH), F32)),
        [
            pltpu.VMEM((8, ATOMS), F32),
            pltpu.VMEM((2 * CH, ATOMS), BF16),
            pltpu.VMEM((PLANE, ATOMS), F32),
            pltpu.VMEM((PLANE, ATOMS), F32),
            pltpu.VMEM((2 * HALF, ATOMS), BF16),
            pltpu.VMEM((2 * HALF, 2 * CH), F32),
            pltpu.VMEM((2 * HALF, 2 * CH), BF16),
        ],
        48,
        10**10,
        place,
        gathered,
        folded,
        table_own,
        miller_own,
        in_weight,
        node_feats,
        local,
    )
    late = exchange(parts, "dp").sum(axis=0)
    last = jnp.concatenate([late, chunk], axis=0).astype(BF16)
    sums = to_all(last, "dp", STRUCTS).astype(F32)
    grad_early = sums[:, 16:].reshape(4 * CH, CH)
    grad_in = sums[:, 0:8].reshape(CH, CH) + grad_early[0:CH]
    grad_filter = sums[:, 8:16].reshape(KSHARE, CH)
    return (updated, grad_filter, grad_in, grad_early[CH:])


def solution(mesh):
    return jax.shard_map(
        shards,
        mesh=mesh,
        in_specs=(
            P("dp", None, "atom"),
            P("dp", None, "atom"),
            P("dp", None, "atom"),
            P("dp", None, "atom"),
            P("dp", "atom"),
            P("dp"),
            P(),
            P(),
            P(),
            P(),
            P(),
            P("dp", None, "atom"),
        ),
        out_specs=(P("dp", None, "atom"), P("atom", None), P(), P()),
        check_vma=False,
    )
```

time: 692 us -> 119 us (0.17)
  waiting for transfers between devices: 454 us -> 38.2 us
  matrix products: 90.6 us -> 0 us
  local copies, waits for them, and re-layouts: 68.7 us -> 10.7 us
  other arithmetic: 42.7 us -> 1.77 us
  blocking collectives: 0 us -> 23.5 us
  Pallas kernels: 0 us -> 17.6 us
  between operations: 15.9 us -> 1.44 us
  starting transfers between devices: 14.7 us -> 24.8 us
    psum x3 -> x0, waiting for transfers between devices: 454 us -> none  [the longest x1 255 us: shards(): grad_in, grad_out = lax.psum((grad_in, grad_out), ('dp', 'atom'))]
    dot_general x33 -> x0, matrix products: 90.6 us -> none  [the longest x2 13.4 us: project(): jnp.dot(imag_coef, sin_table, precision=maximum_degree)]
    all_to_all x0 -> x3, waiting for transfers between devices: none -> 31.8 us  [exchange(): return lax.all_to_all(x, axis, 0, 0)]
    scatter-add x4 -> x0, other arithmetic: 25.7 us -> none  [shards(): grad_hidden.at[:, block_slots.reshape(-1)].add(pulled.reshape(channels, -1))]
    all_to_all x0 -> x2, blocking collectives: none -> 23.5 us  [exchange(): return lax.all_to_all(x, axis, 0, 0)]
    gather x12 -> x0, local copies, waits for them, and re-layouts: 23.2 us -> none  [the longest x8 12 us: edge_terms(): others = jnp.take(frac_ext, slot_index, axis=1)]
    pallas_call x0 -> x4, Pallas kernels: none -> 17.6 us  [call(): pl.pallas_call(kernel, out_shape=out, in_specs=specs, out_specs=jax.tree....]
    dot_general x12 -> x0, local copies, waits for them, and re-layouts: 17.4 us -> none  [the longest x4 6.39 us: edge_sum(): jnp.einsum('ea,cea->ca', spherical_harmonic[0], edge_message[0], precisio...]
  transfers between devices with their start and end apart: 7 -> 5, of which waited for: 3 -> 5; matrix products, arithmetic and copies ran while one was open for 19% -> 1% of each run, Pallas kernels for 0% -> 8%
where the time goes in v1:
time: 119 us; the launch traced here: 118 us
  waiting for transfers between devices  38.2 us (32%)
  starting transfers between devices  24.8 us (21%)
  blocking collectives  23.5 us (20%)
  Pallas kernels  17.6 us (15%)
  local copies, waits for them, and re-layouts  10.7 us (9%)
  other arithmetic  1.77 us (1%)
  between operations  1.44 us (1%)
    all_to_all x3, waiting for transfers between devices, exchange(): return lax.all_to_all(x, axis, 0, 0)  31.8 us
    all_to_all x2, blocking collectives, exchange(): return lax.all_to_all(x, axis, 0, 0)  23.5 us
    pallas_call x4, Pallas kernels, call(): pl.pallas_call(kernel, out_shape=out, in_specs=specs, out_specs=jax.tree....  17.6 us
    all_to_all x3, starting transfers between devices, exchange(): return lax.all_to_all(x, axis, 0, 0)  15.7 us
    ppermute x1, starting transfers between devices, shards(): right = lax.ppermute(halo, 'atom', [((i + 1) % SLABS, i) for i in ring])  9.11 us
    unnamed x29, local copies, waits for them, and re-layouts  7.5 us
    ppermute x1, waiting for transfers between devices, shards(): left = lax.ppermute(halo, 'atom', [(i, (i + 1) % SLABS) for i in ring])  5.36 us
  transfers between devices with their start and end apart: 5, of which 5 were waited for; matrix products, arithmetic and copies ran while one was open for 1% of the time, Pallas kernels for 8%

profile of v1, /device:TPU:1, one launch (start us, length us, event | category | flops | bytes accessed | tf_op | source)
XLA Modules:
  0.0 118.1 jit_solution(7544088568940522323)
XLA Ops:
  2.0 0.8 copy-done
  2.8 0.8 copy-done.1
  4.1 9.1 %collective-permute-start.1 = (bf16[144,128]{1,0:T(8,128)(2,1)S(1)}, bf16[144,128]{1,0:T(8,128)(2,1)S(1)}, u32[]{:S(2)}, u32[]{:S(2)}) collective-permute-start(bf16[144,128]{1,0:T(8,128)(2,1)S(1)} %slice.31), channel_id=1, source_target_pairs={{1,0},{2,1},{3,2},{4,3},{5,4},{6,5},{7,6},{8,7},{9,8},{10,9},{11,1... | collective-permute-start | bytes 110600 | tf_op jit(solution)/shard_map/ppermute | solution.py:415
  13.2 1.1 collective-permute-done.1.right
  14.3 5.4 %collective-permute-done.left = bf16[144,128]{1,0:T(8,128)(2,1)S(1)} collective-permute-done((bf16[144,128]{1,0:T(8,128)(2,1)S(1)}, bf16[144,128]{1,0:T(8,128)(2,1)S(1)}, u32[]{:S(2)}, u32[]{:S(2)}) %collective-permute-start) | collective-permute-done | bytes 36896 | tf_op jit(solution)/shard_map/ppermute | solution.py:414
  19.7 0.9 copy-done.5
  20.6 0.8 copy-done.6
  21.3 0.7 copy-done.8
  22.0 0.7 copy-done.9
  22.8 0.7 copy-done.10
  24.1 7.6 %shard_map.149 = (f32[512,128]{1,0:T(8,128)S(1)}, f32[128,128]{1,0:T(8,128)S(1)}) custom-call(s32[2]{0:T(128)S(1)} %pad_add_fusion.place, bf16[272,128]{1,0:T(8,128)(2,1)S(1)} %shard_map.147.own, bf16[144,128]{1,0:T(8,128)(2,1)S(1)} %collective-permute-done.left, bf16[144,128]{1,0:T(8,128)(2,1)S(1)} %collective-permute-done.1.right, ...), custom_call_target="tpu_custom_call" | custom-call | flops 3000000000 | bytes 1048576 | tf_op jit(solution)/shard_map/pallas_call | solution.py:54
  31.7 13.8 %all_to_all.25 = f32[16,32,128]{2,1,0:T(8,128)} all-to-all(f32[16,32,128]{2,1,0:T(8,128)S(1)} %bitcast.14), channel_id=1, replica_groups=mesh['dp'=16,'atom'=16] {'dp'}, dimensions={0} | all-to-all | bytes 524288 | tf_op jit(solution)/shard_map/all_to_all | solution.py:375
  45.6 1.2 broadcast_in_dim.6
  46.7 3.8 %all-to-all-start = ((bf16[16,272,128]{2,1,0:T(8,128)(2,1)}), bf16[16,272,128]{2,1,0:T(8,128)(2,1)S(1)}, u32[]{:S(2)}, u32[]{:S(2)}) async-start(bf16[16,272,128]{2,1,0:T(8,128)(2,1)} %broadcast_in_dim.6), calls=%async_computation | async-start | bytes 2228224 | tf_op jit(solution)/shard_map/all_to_all | solution.py:375
  50.6 1.7 %shard_map.148 = (f32[1232,128]{1,0:T(8,128)S(1)}, bf16[2464,128]{1,0:T(8,128)(2,1)S(1)}) custom-call(s32[3,2048]{1,0:T(4,128)S(1)} %copy-done.3, f32[2048,128]{1,0:T(8,128)S(1)} %copy-done.4, f32[1,3,128]{2,1,0:T(4,128)S(1)} %copy.18.frac), custom_call_target="tpu_custom_call" | custom-call | flops 3000000000 | bytes 1048576 | tf_op jit(solution)/shard_map/pallas_call | solution.py:54
  52.3 1.0 reduce_sum.28
  53.3 25.3 %all-to-all-done.gathered = bf16[16,272,128]{2,1,0:T(8,128)(2,1)S(1)} async-done(((bf16[16,272,128]{2,1,0:T(8,128)(2,1)}), bf16[16,272,128]{2,1,0:T(8,128)(2,1)S(1)}, u32[]{:S(2)}, u32[]{:S(2)}) %all-to-all-start) | async-done | bytes 1114144 | tf_op jit(solution)/shard_map/all_to_all | solution.py:375
  79.3 6.5 %all-to-all-start.3 = ((bf16[16,32,128]{2,1,0:T(8,128)(2,1)}), bf16[16,32,128]{2,1,0:T(8,128)(2,1)S(1)}, u32[]{:S(2)}, u32[]{:S(2)}) async-start(bf16[16,32,128]{2,1,0:T(8,128)(2,1)} %broadcast_in_dim.7), calls=%async_computation.3 | async-start | bytes 262144 | tf_op jit(solution)/shard_map/all_to_all | solution.py:375
  85.8 0.8 copy-done.13
  86.6 7.8 %shard_map.150 = (bf16[1,128,128]{2,1,0:T(8,128)(2,1)}, f32[16,16,128]{2,1,0:T(8,128)}) custom-call(s32[2]{0:T(128)S(1)} %pad_add_fusion.place, bf16[16,272,128]{2,1,0:T(8,128)(2,1)S(1)} %all-to-all-done.gathered, f32[1232,128]{1,0:T(8,128)S(1)} %get-tuple-element.10.folded, bf16[2464,128]{1,0:T(8,128)(2,1)S(1)} %get-tuple-element.11.table_own, ...), custom_call_target="tpu_custom_call" | custom-call | flops 10000000000 | bytes 1048576 | tf_op jit(solution)/shard_map/pallas_call | solution.py:54
  94.7 5.4 %all-to-all-start.1 = ((f32[16,16,128]{2,1,0:T(8,128)}), f32[16,16,128]{2,1,0:T(8,128)S(1)}, u32[]{:S(2)}, u32[]{:S(2)}) async-start(f32[16,16,128]{2,1,0:T(8,128)} %get-tuple-element.14), calls=%async_computation.1 | async-start | bytes 262144 | tf_op jit(solution)/shard_map/all_to_all | solution.py:375
  100.2 6.2 %all-to-all-done.1 = f32[16,16,128]{2,1,0:T(8,128)S(1)} async-done(((f32[16,16,128]{2,1,0:T(8,128)}), f32[16,16,128]{2,1,0:T(8,128)S(1)}, u32[]{:S(2)}, u32[]{:S(2)}) %all-to-all-start.1) | async-done | bytes 131104 | tf_op jit(solution)/shard_map/all_to_all | solution.py:375
  106.4 9.7 %all_to_all.26 = bf16[16,48,128]{2,1,0:T(8,128)(2,1)S(1)} all-to-all(bf16[16,48,128]{2,1,0:T(8,128)(2,1)S(1)} %broadcast_in_dim.8), channel_id=1, replica_groups=mesh['dp'=16,'atom'=16] {'dp'}, dimensions={0} | all-to-all | bytes 393216 | tf_op jit(solution)/shard_map/all_to_all | solution.py:375
  117.4 0.7 slice.35
  (36 shorter events, 4.4 us)
Async XLA Ops:
  2.0 0.8 copy-start
  2.8 0.8 copy-start.1
  4.1 10.2 %collective-permute-start.1 = (bf16[144,128]{1,0:T(8,128)(2,1)S(1)}, bf16[144,128]{1,0:T(8,128)(2,1)S(1)}, u32[]{:S(2)}, u32[]{:S(2)}) collective-permute-start(bf16[144,128]{1,0:T(8,128)(2,1)S(1)} %slice.31), channel_id=1, source_target_pairs={{1,0},{2,1},{3,2},{4,3},{5,4},{6,5},{7,6},{8,7},{9,8},{10,9},{11,1... | collective-permute-start | bytes 110600 | tf_op jit(solution)/shard_map/ppermute | solution.py:415
  13.2 6.4 %collective-permute-start = (bf16[144,128]{1,0:T(8,128)(2,1)S(1)}, bf16[144,128]{1,0:T(8,128)(2,1)S(1)}, u32[]{:S(2)}, u32[]{:S(2)}) collective-permute-start(bf16[144,128]{1,0:T(8,128)(2,1)S(1)} %slice.31), channel_id=1, source_target_pairs={{0,1},{1,2},{2,3},{3,4},{4,5},{5,6},{6,7},{7,8},{8,9},{9,10},{10,1... | collective-permute-start | bytes 110600 | tf_op jit(solution)/shard_map/ppermute | solution.py:414
  19.7 0.9 copy-start.5
  20.6 0.8 copy-start.6
  21.3 0.7 copy-start.8
  22.0 0.7 copy-start.9
  22.8 0.7 copy-start.10
  23.5 0.7 copy-start.11
  31.7 13.8 %copy-start.12 = (f32[128,128]{1,0:T(8,128)}, f32[128,128]{1,0:T(8,128)S(1)}, u32[]{:S(2)}) copy-start(f32[128,128]{1,0:T(8,128)S(1)} %get-tuple-element.12.local) | copy-start | bytes 196612
  46.7 3.8 %copy-start.3 = (s32[3,2048]{1,0:T(4,128)S(1)}, s32[3,2048]{1,0:T(4,128)}, u32[]{:S(2)}) copy-start(s32[3,2048]{1,0:T(4,128)} %miller.1) | copy-start | bytes 73732
  46.7 3.9 %copy-start.4 = (f32[2048,128]{1,0:T(8,128)S(1)}, f32[2048,128]{1,0:T(8,128)}, u32[]{:S(2)}) copy-start(f32[2048,128]{1,0:T(8,128)} %filter_weight.1) | copy-start | bytes 3145732
  46.7 31.9 %all-to-all-start = ((bf16[16,272,128]{2,1,0:T(8,128)(2,1)}), bf16[16,272,128]{2,1,0:T(8,128)(2,1)S(1)}, u32[]{:S(2)}, u32[]{:S(2)}) async-start(bf16[16,272,128]{2,1,0:T(8,128)(2,1)} %broadcast_in_dim.6), calls=%async_computation | async-start | bytes 2228224 | tf_op jit(solution)/shard_map/all_to_all | solution.py:375
  50.6 35.2 %copy-start.2 = (bf16[1,128,128]{2,1,0:T(8,128)(2,1)S(1)}, bf16[1,128,128]{2,1,0:T(8,128)(2,1)}, u32[]{:S(2)}) copy-start(bf16[1,128,128]{2,1,0:T(8,128)(2,1)} %feats.3) | copy-start | bytes 98308
  50.6 35.2 %copy-start.7 = (bf16[128,128]{1,0:T(8,128)(2,1)S(1)}, bf16[128,128]{1,0:T(8,128)(2,1)}, u32[]{:S(2)}) copy-start(bf16[128,128]{1,0:T(8,128)(2,1)} %in_weight.3) | copy-start | bytes 98308
  79.3 15.4 %all-to-all-start.3 = ((bf16[16,32,128]{2,1,0:T(8,128)(2,1)}), bf16[16,32,128]{2,1,0:T(8,128)(2,1)S(1)}, u32[]{:S(2)}, u32[]{:S(2)}) async-start(bf16[16,32,128]{2,1,0:T(8,128)(2,1)} %broadcast_in_dim.7), calls=%async_computation.3 | async-start | bytes 262144 | tf_op jit(solution)/shard_map/all_to_all | solution.py:375
  85.8 0.8 copy-start.13
  94.7 11.7 %all-to-all-start.1 = ((f32[16,16,128]{2,1,0:T(8,128)}), f32[16,16,128]{2,1,0:T(8,128)S(1)}, u32[]{:S(2)}, u32[]{:S(2)}) async-start(f32[16,16,128]{2,1,0:T(8,128)} %get-tuple-element.14), calls=%async_computation.1 | async-start | bytes 262144 | tf_op jit(solution)/shard_map/all_to_all | solution.py:375

commit v2 on v1

v2 whole, which is shorter than its diff:
```python
import math

import jax
import jax.numpy as jnp
from jax import lax
from jax.experimental import pallas as pl
from jax.experimental.pallas import tpu as pltpu
from jax.sharding import PartitionSpec as P

F32 = jnp.float32
BF16 = jnp.bfloat16
I32 = jnp.int32

CH = 128
ROWS = 128
SLABS = 16
STRUCTS = 16
ATOMS = ROWS * SLABS
SLOTS = 32
EDGES = SLOTS * ROWS
GHOST = 32
KVEC = 2048
KSHARE = KVEC // SLABS
NB = 8
TOP = 6
SIDE = 2 * TOP + 1
PLANE = 128
HALF = (TOP + 1) * PLANE
WAVES = SIDE
BASIS = WAVES * 2 * PLANE
TILE = 256
MINE = CH // SLABS
FRAC_AT = CH
COT_AT = CH + 16
PAY = COT_AT + 16

VMEM = pl.BlockSpec(memory_space=pltpu.VMEM)
SMEM = pl.BlockSpec(memory_space=pltpu.SMEM)
HBM = pl.BlockSpec(memory_space=pltpu.HBM)

NN = (((1,), (0,)), ((), ()))
NT = (((1,), (1,)), ((), ()))
TN = (((0,), (0,)), ((), ()))


def dot(a, b, dims):
    return lax.dot_general(a, b, dims, preferred_element_type=F32)


def split(x):
    hi = x.astype(BF16)
    return hi, (x - hi.astype(F32)).astype(BF16)


def call(kernel, outs, scratch, mib, flops, *args):
    return pl.pallas_call(
        kernel,
        out_shape=[shape for _, shape in outs],
        in_specs=[spec for spec, _ in args],
        out_specs=[spec for spec, _ in outs],
        scratch_shapes=scratch,
        compiler_params=pltpu.CompilerParams(vmem_limit_bytes=mib * 2**20),
        cost_estimate=pl.CostEstimate(
            flops=flops, bytes_accessed=2**16, transcendentals=0
        ),
    )(*[arg for _, arg in args])


def fetch(pairs, sems):
    copies = [
        pltpu.make_async_copy(src, dst, sems.at[n]) for n, (src, dst) in enumerate(pairs)
    ]
    for copy in copies:
        copy.start()
    return copies


def coordinates(frac):
    rows = jnp.pad(frac, ((0, 5), (0, 0)))
    first = jnp.floor(rows * 256.0) * (1.0 / 256.0)
    return jnp.concatenate([first, rows - first], axis=0).astype(BF16)


def joined_frac(block):
    wide = block.astype(F32)
    return wide[0:8] + wide[8:16]


ROOT3, ROOT5, ROOT15 = math.sqrt(3.0), math.sqrt(5.0), math.sqrt(15.0)
STEP = 1.75 / (NB - 1)
BAND = 16
EDGE_COST = 10**10


def edge_kernel(
    place,
    own,
    left,
    right,
    neighbours_hbm,
    images_hbm,
    count_hbm,
    in_weight_hbm,
    radial_weight_hbm,
    out_weight_hbm,
    cot_hbm,
    early,
    local,
    neighbours,
    images,
    count,
    in_weight,
    radial_weight,
    out_weight,
    cot,
    ext,
    hot,
    weights,
    basis,
    radial,
    moved,
    shape_w,
    length,
    feats9,
    up9,
    pulled,
    inv,
    sems,
):
    copies = fetch(
        (
            (neighbours_hbm, neighbours),
            (images_hbm, images),
            (count_hbm, count),
            (in_weight_hbm, in_weight),
            (radial_weight_hbm, radial_weight),
            (out_weight_hbm, out_weight),
            (cot_hbm, cot),
        ),
        sems,
    )
    for copy in copies:
        copy.wait()
    first, live_here, live_left, live_right = place[0], place[1], place[2], place[3]
    lane = lax.broadcasted_iota(I32, (CH, ROWS), 1)
    ext[:, 0:ROWS] = jnp.where(lane < live_here, own[0:CH].astype(F32), 0.0).astype(BF16)
    near_right = jnp.where(lane < live_right, right[0:CH].astype(F32), 0.0)
    near_left = jnp.where(lane < live_left, left[0:CH].astype(F32), 0.0)
    ext[:, ROWS : 2 * ROWS] = jnp.where(lane < GHOST, near_right, near_left).astype(BF16)
    hidden = dot(in_weight[...], ext[...], TN).astype(BF16)

    offset = (neighbours[0] - first) & (ATOMS - 1)
    column = jnp.where(offset < ROWS + GHOST, offset, offset - (ATOMS - 2 * ROWS))
    at = column & (ROWS - 1)
    in_slab = column < ROWS
    frac_own = joined_frac(own[FRAC_AT:COT_AT])
    frac_left = joined_frac(left[FRAC_AT:COT_AT])
    frac_right = joined_frac(right[FRAC_AT:COT_AT])
    lane8 = lax.broadcasted_iota(I32, (8, ROWS), 1)
    frac_far = jnp.where(lane8 < GHOST, frac_right, frac_left)

    code = images[0]
    ninth = (code * 57) >> 9
    third = (code * 171) >> 9
    shifts = (ninth, third - 3 * ninth, code - 3 * third)
    vector = []
    for d in range(3):
        near = jnp.broadcast_to(frac_own[d : d + 1], (SLOTS, ROWS))
        far = jnp.broadcast_to(frac_far[d : d + 1], (SLOTS, ROWS))
        other = jnp.where(
            in_slab,
            jnp.take_along_axis(near, at, axis=1),
            jnp.take_along_axis(far, at, axis=1),
        )
        vector.append(0.5 * (other - near + (shifts[d].astype(F32) - 1.0)))
    x, y, z = vector
    square = x * x + y * y + z * z
    slot = lax.broadcasted_iota(I32, (SLOTS, ROWS), 0)
    lane32 = lax.broadcasted_iota(I32, (SLOTS, ROWS), 1)
    used = (slot < count[...]) & (lane32 < live_here)
    weight = jnp.where(used, SLOTS**-0.5, 0.0)
    harmonics = (
        weight,
        weight * (ROOT3 * x),
        weight * (ROOT3 * y),
        weight * (ROOT3 * z),
        weight * (ROOT15 * x * y),
        weight * (ROOT15 * y * z),
        weight * (0.5 * ROOT5 * (3.0 * z * z - square)),
        weight * (ROOT15 * x * z),
        weight * (0.5 * ROOT15 * (x * x - y * y)),
    )
    for m in range(9):
        shape_w[m] = harmonics[m]
    length[...] = jnp.sqrt(square)

    rows256 = lax.broadcasted_iota(I32, (2 * ROWS, ROWS), 0)
    centre = lax.broadcasted_iota(I32, (NB, ROWS), 0).astype(F32) * STEP
    basis[24:32, :] = jnp.zeros((8, EDGES), F32)
    for e in range(SLOTS):
        here = slice(e * ROWS, (e + 1) * ROWS)
        hot[:, here] = jnp.where(rows256 == column[e : e + 1], 1.0, 0.0).astype(BF16)
        gap = (length[e : e + 1, :] - centre) * (1.0 / STEP)
        gauss = jnp.exp(-(gap * gap))
        hi, lo = split(gauss)
        basis[0:8, here] = hi.astype(F32)
        basis[8:16, here] = lo.astype(F32)
        basis[16:24, here] = hi.astype(F32)
    weights[...] = jnp.zeros((32, 3 * CH), F32)
    for l in range(3):
        hi, lo = split(radial_weight[l])
        part = slice(l * CH, (l + 1) * CH)
        weights[0:8, part] = hi.astype(F32)
        weights[8:16, part] = hi.astype(F32)
        weights[16:24, part] = lo.astype(F32)
    radial[...] = dot(weights[...].astype(BF16), basis[...].astype(BF16), TN)
    moved[...] = dot(hidden, hot[...], NN)

    def forward(step, carry):
        top = pl.multiple_of(step * BAND, BAND)
        total = [jnp.zeros((BAND, ROWS), F32) for _ in range(9)]
        for e in range(SLOTS):
            here = slice(e * ROWS, (e + 1) * ROWS)
            value = moved[pl.ds(top, BAND), here]
            parts = [
                radial[pl.ds(pl.multiple_of(l * CH + top, BAND), BAND), here] * value
                for l in range(3)
            ]
            for m in range(9):
                l = 0 if m == 0 else (1 if m < 4 else 2)
                total[m] = total[m] + shape_w[m, e : e + 1, :] * parts[l]
        for m in range(9):
            feats9[m, pl.ds(top, BAND), :] = total[m]
        squares = [t * t for t in total]
        inv[pl.ds(top, BAND), :] = squares[0].astype(BF16)
        inv[pl.ds(pl.multiple_of(CH + top, BAND), BAND), :] = (
            squares[1] + squares[2] + squares[3]
        ).astype(BF16)
        inv[pl.ds(pl.multiple_of(2 * CH + top, BAND), BAND), :] = (
            squares[4] + squares[5] + squares[6] + squares[7] + squares[8]
        ).astype(BF16)
        return carry

    lax.fori_loop(0, CH // BAND, forward, 0)

    masked = jnp.where(lane < live_here, cot[0].astype(F32), 0.0).astype(BF16)
    local[...] = dot(out_weight[...], inv[...], TN)
    up9[...] = 2.0 * dot(out_weight[...], masked, NN)
    grad_out = dot(inv[...], masked, NT)
    for d in range(4, STRUCTS):
        to = d * SLOTS
        early[to : to + SLOTS, :] = grad_out[(d - 4) * SLOTS : (d - 3) * SLOTS]

    def backward(step, carry):
        top = pl.multiple_of(step * BAND, BAND)
        up = [
            up9[pl.ds(pl.multiple_of(l * CH + top, BAND), BAND), :] for l in range(3)
        ]
        upstream = []
        for m in range(9):
            l = 0 if m == 0 else (1 if m < 4 else 2)
            upstream.append(feats9[m, pl.ds(top, BAND), :] * up[l])
        for e in range(SLOTS):
            here = slice(e * ROWS, (e + 1) * ROWS)
            term = [shape_w[m, e : e + 1, :] * upstream[m] for m in range(9)]
            pull = (
                radial[pl.ds(top, BAND), here] * term[0]
                + radial[pl.ds(pl.multiple_of(CH + top, BAND), BAND), here]
                * (term[1] + term[2] + term[3])
                + radial[pl.ds(pl.multiple_of(2 * CH + top, BAND), BAND), here]
                * (term[4] + term[5] + term[6] + term[7] + term[8])
            )
            pulled[pl.ds(top, BAND), here] = pull.astype(BF16)
        return carry

    lax.fori_loop(0, CH // BAND, backward, 0)
    back = dot(pulled[...], hot[...], NT)
    grad_in = dot(ext[...], back.astype(BF16), NT)
    for d in range(4):
        to = d * SLOTS
        early[to : to + SLOTS, :] = grad_in[d * SLOTS : (d + 1) * SLOTS]


def half_row(miller):
    m0, m1, m2 = miller[0:1], miller[1:2], miller[2:3]
    sign = jnp.where(m0 < 0, -1, 1)
    m0, m1, m2 = sign * m0, sign * m1, sign * m2
    minus = m1 < 0
    turn = jnp.where(minus, -1, 1)
    row = m0 * PLANE + turn * m1 * SIDE + (turn * m2 + TOP)
    return row + jnp.where(minus, HALF, 0)


def turns(frac_row, first, count):
    width = frac_row.shape[1]
    m = (lax.broadcasted_iota(I32, (count, width), 0) + first).astype(F32)
    turn = m * frac_row
    turn = turn - jnp.floor(turn + 0.5)
    quarter = jnp.floor(turn * 4.0 + 0.5)
    arc = (turn - 0.25 * quarter) * (2.0 * math.pi)
    s2 = arc * arc
    sine = arc * (1.0 + s2 * (-1 / 6 + s2 * (1 / 120 + s2 * (-1 / 5040))))
    cosine = 1.0 + s2 * (-0.5 + s2 * (1 / 24 + s2 * (-1 / 720 + s2 * (1 / 40320))))
    odd = jnp.abs(quarter) == 1.0
    back = jnp.abs(quarter) == 2.0
    flip = jnp.where(quarter < 0.0, -1.0, 1.0)
    cos_out = jnp.where(odd, -flip * sine, jnp.where(back, -cosine, cosine))
    sin_out = jnp.where(odd, flip * cosine, jnp.where(back, -sine, sine))
    return cos_out, sin_out


def waves(frac, plane):
    width = plane.shape[1]
    c1, s1 = turns(frac[1:2], 0, 8)
    c2, s2 = turns(frac[2:3], -TOP, 16)
    for k in (0, PLANE):
        plane[k + 88 : k + PLANE, :] = jnp.zeros((PLANE - 88, width), F32)
    for m in range(TOP + 1):
        cm, sm = c1[m : m + 1], s1[m : m + 1]
        plane[m * SIDE : m * SIDE + 16, :] = cm * c2 - sm * s2
        plane[PLANE + m * SIDE : PLANE + m * SIDE + 16, :] = sm * c2 + cm * s2
    c0, s0 = turns(frac[0:1], 0, 8)
    return [c0[m : m + 1] for m in range(TOP + 1)] + [
        s0[m : m + 1] for m in range(1, TOP + 1)
    ]


def one_hot(miller, hot):
    row = half_row(miller[...])
    point = lax.broadcasted_iota(I32, (2 * HALF, TILE), 0)
    for k in range(KVEC // TILE):
        here = slice(k * TILE, (k + 1) * TILE)
        hot[:, here] = jnp.where(point == row[:, here], 1.0, 0.0).astype(BF16)


def lattice_kernel(miller, filter_weight, frac, folded, table, hot, plane, pad):
    one_hot(miller, hot)
    hi, lo = split(filter_weight[...] * (1.0 / math.sqrt(KVEC * ATOMS)))
    both = dot(hot[...], jnp.concatenate([hi, lo], axis=1), NN)
    both = both[:, 0:CH] + both[:, CH : 2 * CH]
    folded[0:CH, :] = (both[0:HALF] + both[HALF : 2 * HALF]).T
    folded[CH : 2 * CH, :] = (both[0:HALF] - both[HALF : 2 * HALF]).T
    pad[...] = jnp.zeros((8, ROWS), F32)
    for d in range(3):
        pad[d : d + 1, :] = frac[d]
    for f, wave in enumerate(waves(pad[...], plane)):
        here = slice(f * 2 * PLANE, (f + 1) * 2 * PLANE)
        table[here, :] = (wave * plane[...]).astype(BF16)


def blocks(x, m):
    at = 2 * m * PLANE
    cc, cs = x[:, at : at + PLANE], x[:, at + PLANE : at + 2 * PLANE]
    if m == 0:
        return cc, None, None, cs
    at = 2 * (TOP + m) * PLANE
    sc, ss = x[:, at : at + PLANE], x[:, at + PLANE : at + 2 * PLANE]
    return cc, ss, sc, cs


def filtered(plus, minus, x):
    first, second = [], []
    for m in range(TOP + 1):
        here = slice(m * PLANE, (m + 1) * PLANE)
        p, d = plus[:, here], minus[:, here]
        cc, ss, sc, cs = blocks(x, m)
        if m == 0:
            first += [p * cc, p * cs]
        else:
            first += [p * cc - d * ss, p * cs + d * sc]
            second += [p * sc + d * cs, p * ss - d * cc]
    return first + second


def spectrum_kernel(
    place,
    gathered,
    folded,
    miller,
    own_weight,
    early,
    parts,
    factor,
    hot,
    frac,
    values,
    plane,
    wide,
):
    for p in range(SLABS):
        here = slice(p * ROWS, (p + 1) * ROWS)
        values[0:CH, here] = gathered[p, 0:CH]
        values[CH : CH + 16, here] = gathered[p, COT_AT:PAY]
        frac[:, here] = joined_frac(gathered[p, FRAC_AT:COT_AT])
    rows = CH + 16
    along = waves(frac[...], plane)
    live = (lax.broadcasted_iota(I32, (1, ATOMS), 1) < place[0] + place[1]).astype(F32)
    around = plane[...].astype(BF16)
    for low, high in ((0, TOP + 1), (TOP + 1, WAVES)):
        for f in range(low, high):
            wide[f * rows : (f + 1) * rows, :] = (
                values[...].astype(F32) * (along[f] * live)
            ).astype(BF16)
        both = dot(wide[low * rows : high * rows, :], around, NT)
        for f in range(low, high):
            here = slice(f * 2 * PLANE, (f + 1) * 2 * PLANE)
            factor[:, here] = both[(f - low) * rows : (f - low + 1) * rows]
        if low == 0:
            one_hot(miller, hot)

    top = pl.multiple_of(place[4], MINE)
    feats_hi, feats_lo = split(factor[0:CH, :])
    s = dot(own_weight[...], jnp.concatenate([feats_hi, feats_lo], axis=0), NN)[0:MINE]
    g = factor[CH : CH + MINE, :]
    plus = folded[pl.ds(top, MINE), :]
    minus = folded[pl.ds(pl.multiple_of(CH + top, MINE), MINE), :]
    grad = split(jnp.concatenate(filtered(plus, minus, g), axis=1))
    grad_in = dot(jnp.concatenate(grad, axis=0), feats_hi, NT)
    grad_in = grad_in[0:MINE] + grad_in[MINE : 2 * MINE]
    pair_plus, pair_minus = [], []
    for m in range(TOP + 1):
        cc, ss, sc, cs = blocks(s, m)
        gcc, gss, gsc, gcs = blocks(g, m)
        even, odd = cc * gcc + cs * gcs, 0.0
        if m > 0:
            even = even + ss * gss + sc * gsc
            odd = sc * gcs + cs * gsc - cc * gss - ss * gcc
        pair_plus.append(even + odd)
        pair_minus.append(even - odd)
    pair = jnp.concatenate(pair_plus + pair_minus, axis=1)
    pair = split(pair * (1.0 / math.sqrt(KVEC * ATOMS)))
    pair = dot(jnp.concatenate(pair, axis=0), hot[...], NN)
    pair = pair[0:MINE] + pair[MINE : 2 * MINE]
    for d in range(STRUCTS):
        parts[d, 0:16, :] = jnp.concatenate(
            [pair[:, d * KSHARE : (d + 1) * KSHARE], grad_in], axis=0
        ).astype(BF16)
        parts[d, 16:48, :] = early[d * SLOTS : (d + 1) * SLOTS, :].astype(BF16)


SPECTRUM_SCRATCH = [
    pltpu.VMEM((2 * HALF, KVEC), BF16),
    pltpu.VMEM((8, ATOMS), F32),
    pltpu.VMEM((CH + 16, ATOMS), BF16),
    pltpu.VMEM((2 * PLANE, ATOMS), F32),
    pltpu.VMEM((WAVES * (CH + 16), ATOMS), BF16),
]


def update_kernel(
    place, factor, folded, table_own, in_weight, feats, local, updated, coef
):
    both = jnp.concatenate(split(factor[0:CH, :]), axis=0)
    s = dot(in_weight[...], both, NN)
    pieces = filtered(folded[0:CH, :], folded[CH : 2 * CH, :], s)
    for n, piece in enumerate(pieces):
        coef[:, n * PLANE : (n + 1) * PLANE] = piece.astype(BF16)
    ewald = dot(coef[...], table_own[...], NN)
    here = lax.broadcasted_iota(I32, (CH, ROWS), 1) < place[1]
    updated[0] = jnp.where(
        here, feats[0].astype(F32) + local[...] + ewald, 0.0
    ).astype(BF16)


def middle_kernel(place, sums, last, grad_in):
    row = lax.broadcasted_iota(I32, (8, KSHARE), 0)
    lane = lax.broadcasted_iota(I32, (8, KSHARE), 1)
    pick = jnp.where(lane == row + place[4], 1.0, 0.0).astype(BF16)
    pairs = jnp.concatenate([sums[p, 0:16].astype(F32)[0:8] for p in range(SLABS)], axis=0)
    grads = jnp.concatenate([sums[p, 0:16].astype(F32)[8:16] for p in range(SLABS)], axis=0)
    grad_in[...] = grads.T
    total = sums[0, 16:48].astype(F32)
    for p in range(1, SLABS):
        total = total + sums[p, 16:48].astype(F32)
    last[0:32] = total.astype(BF16)
    picked = dot(pick, pairs.astype(BF16), NT)
    last[32:48] = jnp.concatenate([picked, picked], axis=0).astype(BF16)


def finish_kernel(sums, ewald_in, grad_filter, grad_in, grad_out):
    for d in range(STRUCTS):
        late = sums[d, 32:48].astype(F32)
        grad_filter[8 * d : 8 * d + 8, :] = late[0:8]
    for d in range(4):
        here = slice(d * SLOTS, (d + 1) * SLOTS)
        grad_in[here, :] = ewald_in[here, :] + sums[d, 0:32].astype(F32)
    for d in range(4, STRUCTS):
        grad_out[(d - 4) * SLOTS : (d - 3) * SLOTS, :] = sums[d, 0:32].astype(F32)


def exchange(x, axis):
    return lax.all_to_all(x, axis, 0, 0)


def to_all(x, axis, count):
    return exchange(jnp.broadcast_to(x[None], (count,) + x.shape), axis)


def shards(
    node_feats,
    frac,
    neighbours,
    images,
    neighbour_count,
    atom_count,
    miller,
    in_weight,
    radial_weight,
    out_weight,
    filter_weight,
    cotangent,
):
    slab = lax.axis_index("atom")
    first = slab * ROWS
    live = atom_count[0] - jnp.stack(
        [first, (first - ROWS) % ATOMS, (first + ROWS) % ATOMS]
    )
    place = jnp.concatenate([first[None], live, slab[None] * MINE]).astype(I32)
    struct = jax.ShapeDtypeStruct

    halo = jnp.concatenate([node_feats[0], coordinates(frac[0])], axis=0)
    ring = range(SLABS)
    left = lax.ppermute(halo, "atom", [(i, (i + 1) % SLABS) for i in ring])
    right = lax.ppermute(halo, "atom", [((i + 1) % SLABS, i) for i in ring])
    cot_parts = jnp.pad(cotangent.reshape(SLABS, MINE, ROWS), ((0, 0), (0, 8), (0, 0)))
    gathered = exchange(
        jnp.concatenate(
            [jnp.broadcast_to(halo[None], (SLABS, COT_AT, ROWS)), cot_parts], axis=1
        ),
        "atom",
    )
    frac = frac.transpose(1, 0, 2)

    order = (SLABS, STRUCTS, KVEC // SLABS // STRUCTS)
    miller = miller.reshape((3,) + order).transpose(0, 2, 1, 3).reshape(3, KVEC)
    filter_weight = (
        filter_weight.reshape(order + (CH,)).transpose(1, 0, 2, 3).reshape(KVEC, CH)
    )
    folded, table_own = call(
        lattice_kernel,
        [
            (VMEM, struct((2 * CH, HALF), F32)),
            (VMEM, struct((BASIS, ROWS), BF16)),
        ],
        [
            pltpu.VMEM((2 * HALF, KVEC), BF16),
            pltpu.VMEM((2 * PLANE, ROWS), F32),
            pltpu.VMEM((8, ROWS), F32),
        ],
        24,
        10**8,
        (VMEM, miller),
        (VMEM, filter_weight),
        (VMEM, frac),
    )
    early, local = call(
        edge_kernel,
        [(VMEM, struct((4 * CH, CH), F32)), (VMEM, struct((CH, ROWS), F32))],
        [
            pltpu.VMEM((1, SLOTS, ROWS), I32),
            pltpu.VMEM((1, SLOTS, ROWS), I32),
            pltpu.VMEM((1, ROWS), I32),
            pltpu.VMEM((CH, CH), BF16),
            pltpu.VMEM((3, NB, CH), F32),
            pltpu.VMEM((3 * CH, CH), BF16),
            pltpu.VMEM((1, CH, ROWS), BF16),
            pltpu.VMEM((CH, 2 * ROWS), BF16),
            pltpu.VMEM((2 * ROWS, EDGES), BF16),
            pltpu.VMEM((32, 3 * CH), F32),
            pltpu.VMEM((32, EDGES), F32),
            pltpu.VMEM((3 * CH, EDGES), F32),
            pltpu.VMEM((CH, EDGES), F32),
            pltpu.VMEM((9, SLOTS, ROWS), F32),
            pltpu.VMEM((SLOTS, ROWS), F32),
            pltpu.VMEM((9, CH, ROWS), F32),
            pltpu.VMEM((3 * CH, ROWS), F32),
            pltpu.VMEM((CH, EDGES), BF16),
            pltpu.VMEM((3 * CH, ROWS), BF16),
            pltpu.SemaphoreType.DMA((7,)),
        ],
        24,
        EDGE_COST,
        (SMEM, place),
        (VMEM, halo),
        (VMEM, left),
        (VMEM, right),
        (HBM, neighbours),
        (HBM, images),
        (HBM, neighbour_count),
        (HBM, in_weight),
        (HBM, radial_weight),
        (HBM, out_weight),
        (HBM, cotangent),
    )
    weight_t = jnp.concatenate([in_weight, in_weight], axis=0).T
    own_weight = lax.dynamic_slice_in_dim(in_weight, slab * MINE, MINE, 1)
    own_weight = jnp.pad(jnp.concatenate([own_weight, own_weight], axis=0).T, ((0, 8), (0, 0)))
    parts, factor = call(
        spectrum_kernel,
        [
            (VMEM, struct((STRUCTS, 48, CH), BF16)),
            (VMEM, struct((CH + 16, BASIS), F32)),
        ],
        SPECTRUM_SCRATCH,
        32,
        10**10,
        (SMEM, place),
        (VMEM, gathered),
        (VMEM, folded),
        (VMEM, miller),
        (VMEM, own_weight),
        (VMEM, early),
    )
    (updated,) = call(
        update_kernel,
        [(VMEM, struct((1, CH, ROWS), BF16))],
        [pltpu.VMEM((CH, BASIS), BF16)],
        24,
        10**9,
        (SMEM, place),
        (VMEM, factor),
        (VMEM, folded),
        (VMEM, table_own),
        (VMEM, weight_t),
        (VMEM, node_feats),
        (VMEM, local),
    )
    sums = exchange(parts, "dp").astype(F32).sum(axis=0).astype(BF16)
    last, ewald_in = call(
        middle_kernel,
        [(VMEM, struct((48, CH), BF16)), (VMEM, struct((CH, CH), F32))],
        [],
        16,
        10**6,
        (SMEM, place),
        (VMEM, to_all(sums, "atom", SLABS)),
    )
    grads = call(
        finish_kernel,
        [
            (VMEM, struct((KSHARE, CH), F32)),
            (VMEM, struct((CH, CH), F32)),
            (VMEM, struct((3 * CH, CH), F32)),
        ],
        [],
        16,
        10**6,
        (VMEM, to_all(last, "dp", STRUCTS)),
        (VMEM, ewald_in),
    )
    return (updated, *grads)


def solution(mesh):
    return jax.shard_map(
        shards,
        mesh=mesh,
        in_specs=(
            P("dp", None, "atom"),
            P("dp", None, "atom"),
            P("dp", None, "atom"),
            P("dp", None, "atom"),
            P("dp", "atom"),
            P("dp"),
            P(),
            P(),
            P(),
            P(),
            P(),
            P("dp", None, "atom"),
        ),
        out_specs=(P("dp", None, "atom"), P("atom", None), P(), P()),
        check_vma=False,
    )
```

time: 119 us -> 85.7 us (0.72)
  waiting for transfers between devices: 38.2 us -> 6.11 us
  blocking collectives: 23.5 us -> 28.9 us
  starting transfers between devices: 24.8 us -> 20.1 us
  local copies, waits for them, and re-layouts: 10.7 us -> 7.17 us
    all_to_all x3 -> x2, waiting for transfers between devices: 31.8 us -> 6.11 us  [exchange(): return lax.all_to_all(x, axis, 0, 0)]
    all_to_all x2, blocking collectives: 23.5 us -> 28.9 us  [exchange(): return lax.all_to_all(x, axis, 0, 0)]
    ppermute x1, waiting for transfers between devices: 5.36 us -> 0.01 us  [shards(): left = lax.ppermute(halo, 'atom', [(i, (i + 1) % SLABS) for i in ring])]
    all_to_all x3 -> x2, starting transfers between devices: 15.7 us -> 11 us  [exchange(): return lax.all_to_all(x, axis, 0, 0)]
    ppermute x1, starting transfers between devices: 9.11 us -> 6.57 us  [shards(): right = lax.ppermute(halo, 'atom', [((i + 1) % SLABS, i) for i in ring])]
    concatenate x1 -> x3, other arithmetic: 0.01 us -> 2.51 us  [the longest x1 1.67 us: shards(): jnp.concatenate([jnp.broadcast_to(halo[None], (SLABS, COT_AT, ROWS)), cot...]
    ppermute x1, starting transfers between devices: 0.01 us -> 2.47 us  [shards(): left = lax.ppermute(halo, 'atom', [(i, (i + 1) % SLABS) for i in ring])]
    unnamed x29 -> x40, local copies, waits for them, and re-layouts: 7.5 us -> 5.65 us
  transfers between devices with their start and end apart: 5 -> 4, of which waited for: 5 -> 2; matrix products, arithmetic and copies ran while one was open for 1% -> 3% of each run, Pallas kernels for 8% -> 15%
where the time goes in v2:
time: 85.7 us; the launch traced here: 85.1 us
  blocking collectives  28.9 us (34%)
  starting transfers between devices  20.1 us (23%)
  Pallas kernels  18.6 us (22%)
  local copies, waits for them, and re-layouts  7.17 us (8%)
  waiting for transfers between devices  6.11 us (7%)
  other arithmetic  2.64 us (3%)
  between operations  1.6 us (2%)
    all_to_all x2, blocking collectives, exchange(): return lax.all_to_all(x, axis, 0, 0)  28.9 us
    pallas_call x6, Pallas kernels, call(): pl.pallas_call(kernel, out_shape=[shape for _, shape in outs], in_specs=[...  18.6 us
    all_to_all x2, starting transfers between devices, exchange(): return lax.all_to_all(x, axis, 0, 0)  11 us
    ppermute x1, starting transfers between devices, shards(): right = lax.ppermute(halo, 'atom', [((i + 1) % SLABS, i) for i in ring])  6.57 us
    all_to_all x2, waiting for transfers between devices, exchange(): return lax.all_to_all(x, axis, 0, 0)  6.11 us
    unnamed x40, local copies, waits for them, and re-layouts  5.65 us
    ppermute x1, starting transfers between devices, shards(): left = lax.ppermute(halo, 'atom', [(i, (i + 1) % SLABS) for i in ring])  2.47 us
  transfers between devices with their start and end apart: 4, of which 2 were waited for; matrix products, arithmetic and copies ran while one was open for 3% of the time, Pallas kernels for 15%

profile of v2, /device:TPU:1, one launch (start us, length us, event | category | flops | bytes accessed | tf_op | source)
XLA Modules:
  0.0 85.1 jit_solution(2231442337922177432)
XLA Ops:
  0.6 0.7 copy.28
  1.3 0.8 pad_maximum_fusion.own
  2.1 2.5 %collective-permute-start = (bf16[144,128]{1,0:T(8,128)(2,1)S(1)}, bf16[144,128]{1,0:T(8,128)(2,1)S(1)}, u32[]{:S(2)}, u32[]{:S(2)}) collective-permute-start(bf16[144,128]{1,0:T(8,128)(2,1)S(1)} %pad_maximum_fusion.own), channel_id=1, source_target_pairs={{0,1},{1,2},{2,3},{3,4},{4,5},{5,6},{6,7},{7,8},{8,9},{9,10},{10,1... | collective-permute-start | bytes 110600 | tf_op jit(solution)/shard_map/ppermute | solution.py:523
  4.6 6.6 %collective-permute-start.1 = (bf16[144,128]{1,0:T(8,128)(2,1)S(1)}, bf16[144,128]{1,0:T(8,128)(2,1)S(1)}, u32[]{:S(2)}, u32[]{:S(2)}) collective-permute-start(bf16[144,128]{1,0:T(8,128)(2,1)S(1)} %pad_maximum_fusion.own), channel_id=1, source_target_pairs={{1,0},{2,1},{3,2},{4,3},{5,4},{6,5},{7,6},{8,7},{9,8},{10,9},{11,1... | collective-permute-start | bytes 110600 | tf_op jit(solution)/shard_map/ppermute | solution.py:524
  11.2 1.7 %fusion.1 = bf16[16,160,128]{2,1,0:T(8,128)(2,1)} fusion(bf16[16,8,128]{2,1,0:T(8,128)(2,1)} %bitcast.25, bf16[16,144,128]{2,1,0:T(8,128)(2,1)S(1)} %broadcast_in_dim.9), kind=kLoop, calls=%fused_computation.2 | loop fusion | flops 1966080 | bytes 1277952 | tf_op jit(solution)/shard_map/concatenate | solution.py:527
  12.9 5.5 %all-to-all-start = ((bf16[16,160,128]{2,1,0:T(8,128)(2,1)}), bf16[16,160,128]{2,1,0:T(8,128)(2,1)S(1)}, u32[]{:S(2)}, u32[]{:S(2)}) async-start(bf16[16,160,128]{2,1,0:T(8,128)(2,1)} %fusion.1), calls=%async_computation | async-start | bytes 1310720 | tf_op jit(solution)/shard_map/all_to_all | solution.py:492
  20.4 0.2 copy-done.7
  20.7 2.3 %shard_map.147 = (f32[256,896]{1,0:T(8,128)S(1)}, bf16[3328,128]{1,0:T(8,128)(2,1)S(1)}) custom-call(s32[3,2048]{1,0:T(4,128)S(1)} %reshape.30.miller, f32[2048,128]{1,0:T(8,128)S(1)} %bitcast.23, f32[3,1,128]{2,1,0:T(1,128)S(1)} %bitcast.26), custom_call_target="tpu_custom_call" | custom-call | flops 100000000 | bytes 65536 | tf_op jit(solution)/shard_map/pallas_call | solution.py:56
  23.0 0.9 %copy-done = bf16[3328,128]{1,0:T(8,128)(2,1)} copy-done((bf16[3328,128]{1,0:T(8,128)(2,1)}, bf16[3328,128]{1,0:T(8,128)(2,1)S(1)}, u32[]{:S(2)}) %copy-start) | copy-done | bytes 851992
  24.0 8.2 %shard_map.148 = (f32[512,128]{1,0:T(8,128)S(1)}, f32[128,128]{1,0:T(8,128)S(1)}) custom-call(s32[5]{0:T(128)S(1)} %pad_add_fusion.place, bf16[144,128]{1,0:T(8,128)(2,1)S(1)} %pad_maximum_fusion.own, bf16[144,128]{1,0:T(8,128)(2,1)S(1)} %collective-permute-done.left, bf16[144,128]{1,0:T(8,128)(2,1)S(1)} %collective-permute-done.1.right, ...), custom_call_target="tpu_custom_call" | custom-call | flops 10000000000 | bytes 65536 | tf_op jit(solution)/shard_map/pallas_call | solution.py:56
  32.2 0.6 copy-done.3
  32.8 0.7 copy-done.13
  33.5 2.4 %all-to-all-done.gathered = bf16[16,160,128]{2,1,0:T(8,128)(2,1)S(1)} async-done(((bf16[16,160,128]{2,1,0:T(8,128)(2,1)}), bf16[16,160,128]{2,1,0:T(8,128)(2,1)S(1)}, u32[]{:S(2)}, u32[]{:S(2)}) %all-to-all-start) | async-done | bytes 655392 | tf_op jit(solution)/shard_map/all_to_all | solution.py:492
  36.0 0.9 %copy-done.14 = f32[512,128]{1,0:T(8,128)S(1)} copy-done((f32[512,128]{1,0:T(8,128)S(1)}, f32[512,128]{1,0:T(8,128)}, u32[]{:S(2)}) %copy-start.14) | copy-done | bytes 262168
  36.9 4.7 %shard_map.149 = (bf16[16,48,128]{2,1,0:T(8,128)(2,1)S(1)}, f32[144,3328]{1,0:T(8,128)S(1)}) custom-call(s32[5]{0:T(128)S(1)} %pad_add_fusion.place, bf16[16,160,128]{2,1,0:T(8,128)(2,1)S(1)} %all-to-all-done.gathered, f32[256,896]{1,0:T(8,128)S(1)} %get-tuple-element.15.folded, s32[3,2048]{1,0:T(4,128)S(1)} %reshape.30.miller, ...), custom_call_target="tpu_custom_call" | custom-call | flops 10000000000 | bytes 65536 | tf_op jit(solution)/shard_map/pallas_call | solution.py:56
  41.6 14.5 %all_to_all.20 = bf16[16,48,128]{2,1,0:T(8,128)(2,1)S(1)} all-to-all(bf16[16,48,128]{2,1,0:T(8,128)(2,1)S(1)} %get-tuple-element.20), channel_id=1, replica_groups=mesh['dp'=16,'atom'=16] {'dp'}, dimensions={0} | all-to-all | bytes 393216 | tf_op jit(solution)/shard_map/all_to_all | solution.py:492
  56.2 14.4 %all_to_all.21.sums = bf16[16,48,128]{2,1,0:T(8,128)(2,1)S(1)} all-to-all(bf16[16,48,128]{2,1,0:T(8,128)(2,1)S(1)} %broadcast_in_dim.10), channel_id=1, replica_groups=mesh['dp'=16,'atom'=16] {'atom'}, dimensions={0} | all-to-all | bytes 393216 | tf_op jit(solution)/shard_map/all_to_all | solution.py:492
  70.6 0.7 shard_map.151
  71.3 0.7 broadcast_in_dim.11
  72.0 5.5 %all-to-all-start.3 = ((bf16[16,48,128]{2,1,0:T(8,128)(2,1)}), bf16[16,48,128]{2,1,0:T(8,128)(2,1)S(1)}, u32[]{:S(2)}, u32[]{:S(2)}) async-start(bf16[16,48,128]{2,1,0:T(8,128)(2,1)} %broadcast_in_dim.11), calls=%async_computation.3 | async-start | bytes 393216 | tf_op jit(solution)/shard_map/all_to_all | solution.py:492
  77.6 1.1 %copy-done.1 = bf16[3328,128]{1,0:T(8,128)(2,1)S(1)} copy-done((bf16[3328,128]{1,0:T(8,128)(2,1)S(1)}, bf16[3328,128]{1,0:T(8,128)(2,1)}, u32[]{:S(2)}) %copy-start.1) | copy-done | bytes 851992
  78.7 2.0 %shard_map.150 = bf16[1,128,128]{2,1,0:T(8,128)(2,1)} custom-call(s32[5]{0:T(128)S(1)} %pad_add_fusion.place, f32[144,3328]{1,0:T(8,128)S(1)} %get-tuple-element.17.factor, f32[256,896]{1,0:T(8,128)S(1)} %get-tuple-element.15.folded, bf16[3328,128]{1,0:T(8,128)(2,1)S(1)} %copy-done.1, bf16[128,256]{1,0:T(8,128)(2,1)S(1)} %maximum_bitcast_fusion.in_weight, ...), custom_call_target="tpu_custom_call" | custom-call | flops 1000000000 | bytes 65536 | tf_op jit(solution)/shard_map/pallas_call | solution.py:56
  80.7 3.7 %all-to-all-done.3.sums = bf16[16,48,128]{2,1,0:T(8,128)(2,1)S(1)} async-done(((bf16[16,48,128]{2,1,0:T(8,128)(2,1)}), bf16[16,48,128]{2,1,0:T(8,128)(2,1)S(1)}, u32[]{:S(2)}, u32[]{:S(2)}) %all-to-all-start.3) | async-done | bytes 196640 | tf_op jit(solution)/shard_map/all_to_all | solution.py:492
  84.4 0.7 shard_map.152
  (49 shorter events, 1.4 us)
Async XLA Ops:
  2.1 21.8 %collective-permute-start = (bf16[144,128]{1,0:T(8,128)(2,1)S(1)}, bf16[144,128]{1,0:T(8,128)(2,1)S(1)}, u32[]{:S(2)}, u32[]{:S(2)}) collective-permute-start(bf16[144,128]{1,0:T(8,128)(2,1)S(1)} %pad_maximum_fusion.own), channel_id=1, source_target_pairs={{0,1},{1,2},{2,3},{3,4},{4,5},{5,6},{6,7},{7,8},{8,9},{9,10},{10,1... | collective-permute-start | bytes 110600 | tf_op jit(solution)/shard_map/ppermute | solution.py:523
  4.6 19.4 %collective-permute-start.1 = (bf16[144,128]{1,0:T(8,128)(2,1)S(1)}, bf16[144,128]{1,0:T(8,128)(2,1)S(1)}, u32[]{:S(2)}, u32[]{:S(2)}) collective-permute-start(bf16[144,128]{1,0:T(8,128)(2,1)S(1)} %pad_maximum_fusion.own), channel_id=1, source_target_pairs={{1,0},{2,1},{3,2},{4,3},{5,4},{6,5},{7,6},{8,7},{9,8},{10,9},{11,1... | collective-permute-start | bytes 110600 | tf_op jit(solution)/shard_map/ppermute | solution.py:524
  11.2 7.9 %copy-start.6 = (bf16[128,128]{1,0:T(8,128)(2,1)S(1)}, bf16[128,128]{1,0:T(8,128)(2,1)}, u32[]{:S(2)}) copy-start(bf16[128,128]{1,0:T(8,128)(2,1)} %in_weight_hbm.1) | copy-start | bytes 98308
  11.2 8.2 %copy-start.18 = (s32[3,2048]{1,0:T(4,128)S(1)}, s32[3,2048]{1,0:T(4,128)}, u32[]{:S(2)}) copy-start(s32[3,2048]{1,0:T(4,128)} %param.18) | copy-start | bytes 73732
  12.9 7.3 %copy-start.15 = (f32[2048,128]{1,0:T(8,128)S(1)}, f32[2048,128]{1,0:T(8,128)}, u32[]{:S(2)}) copy-start(f32[2048,128]{1,0:T(8,128)} %param.22) | copy-start | bytes 3145732
  12.9 23.1 %all-to-all-start = ((bf16[16,160,128]{2,1,0:T(8,128)(2,1)}), bf16[16,160,128]{2,1,0:T(8,128)(2,1)S(1)}, u32[]{:S(2)}, u32[]{:S(2)}) async-start(bf16[16,160,128]{2,1,0:T(8,128)(2,1)} %fusion.1), calls=%async_computation | async-start | bytes 1310720 | tf_op jit(solution)/shard_map/all_to_all | solution.py:492
  19.2 0.6 copy-start.16
  20.0 0.7 copy-start.7
  20.2 3.7 %copy-start.5 = (bf16[1,128,128]{2,1,0:T(8,128)(2,1)S(1)}, bf16[1,128,128]{2,1,0:T(8,128)(2,1)}, u32[]{:S(2)}) copy-start(bf16[1,128,128]{2,1,0:T(8,128)(2,1)} %cot_hbm.1) | copy-start | bytes 98308
  20.2 3.7 %copy-start.8 = (bf16[384,128]{1,0:T(8,128)(2,1)S(1)}, bf16[384,128]{1,0:T(8,128)(2,1)}, u32[]{:S(2)}) copy-start(bf16[384,128]{1,0:T(8,128)(2,1)} %out_weight_hbm.1) | copy-start | bytes 294916
  20.3 3.7 %copy-start.9 = (s32[1,32,128]{2,1,0:T(8,128)S(1)}, s32[1,32,128]{2,1,0:T(8,128)}, u32[]{:S(2)}) copy-start(s32[1,32,128]{2,1,0:T(8,128)} %neighbours_hbm.1) | copy-start | bytes 49156
  20.3 3.7 %copy-start.10 = (s32[1,32,128]{2,1,0:T(8,128)S(1)}, s32[1,32,128]{2,1,0:T(8,128)}, u32[]{:S(2)}) copy-start(s32[1,32,128]{2,1,0:T(8,128)} %images_hbm.1) | copy-start | bytes 49156
  20.3 3.7 %copy-start.11 = (f32[3,8,128]{2,1,0:T(8,128)S(1)}, f32[3,8,128]{2,1,0:T(8,128)}, u32[]{:S(2)}) copy-start(f32[3,8,128]{2,1,0:T(8,128)} %radial_weight_hbm.1) | copy-start | bytes 36868
  20.3 3.7 %copy-start.12 = (s32[1,128]{1,0:T(1,128)S(1)}, s32[1,128]{1,0:T(1,128)}, u32[]{:S(2)}) copy-start(s32[1,128]{1,0:T(1,128)} %count_hbm.1) | copy-start | bytes 1540
  23.0 0.9 %copy-start = (bf16[3328,128]{1,0:T(8,128)(2,1)}, bf16[3328,128]{1,0:T(8,128)(2,1)S(1)}, u32[]{:S(2)}) copy-start(bf16[3328,128]{1,0:T(8,128)(2,1)S(1)} %get-tuple-element.18.table_own) | copy-start | bytes 2555908
  32.2 0.6 copy-start.3
  32.8 0.7 copy-start.13
  36.0 1.0 %copy-start.14 = (f32[512,128]{1,0:T(8,128)S(1)}, f32[512,128]{1,0:T(8,128)}, u32[]{:S(2)}) copy-start(f32[512,128]{1,0:T(8,128)} %copy-done.13) | copy-start | bytes 786436
  41.6 35.9 %copy-start.17 = (bf16[128,128]{0,1:T(8,128)(2,1)S(1)}, bf16[128,128]{0,1:T(8,128)(2,1)}, u32[]{:S(2)}) copy-start(bf16[128,128]{0,1:T(8,128)(2,1)} %copy-done.16) | copy-start | bytes 98308
  41.6 35.9 %copy-start.2 = (bf16[1,128,128]{2,1,0:T(8,128)(2,1)S(1)}, bf16[1,128,128]{2,1,0:T(8,128)(2,1)}, u32[]{:S(2)}) copy-start(bf16[1,128,128]{2,1,0:T(8,128)(2,1)} %feats.1) | copy-start | bytes 98308
  41.6 35.9 %copy-start.4 = (f32[128,128]{1,0:T(8,128)S(1)}, f32[128,128]{1,0:T(8,128)}, u32[]{:S(2)}) copy-start(f32[128,128]{1,0:T(8,128)} %copy-done.3) | copy-start | bytes 196612
  72.0 12.3 %all-to-all-start.3 = ((bf16[16,48,128]{2,1,0:T(8,128)(2,1)}), bf16[16,48,128]{2,1,0:T(8,128)(2,1)S(1)}, u32[]{:S(2)}, u32[]{:S(2)}) async-start(bf16[16,48,128]{2,1,0:T(8,128)(2,1)} %broadcast_in_dim.11), calls=%async_computation.3 | async-start | bytes 393216 | tf_op jit(solution)/shard_map/all_to_all | solution.py:492
  77.6 1.2 %copy-start.1 = (bf16[3328,128]{1,0:T(8,128)(2,1)S(1)}, bf16[3328,128]{1,0:T(8,128)(2,1)}, u32[]{:S(2)}) copy-start(bf16[3328,128]{1,0:T(8,128)(2,1)} %copy-done) | copy-start | bytes 2555908

commit v3 on v2

--- a/solution.py
+++ b/solution.py
@@ -30,13 +30,13 @@
 BASIS = WAVES * 2 * PLANE
 TILE = 256
 MINE = CH // SLABS
+QUARTER = CH // 4
 FRAC_AT = CH
-COT_AT = CH + 16
-PAY = COT_AT + 16
+HALO = CH + 16
+COT_AT, HID_AT, PAY = QUARTER, 2 * QUARTER, 2 * QUARTER + 16
 
 VMEM = pl.BlockSpec(memory_space=pltpu.VMEM)
 SMEM = pl.BlockSpec(memory_space=pltpu.SMEM)
-HBM = pl.BlockSpec(memory_space=pltpu.HBM)
 
 NN = (((1,), (0,)), ((), ()))
 NT = (((1,), (1,)), ((), ()))
@@ -66,24 +66,16 @@
     )(*[arg for _, arg in args])
 
 
-def fetch(pairs, sems):
-    copies = [
-        pltpu.make_async_copy(src, dst, sems.at[n]) for n, (src, dst) in enumerate(pairs)
-    ]
-    for copy in copies:
-        copy.start()
-    return copies
-
-
 def coordinates(frac):
-    rows = jnp.pad(frac, ((0, 5), (0, 0)))
+    rows = jnp.concatenate([frac, frac, jnp.zeros((10, frac.shape[1]), F32)], axis=0)
     first = jnp.floor(rows * 256.0) * (1.0 / 256.0)
-    return jnp.concatenate([first, rows - first], axis=0).astype(BF16)
-
-
-def joined_frac(block):
-    wide = block.astype(F32)
-    return wide[0:8] + wide[8:16]
+    top = lax.broadcasted_iota(I32, rows.shape, 0) < 3
+    return jnp.where(top, first, rows - first).astype(BF16)
+
+
+def joined_frac(rows):
+    wide = rows.astype(F32)
+    return [wide[d : d + 1] + wide[d + 3 : d + 4] for d in range(3)]
 
 
 ROOT3, ROOT5, ROOT15 = math.sqrt(3.0), math.sqrt(5.0), math.sqrt(15.0)
@@ -97,15 +89,6 @@
     own,
     left,
     right,
-    neighbours_hbm,
-    images_hbm,
-    count_hbm,
-    in_weight_hbm,
-    radial_weight_hbm,
-    out_weight_hbm,
-    cot_hbm,
-    early,
-    local,
     neighbours,
     images,
     count,
@@ -113,6 +96,8 @@
     radial_weight,
     out_weight,
     cot,
+    early,
+    local,
     ext,
     hot,
     weights,
@@ -125,22 +110,7 @@
     up9,
     pulled,
     inv,
-    sems,
 ):
-    copies = fetch(
-        (
-            (neighbours_hbm, neighbours),
-            (images_hbm, images),
-            (count_hbm, count),
-            (in_weight_hbm, in_weight),
-            (radial_weight_hbm, radial_weight),
-            (out_weight_hbm, out_weight),
-            (cot_hbm, cot),
-        ),
-        sems,
-    )
-    for copy in copies:
-        copy.wait()
     first, live_here, live_left, live_right = place[0], place[1], place[2], place[3]
     lane = lax.broadcasted_iota(I32, (CH, ROWS), 1)
     ext[:, 0:ROWS] = jnp.where(lane < live_here, own[0:CH].astype(F32), 0.0).astype(BF16)
@@ -153,11 +123,10 @@
     column = jnp.where(offset < ROWS + GHOST, offset, offset - (ATOMS - 2 * ROWS))
     at = column & (ROWS - 1)
     in_slab = column < ROWS
-    frac_own = joined_frac(own[FRAC_AT:COT_AT])
-    frac_left = joined_frac(left[FRAC_AT:COT_AT])
-    frac_right = joined_frac(right[FRAC_AT:COT_AT])
-    lane8 = lax.broadcasted_iota(I32, (8, ROWS), 1)
-    frac_far = jnp.where(lane8 < GHOST, frac_right, frac_left)
+    frac_own = joined_frac(own[FRAC_AT:HALO])
+    frac_left = joined_frac(left[FRAC_AT:HALO])
+    frac_right = joined_frac(right[FRAC_AT:HALO])
+    lane1 = lax.broadcasted_iota(I32, (1, ROWS), 1)
 
     code = images[0]
     ninth = (code * 57) >> 9
@@ -165,8 +134,9 @@
     shifts = (ninth, third - 3 * ninth, code - 3 * third)
     vector = []
     for d in range(3):
-        near = jnp.broadcast_to(frac_own[d : d + 1], (SLOTS, ROWS))
-        far = jnp.broadcast_to(frac_far[d : d + 1], (SLOTS, ROWS))
+        near = jnp.broadcast_to(frac_own[d], (SLOTS, ROWS))
+        far = jnp.where(lane1 < GHOST, frac_right[d], frac_left[d])
+        far = jnp.broadcast_to(far, (SLOTS, ROWS))
         other = jnp.where(
             in_slab,
             jnp.take_along_axis(near, at, axis=1),
@@ -281,14 +251,19 @@
         early[to : to + SLOTS, :] = grad_in[d * SLOTS : (d + 1) * SLOTS]
 
 
-def half_row(miller):
+def half_point(miller):
     m0, m1, m2 = miller[0:1], miller[1:2], miller[2:3]
     sign = jnp.where(m0 < 0, -1, 1)
     m0, m1, m2 = sign * m0, sign * m1, sign * m2
     minus = m1 < 0
     turn = jnp.where(minus, -1, 1)
-    row = m0 * PLANE + turn * m1 * SIDE + (turn * m2 + TOP)
-    return row + jnp.where(minus, HALF, 0)
+    plane = m0 + jnp.where(minus, TOP + 1, 0)
+    return plane, turn * m1 * SIDE + (turn * m2 + TOP)
+
+
+def one_hot(point):
+    row = lax.broadcasted_iota(I32, (PLANE, KVEC), 0)
+    return jnp.where(row == point, 1.0, 0.0).astype(BF16)
 
 
 def turns(frac_row, first, count):
@@ -311,41 +286,35 @@
 
 def waves(frac, plane):
     width = plane.shape[1]
-    c1, s1 = turns(frac[1:2], 0, 8)
-    c2, s2 = turns(frac[2:3], -TOP, 16)
+    c1, s1 = turns(frac[1], 0, 8)
+    c2, s2 = turns(frac[2], -TOP, 16)
     for k in (0, PLANE):
         plane[k + 88 : k + PLANE, :] = jnp.zeros((PLANE - 88, width), F32)
     for m in range(TOP + 1):
         cm, sm = c1[m : m + 1], s1[m : m + 1]
         plane[m * SIDE : m * SIDE + 16, :] = cm * c2 - sm * s2
         plane[PLANE + m * SIDE : PLANE + m * SIDE + 16, :] = sm * c2 + cm * s2
-    c0, s0 = turns(frac[0:1], 0, 8)
+    c0, s0 = turns(frac[0], 0, 8)
     return [c0[m : m + 1] for m in range(TOP + 1)] + [
         s0[m : m + 1] for m in range(1, TOP + 1)
     ]
 
 
-def one_hot(miller, hot):
-    row = half_row(miller[...])
-    point = lax.broadcasted_iota(I32, (2 * HALF, TILE), 0)
-    for k in range(KVEC // TILE):
-        here = slice(k * TILE, (k + 1) * TILE)
-        hot[:, here] = jnp.where(point == row[:, here], 1.0, 0.0).astype(BF16)
-
-
-def lattice_kernel(miller, filter_weight, frac, folded, table, hot, plane, pad):
-    one_hot(miller, hot)
-    hi, lo = split(filter_weight[...] * (1.0 / math.sqrt(KVEC * ATOMS)))
-    both = dot(hot[...], jnp.concatenate([hi, lo], axis=1), NN)
-    both = both[:, 0:CH] + both[:, CH : 2 * CH]
-    folded[0:CH, :] = (both[0:HALF] + both[HALF : 2 * HALF]).T
-    folded[CH : 2 * CH, :] = (both[0:HALF] - both[HALF : 2 * HALF]).T
-    pad[...] = jnp.zeros((8, ROWS), F32)
-    for d in range(3):
-        pad[d : d + 1, :] = frac[d]
-    for f, wave in enumerate(waves(pad[...], plane)):
-        here = slice(f * 2 * PLANE, (f + 1) * 2 * PLANE)
-        table[here, :] = (wave * plane[...]).astype(BF16)
+def lattice_kernel(place, miller, filter_weight, folded, turned, wide):
+    plane, point = half_point(miller[...])
+    turned[...] = filter_weight[...].T * (1.0 / math.sqrt(KVEC * ATOMS))
+    mine = turned[pl.ds(pl.multiple_of(place[5], QUARTER), QUARTER), :]
+    for b in range(2 * (TOP + 1)):
+        here = slice(b * QUARTER, (b + 1) * QUARTER)
+        wide[here, :] = jnp.where(plane == b, mine, 0.0).astype(BF16)
+    sums = dot(wide[...], one_hot(point), NT)
+    half = (TOP + 1) * QUARTER
+    for m in range(TOP + 1):
+        here = slice(m * QUARTER, (m + 1) * QUARTER)
+        there = slice(half + m * QUARTER, half + (m + 1) * QUARTER)
+        lanes = slice(m * PLANE, (m + 1) * PLANE)
+        folded[0:QUARTER, lanes] = sums[here] + sums[there]
+        folded[QUARTER : 2 * QUARTER, lanes] = sums[here] - sums[there]
 
 
 def blocks(x, m):
@@ -373,50 +342,31 @@
 
 
 def spectrum_kernel(
-    place,
-    gathered,
-    folded,
-    miller,
-    own_weight,
-    early,
-    parts,
-    factor,
-    hot,
-    frac,
-    values,
-    plane,
-    wide,
+    place, gathered, folded, miller, early, parts, ewald, factor, frac, values, plane, wide
 ):
     for p in range(SLABS):
         here = slice(p * ROWS, (p + 1) * ROWS)
-        values[0:CH, here] = gathered[p, 0:CH]
-        values[CH : CH + 16, here] = gathered[p, COT_AT:PAY]
-        frac[:, here] = joined_frac(gathered[p, FRAC_AT:COT_AT])
-    rows = CH + 16
-    along = waves(frac[...], plane)
+        values[:, here] = gathered[p]
+        tail = gathered[p, HID_AT:PAY].astype(F32)
+        frac[0:3, here] = tail[MINE : MINE + 3] + tail[MINE + 3 : MINE + 6]
+    along = waves([frac[d : d + 1, :] for d in range(3)], plane)
     live = (lax.broadcasted_iota(I32, (1, ATOMS), 1) < place[0] + place[1]).astype(F32)
     around = plane[...].astype(BF16)
     for low, high in ((0, TOP + 1), (TOP + 1, WAVES)):
         for f in range(low, high):
-            wide[f * rows : (f + 1) * rows, :] = (
+            wide[f * PAY : (f + 1) * PAY, :] = (
                 values[...].astype(F32) * (along[f] * live)
             ).astype(BF16)
-        both = dot(wide[low * rows : high * rows, :], around, NT)
+        both = dot(wide[low * PAY : high * PAY, :], around, NT)
         for f in range(low, high):
             here = slice(f * 2 * PLANE, (f + 1) * 2 * PLANE)
-            factor[:, here] = both[(f - low) * rows : (f - low + 1) * rows]
-        if low == 0:
-            one_hot(miller, hot)
-
-    top = pl.multiple_of(place[4], MINE)
-    feats_hi, feats_lo = split(factor[0:CH, :])
-    s = dot(own_weight[...], jnp.concatenate([feats_hi, feats_lo], axis=0), NN)[0:MINE]
-    g = factor[CH : CH + MINE, :]
-    plus = folded[pl.ds(top, MINE), :]
-    minus = folded[pl.ds(pl.multiple_of(CH + top, MINE), MINE), :]
-    grad = split(jnp.concatenate(filtered(plus, minus, g), axis=1))
-    grad_in = dot(jnp.concatenate(grad, axis=0), feats_hi, NT)
-    grad_in = grad_in[0:MINE] + grad_in[MINE : 2 * MINE]
+            factor[:, here] = both[(f - low) * PAY : (f - low + 1) * PAY]
+
+    at = pl.multiple_of(place[4] - place[5], MINE)
+    s = factor[HID_AT : HID_AT + MINE, :]
+    g = factor[pl.ds(pl.multiple_of(COT_AT + at, MINE), MINE), :]
+    plus = folded[pl.ds(at, MINE), :]
+    minus = folded[pl.ds(pl.multiple_of(QUARTER + at, MINE), MINE), :]
     pair_plus, pair_minus = [], []
     for m in range(TOP + 1):
         cc, ss, sc, cs = blocks(s, m)
@@ -427,54 +377,78 @@
             odd = sc * gcs + cs * gsc - cc * gss - ss * gcc
         pair_plus.append(even + odd)
         pair_minus.append(even - odd)
-    pair = jnp.concatenate(pair_plus + pair_minus, axis=1)
+    pair = jnp.concatenate(pair_plus + pair_minus, axis=0)
     pair = split(pair * (1.0 / math.sqrt(KVEC * ATOMS)))
-    pair = dot(jnp.concatenate(pair, axis=0), hot[...], NN)
-    pair = pair[0:MINE] + pair[MINE : 2 * MINE]
+    around_plane, point = half_point(miller[...])
+    found = dot(jnp.concatenate(pair, axis=0), one_hot(point), NN)
+    planes = 2 * (TOP + 1)
+    pair = jnp.zeros((MINE, KVEC), F32)
+    for b in range(planes):
+        value = found[b * MINE : (b + 1) * MINE] + found[(planes + b) * MINE : (planes + b + 1) * MINE]
+        pair = jnp.where(around_plane == b, value, pair)
+    grad = filtered(
+        folded[0:QUARTER, :],
+        folded[QUARTER : 2 * QUARTER, :],
+        factor[COT_AT:HID_AT, :],
+    )
+    grad = jnp.concatenate(split(jnp.concatenate(grad, axis=1)), axis=0)
+    block = dot(grad, factor[0:QUARTER, :].astype(BF16), NT)
+    block = block[0:QUARTER] + block[QUARTER : 2 * QUARTER]
+    block = jnp.concatenate([block[8 * q : 8 * q + 8] for q in range(4)], axis=1)
     for d in range(STRUCTS):
         parts[d, 0:16, :] = jnp.concatenate(
-            [pair[:, d * KSHARE : (d + 1) * KSHARE], grad_in], axis=0
+            [pair[:, d * KSHARE : (d + 1) * KSHARE], block], axis=0
         ).astype(BF16)
         parts[d, 16:48, :] = early[d * SLOTS : (d + 1) * SLOTS, :].astype(BF16)
+    coef = filtered(plus, minus, s)
+    coef = [
+        jnp.concatenate([coef[2 * f], coef[2 * f + 1]], axis=1) for f in range(WAVES)
+    ]
+    field = dot(jnp.concatenate(coef, axis=0).astype(BF16), around, NN)
+    total = field[0:MINE] * along[0]
+    for f in range(1, WAVES):
+        total = total + field[f * MINE : (f + 1) * MINE] * along[f]
+    for p in range(SLABS):
+        ewald[p] = total[:, p * ROWS : (p + 1) * ROWS].astype(BF16)
 
 
 SPECTRUM_SCRATCH = [
-    pltpu.VMEM((2 * HALF, KVEC), BF16),
+    pltpu.VMEM((PAY, BASIS), F32),
     pltpu.VMEM((8, ATOMS), F32),
-    pltpu.VMEM((CH + 16, ATOMS), BF16),
+    pltpu.VMEM((PAY, ATOMS), BF16),
     pltpu.VMEM((2 * PLANE, ATOMS), F32),
-    pltpu.VMEM((WAVES * (CH + 16), ATOMS), BF16),
+    pltpu.VMEM((WAVES * PAY, ATOMS), BF16),
 ]
 
 
-def update_kernel(
-    place, factor, folded, table_own, in_weight, feats, local, updated, coef
-):
-    both = jnp.concatenate(split(factor[0:CH, :]), axis=0)
-    s = dot(in_weight[...], both, NN)
-    pieces = filtered(folded[0:CH, :], folded[CH : 2 * CH, :], s)
-    for n, piece in enumerate(pieces):
-        coef[:, n * PLANE : (n + 1) * PLANE] = piece.astype(BF16)
-    ewald = dot(coef[...], table_own[...], NN)
+def middle_kernel(place, sums, feats, local, last, grad_in, updated):
+    row = lax.broadcasted_iota(I32, (8, KSHARE), 0)
+    lane = lax.broadcasted_iota(I32, (8, KSHARE), 1)
+    pick = jnp.where(lane == row + place[4], 1.0, 0.0).astype(BF16)
+    blocks = [sums[p].astype(F32) for p in range(SLABS)]
+    pairs = jnp.concatenate([block[0:8] for block in blocks], axis=0)
+    picked = dot(pick, pairs.astype(BF16), NT)
+    total = blocks[0][16:48]
+    for block in blocks[1:]:
+        total = total + block[16:48]
+    out = jnp.concatenate([total, picked, picked], axis=0).astype(BF16)
+    for d in range(STRUCTS):
+        last[d] = out
+    grads = []
+    for c in range(0, CH, 8):
+        at, g = c % QUARTER // 8, c // QUARTER
+        eight = blocks[4 * g][8:16]
+        eight = pltpu.roll(eight, (0 - at) * QUARTER % CH, 1)
+        for q in range(1, 4):
+            turned = pltpu.roll(blocks[4 * g + q][8:16], (q - at) * QUARTER % CH, 1)
+            eight = jnp.where(lane < q * QUARTER, eight, turned)
+        grads.append(eight)
+    grad_in[...] = jnp.concatenate(grads, axis=0).T
+    ewald = jnp.concatenate([block[48:56] for block in blocks], axis=0)
     here = lax.broadcasted_iota(I32, (CH, ROWS), 1) < place[1]
     updated[0] = jnp.where(
         here, feats[0].astype(F32) + local[...] + ewald, 0.0
     ).astype(BF16)
-
-
-def middle_kernel(place, sums, last, grad_in):
-    row = lax.broadcasted_iota(I32, (8, KSHARE), 0)
-    lane = lax.broadcasted_iota(I32, (8, KSHARE), 1)
-    pick = jnp.where(lane == row + place[4], 1.0, 0.0).astype(BF16)
-    pairs = jnp.concatenate([sums[p, 0:16].astype(F32)[0:8] for p in range(SLABS)], axis=0)
-    grads = jnp.concatenate([sums[p, 0:16].astype(F32)[8:16] for p in range(SLABS)], axis=0)
-    grad_in[...] = grads.T
-    total = sums[0, 16:48].astype(F32)
-    for p in range(1, SLABS):
-        total = total + sums[p, 16:48].astype(F32)
-    last[0:32] = total.astype(BF16)
-    picked = dot(pick, pairs.astype(BF16), NT)
-    last[32:48] = jnp.concatenate([picked, picked], axis=0).astype(BF16)
 
 
 def finish_kernel(sums, ewald_in, grad_filter, grad_in, grad_out):
@@ -490,10 +464,6 @@
 
 def exchange(x, axis):
     return lax.all_to_all(x, axis, 0, 0)
-
-
-def to_all(x, axis, count):
-    return exchange(jnp.broadcast_to(x[None], (count,) + x.shape), axis)
 
 
 def shards(
@@ -515,55 +485,46 @@
     live = atom_count[0] - jnp.stack(
         [first, (first - ROWS) % ATOMS, (first + ROWS) % ATOMS]
     )
-    place = jnp.concatenate([first[None], live, slab[None] * MINE]).astype(I32)
+    place = jnp.stack([slab * MINE, slab // 4 * QUARTER])
+    place = jnp.concatenate([first[None], live, place]).astype(I32)
     struct = jax.ShapeDtypeStruct
 
-    halo = jnp.concatenate([node_feats[0], coordinates(frac[0])], axis=0)
+    feats = node_feats[0]
+    halo = jnp.concatenate([feats, coordinates(frac[0])], axis=0)
+    where = halo[FRAC_AT : FRAC_AT + 8]
     ring = range(SLABS)
     left = lax.ppermute(halo, "atom", [(i, (i + 1) % SLABS) for i in ring])
     right = lax.ppermute(halo, "atom", [((i + 1) % SLABS, i) for i in ring])
-    cot_parts = jnp.pad(cotangent.reshape(SLABS, MINE, ROWS), ((0, 0), (0, 8), (0, 0)))
-    gathered = exchange(
-        jnp.concatenate(
-            [jnp.broadcast_to(halo[None], (SLABS, COT_AT, ROWS)), cot_parts], axis=1
-        ),
-        "atom",
-    )
-    frac = frac.transpose(1, 0, 2)
-
-    order = (SLABS, STRUCTS, KVEC // SLABS // STRUCTS)
-    miller = miller.reshape((3,) + order).transpose(0, 2, 1, 3).reshape(3, KVEC)
-    filter_weight = (
-        filter_weight.reshape(order + (CH,)).transpose(1, 0, 2, 3).reshape(KVEC, CH)
-    )
-    folded, table_own = call(
+    hidden = dot(in_weight, feats, TN).astype(BF16)
+    square = (4, 4, QUARTER, ROWS)
+    payload = [
+        jnp.broadcast_to(feats.reshape(1, 4, QUARTER, ROWS), square),
+        jnp.broadcast_to(cotangent[0].reshape(4, 1, QUARTER, ROWS), square),
+        hidden.reshape(4, 4, MINE, ROWS),
+        jnp.broadcast_to(where, (4, 4, 8, ROWS)),
+    ]
+    payload = jnp.concatenate(payload, axis=2).reshape(SLABS, PAY, ROWS)
+    gathered = exchange(payload, "atom")
+
+    (folded,) = call(
         lattice_kernel,
+        [(VMEM, struct((2 * QUARTER, HALF), F32))],
         [
-            (VMEM, struct((2 * CH, HALF), F32)),
-            (VMEM, struct((BASIS, ROWS), BF16)),
+            pltpu.VMEM((CH, KVEC), F32),
+            pltpu.VMEM((2 * (TOP + 1) * QUARTER, KVEC), BF16),
         ],
-        [
-            pltpu.VMEM((2 * HALF, KVEC), BF16),
-            pltpu.VMEM((2 * PLANE, ROWS), F32),
-            pltpu.VMEM((8, ROWS), F32),
-        ],
-        24,
+        12,
         10**8,
+        (SMEM, place),
         (VMEM, miller),
         (VMEM, filter_weight),
-        (VMEM, frac),
-    )
+    )
+    order = (3, SLABS, STRUCTS, KVEC // SLABS // STRUCTS)
+    miller = miller.reshape(order).transpose(0, 2, 1, 3).reshape(3, KVEC)
     early, local = call(
         edge_kernel,
         [(VMEM, struct((4 * CH, CH), F32)), (VMEM, struct((CH, ROWS), F32))],
         [
-            pltpu.VMEM((1, SLOTS, ROWS), I32),
-            pltpu.VMEM((1, SLOTS, ROWS), I32),
-            pltpu.VMEM((1, ROWS), I32),
-            pltpu.VMEM((CH, CH), BF16),
-            pltpu.VMEM((3, NB, CH), F32),
-            pltpu.VMEM((3 * CH, CH), BF16),
-            pltpu.VMEM((1, CH, ROWS), BF16),
             pltpu.VMEM((CH, 2 * ROWS), BF16),
             pltpu.VMEM((2 * ROWS, EDGES), BF16),
             pltpu.VMEM((32, 3 * CH), F32),
@@ -576,64 +537,52 @@
             pltpu.VMEM((3 * CH, ROWS), F32),
             pltpu.VMEM((CH, EDGES), BF16),
             pltpu.VMEM((3 * CH, ROWS), BF16),
-            pltpu.SemaphoreType.DMA((7,)),
         ],
-        24,
+        20,
         EDGE_COST,
         (SMEM, place),
         (VMEM, halo),
         (VMEM, left),
         (VMEM, right),
-        (HBM, neighbours),
-        (HBM, images),
-        (HBM, neighbour_count),
-        (HBM, in_weight),
-        (HBM, radial_weight),
-        (HBM, out_weight),
-        (HBM, cotangent),
-    )
-    weight_t = jnp.concatenate([in_weight, in_weight], axis=0).T
-    own_weight = lax.dynamic_slice_in_dim(in_weight, slab * MINE, MINE, 1)
-    own_weight = jnp.pad(jnp.concatenate([own_weight, own_weight], axis=0).T, ((0, 8), (0, 0)))
-    parts, factor = call(
+        (VMEM, neighbours),
+        (VMEM, images),
+        (VMEM, neighbour_count),
+        (VMEM, in_weight),
+        (VMEM, radial_weight),
+        (VMEM, out_weight),
+        (VMEM, cotangent),
+    )
+    parts, ewald = call(
         spectrum_kernel,
         [
             (VMEM, struct((STRUCTS, 48, CH), BF16)),
-            (VMEM, struct((CH + 16, BASIS), F32)),
+            (VMEM, struct((SLABS, MINE, ROWS), BF16)),
         ],
         SPECTRUM_SCRATCH,
-        32,
+        20,
         10**10,
         (SMEM, place),
         (VMEM, gathered),
         (VMEM, folded),
         (VMEM, miller),
-        (VMEM, own_weight),
         (VMEM, early),
     )
-    (updated,) = call(
-        update_kernel,
-        [(VMEM, struct((1, CH, ROWS), BF16))],
-        [pltpu.VMEM((CH, BASIS), BF16)],
-        24,
-        10**9,
-        (SMEM, place),
-        (VMEM, factor),
-        (VMEM, folded),
-        (VMEM, table_own),
-        (VMEM, weight_t),
-        (VMEM, node_feats),
-        (VMEM, local),
-    )
     sums = exchange(parts, "dp").astype(F32).sum(axis=0).astype(BF16)
-    last, ewald_in = call(
+    sums = jnp.broadcast_to(sums[None], (SLABS, 48, CH))
+    last, ewald_in, updated = call(
         middle_kernel,
-        [(VMEM, struct((48, CH), BF16)), (VMEM, struct((CH, CH), F32))],
+        [
+            (VMEM, struct((STRUCTS, 48, CH), BF16)),
+            (VMEM, struct((CH, CH), F32)),
+            (VMEM, struct((1, CH, ROWS), BF16)),
+        ],
         [],
         16,
         10**6,
         (SMEM, place),
-        (VMEM, to_all(sums, "atom", SLABS)),
+        (VMEM, exchange(jnp.concatenate([sums, ewald], axis=1), "atom")),
+        (VMEM, node_feats),
+        (VMEM, local),
     )
     grads = call(
         finish_kernel,
@@ -645,7 +594,7 @@
         [],
         16,
         10**6,
-        (VMEM, to_all(last, "dp", STRUCTS)),
+        (VMEM, exchange(last, "dp")),
         (VMEM, ewald_in),
     )
     return (updated, *grads)

time: 85.7 us -> 78.8 us (0.919)
  blocking collectives: 28.9 us -> 43.2 us
  waiting for transfers between devices: 6.11 us -> 0.01 us
  starting transfers between devices: 20.1 us -> 14.6 us
  local copies, waits for them, and re-layouts: 7.17 us -> 2.7 us
  Pallas kernels: 18.6 us -> 14.2 us
    all_to_all x2 -> x3, blocking collectives: 28.9 us -> 43.2 us  [exchange(): return lax.all_to_all(x, axis, 0, 0)]
    all_to_all x2 -> x1, waiting for transfers between devices: 6.11 us -> 0.01 us  [exchange(): return lax.all_to_all(x, axis, 0, 0)]
    all_to_all x2 -> x1, starting transfers between devices: 11 us -> 5.52 us  [exchange(): return lax.all_to_all(x, axis, 0, 0)]
    pallas_call x6 -> x5, Pallas kernels: 18.6 us -> 14.2 us  [call(): pl.pallas_call(kernel, out_shape=[shape for _, shape in outs], in_specs=[...]
    unnamed x40 -> x25, local copies, waits for them, and re-layouts: 5.65 us -> 1.47 us
    concatenate x3 -> x4, other arithmetic: 2.51 us -> 1.67 us  [the longest x1 0.81 us: shards(): halo = jnp.concatenate([feats, coordinates(frac[0])], axis=0)]
  transfers between devices with their start and end apart: 4 -> 3, of which waited for: 2 -> 0; matrix products, arithmetic and copies ran while one was open for 3% -> 2% of each run, Pallas kernels for 15% -> 12%
where the time goes in v3:
time: 78.8 us; the launch traced here: 78.3 us
  blocking collectives  43.2 us (55%)
  starting transfers between devices  14.6 us (19%)
  Pallas kernels  14.2 us (18%)
  local copies, waits for them, and re-layouts  2.7 us (3%)
  other arithmetic  1.87 us (2%)
  between operations  1.56 us (2%)
    all_to_all x3, blocking collectives, exchange(): return lax.all_to_all(x, axis, 0, 0)  43.2 us
    pallas_call x5, Pallas kernels, call(): pl.pallas_call(kernel, out_shape=[shape for _, shape in outs], in_specs=[...  14.2 us
    ppermute x1, starting transfers between devices, shards(): right = lax.ppermute(halo, 'atom', [((i + 1) % SLABS, i) for i in ring])  6.57 us
    all_to_all x1, starting transfers between devices, exchange(): return lax.all_to_all(x, axis, 0, 0)  5.52 us
    ppermute x1, starting transfers between devices, shards(): left = lax.ppermute(halo, 'atom', [(i, (i + 1) % SLABS) for i in ring])  2.47 us
  transfers between devices with their start and end apart: 3, of which 0 were waited for; matrix products, arithmetic and copies ran while one was open for 2% of the time, Pallas kernels for 12%

profile of v3, /device:TPU:1, one launch (start us, length us, event | category | flops | bytes accessed | tf_op | source)
XLA Modules:
  0.0 78.3 jit_solution(7559885932177658369)
XLA Ops:
  0.7 0.7 copy-done.11
  1.3 0.1 pad.10.clone
  1.4 0.1 fusion.1
  1.5 0.8 %pad_maximum_fusion.2.own = bf16[144,128]{1,0:T(8,128)(2,1)S(1)} fusion(bf16[16,128]{1,0:T(8,128)(2,1)S(1)} %fusion.1, bf16[128,128]{1,0:T(8,128)(2,1)} %bitcast.23), kind=kLoop, calls=%fused_computation.4 | loop fusion | flops 73728 | bytes 73728 | tf_op jit(solution)/shard_map/concatenate | solution.py:493
  2.3 2.5 %collective-permute-start = (bf16[144,128]{1,0:T(8,128)(2,1)S(1)}, bf16[144,128]{1,0:T(8,128)(2,1)S(1)}, u32[]{:S(2)}, u32[]{:S(2)}) collective-permute-start(bf16[144,128]{1,0:T(8,128)(2,1)S(1)} %pad_maximum_fusion.2.own), channel_id=1, source_target_pairs={{0,1},{1,2},{2,3},{3,4},{4,5},{5,6},{6,7},{7,8},{8,9},{9,10},{10,1... | collective-permute-start | bytes 110600 | tf_op jit(solution)/shard_map/ppermute | solution.py:496
  4.8 6.6 %collective-permute-start.1 = (bf16[144,128]{1,0:T(8,128)(2,1)S(1)}, bf16[144,128]{1,0:T(8,128)(2,1)S(1)}, u32[]{:S(2)}, u32[]{:S(2)}) collective-permute-start(bf16[144,128]{1,0:T(8,128)(2,1)S(1)} %pad_maximum_fusion.2.own), channel_id=1, source_target_pairs={{1,0},{2,1},{3,2},{4,3},{5,4},{6,5},{7,6},{8,7},{9,8},{10,9},{11,1... | collective-permute-start | bytes 110600 | tf_op jit(solution)/shard_map/ppermute | solution.py:497
  11.4 0.2 fusion
  11.6 0.5 slice-done
  12.1 0.8 copy-done.4
  12.9 0.8 pad_maximum_fusion
  13.6 5.5 %all-to-all-start = ((bf16[16,80,128]{2,1,0:T(8,128)(2,1)}), bf16[16,80,128]{2,1,0:T(8,128)(2,1)S(1)}, u32[]{:S(2)}, u32[]{:S(2)}) async-start(bf16[16,80,128]{2,1,0:T(8,128)(2,1)} %pad_maximum_fusion), calls=%async_computation | async-start | bytes 655360 | tf_op jit(solution)/shard_map/all_to_all | solution.py:466
  19.8 0.1 add_subtract_fusion
  19.9 0.1 pad_add_fusion.place
  20.0 0.2 reshape.24
  20.2 0.1 copy.17
  20.4 0.2 reshape.25.miller
  20.7 1.5 %shard_map.147.folded = f32[64,896]{1,0:T(8,128)S(1)} custom-call(s32[6]{0:T(128)S(1)} %pad_add_fusion.place, s32[3,2048]{1,0:T(4,128)S(1)} %copy-done.2, f32[2048,128]{1,0:T(8,128)S(1)} %copy-done), custom_call_target="tpu_custom_call" | custom-call | flops 100000000 | bytes 65536 | tf_op jit(solution)/shard_map/pallas_call | solution.py:56
  22.2 7.6 %shard_map.148 = (f32[512,128]{1,0:T(8,128)S(1)}, f32[128,128]{1,0:T(8,128)S(1)}) custom-call(s32[6]{0:T(128)S(1)} %pad_add_fusion.place, bf16[144,128]{1,0:T(8,128)(2,1)S(1)} %pad_maximum_fusion.2.own, bf16[144,128]{1,0:T(8,128)(2,1)S(1)} %collective-permute-done.left, bf16[144,128]{1,0:T(8,128)(2,1)S(1)} %collective-permute-done.1.right, ...), custom_call_target="tpu_custom_call" | custom-call | flops 10000000000 | bytes 65536 | tf_op jit(solution)/shard_map/pallas_call | solution.py:56
  29.9 3.1 %shard_map.149 = (bf16[16,48,128]{2,1,0:T(8,128)(2,1)S(1)}, bf16[16,8,128]{2,1,0:T(8,128)(2,1)S(1)}) custom-call(s32[6]{0:T(128)S(1)} %pad_add_fusion.place, bf16[16,80,128]{2,1,0:T(8,128)(2,1)S(1)} %all-to-all-done.gathered, f32[64,896]{1,0:T(8,128)S(1)} %shard_map.147.folded, s32[3,2048]{1,0:T(4,128)S(1)} %reshape.25.miller, ...), custom_call_target="tpu_custom_call" | custom-call | flops 10000000000 | bytes 65536 | tf_op jit(solution)/shard_map/pallas_call | solution.py:56
  33.0 14.0 %all_to_all.20 = bf16[16,48,128]{2,1,0:T(8,128)(2,1)S(1)} all-to-all(bf16[16,48,128]{2,1,0:T(8,128)(2,1)S(1)} %get-tuple-element.15), channel_id=1, replica_groups=mesh['dp'=16,'atom'=16] {'dp'}, dimensions={0} | all-to-all | bytes 393216 | tf_op jit(solution)/shard_map/all_to_all | solution.py:466
  47.1 17.5 %all_to_all.21.sums = bf16[16,56,128]{2,1,0:T(8,128)(2,1)S(1)} all-to-all(bf16[16,56,128]{2,1,0:T(8,128)(2,1)S(1)} %pad_maximum_fusion.1), channel_id=1, replica_groups=mesh['dp'=16,'atom'=16] {'atom'}, dimensions={0} | all-to-all | bytes 458752 | tf_op jit(solution)/shard_map/all_to_all | solution.py:466
  64.6 1.3 %shard_map.150 = (bf16[16,48,128]{2,1,0:T(8,128)(2,1)S(1)}, f32[128,128]{1,0:T(8,128)S(1)}, bf16[1,128,128]{2,1,0:T(8,128)(2,1)}) custom-call(s32[6]{0:T(128)S(1)} %pad_add_fusion.place, bf16[16,56,128]{2,1,0:T(8,128)(2,1)S(1)} %all_to_all.21.sums, bf16[1,128,128]{2,1,0:T(8,128)(2,1)S(1)} %copy-done.1, f32[128,128]{1,0:T(8,128)S(1)} %get-tuple-element.17.local), custom_call_target="tpu_custom_call" | custom-call | flops 1000000 | bytes 65536 | tf_op jit(solution)/shard_map/pallas_call | solution.py:56
  65.9 11.7 %all_to_all.22.sums = bf16[16,48,128]{2,1,0:T(8,128)(2,1)S(1)} all-to-all(bf16[16,48,128]{2,1,0:T(8,128)(2,1)S(1)} %get-tuple-element.19), channel_id=1, replica_groups=mesh['dp'=16,'atom'=16] {'dp'}, dimensions={0} | all-to-all | bytes 393216 | tf_op jit(solution)/shard_map/all_to_all | solution.py:466
  77.6 0.7 shard_map.151
  (35 shorter events, 0.2 us)
Async XLA Ops:
  0.6 0.7 copy-start.11
  1.5 9.9 %copy-start.10 = (bf16[16,128]{1,0:T(8,128)(2,1)}, bf16[16,128]{1,0:T(8,128)(2,1)S(1)}, u32[]{:S(2)}) copy-start(bf16[16,128]{1,0:T(8,128)(2,1)S(1)} %fusion.1) | copy-start | bytes 12292
  1.5 9.9 %copy-start.1 = (bf16[1,128,128]{2,1,0:T(8,128)(2,1)S(1)}, bf16[1,128,128]{2,1,0:T(8,128)(2,1)}, u32[]{:S(2)}) copy-start(bf16[1,128,128]{2,1,0:T(8,128)(2,1)} %feats.1) | copy-start | bytes 98308
  1.5 9.9 %copy-start.3 = (bf16[128,128]{1,0:T(8,128)(2,1)S(1)}, bf16[128,128]{1,0:T(8,128)(2,1)}, u32[]{:S(2)}) copy-start(bf16[128,128]{1,0:T(8,128)(2,1)} %in_weight.1) | copy-start | bytes 98308
  2.3 19.9 %collective-permute-start = (bf16[144,128]{1,0:T(8,128)(2,1)S(1)}, bf16[144,128]{1,0:T(8,128)(2,1)S(1)}, u32[]{:S(2)}, u32[]{:S(2)}) collective-permute-start(bf16[144,128]{1,0:T(8,128)(2,1)S(1)} %pad_maximum_fusion.2.own), channel_id=1, source_target_pairs={{0,1},{1,2},{2,3},{3,4},{4,5},{5,6},{6,7},{7,8},{8,9},{9,10},{10,1... | collective-permute-start | bytes 110600 | tf_op jit(solution)/shard_map/ppermute | solution.py:496
  4.8 17.4 %collective-permute-start.1 = (bf16[144,128]{1,0:T(8,128)(2,1)S(1)}, bf16[144,128]{1,0:T(8,128)(2,1)S(1)}, u32[]{:S(2)}, u32[]{:S(2)}) collective-permute-start(bf16[144,128]{1,0:T(8,128)(2,1)S(1)} %pad_maximum_fusion.2.own), channel_id=1, source_target_pairs={{1,0},{2,1},{3,2},{4,3},{5,4},{6,5},{7,6},{8,7},{9,8},{10,9},{11,1... | collective-permute-start | bytes 110600 | tf_op jit(solution)/shard_map/ppermute | solution.py:497
  11.4 0.7 slice-start
  12.0 0.8 copy-start.4
  12.9 7.1 %copy-start.2 = (s32[3,2048]{1,0:T(4,128)S(1)}, s32[3,2048]{1,0:T(4,128)}, u32[]{:S(2)}) copy-start(s32[3,2048]{1,0:T(4,128)} %miller.1) | copy-start | bytes 73732
  13.6 7.0 %copy-start = (f32[2048,128]{1,0:T(8,128)S(1)}, f32[2048,128]{1,0:T(8,128)}, u32[]{:S(2)}) copy-start(f32[2048,128]{1,0:T(8,128)} %filter_weight.1) | copy-start | bytes 3145732
  13.6 16.2 %all-to-all-start = ((bf16[16,80,128]{2,1,0:T(8,128)(2,1)}), bf16[16,80,128]{2,1,0:T(8,128)(2,1)S(1)}, u32[]{:S(2)}, u32[]{:S(2)}) async-start(bf16[16,80,128]{2,1,0:T(8,128)(2,1)} %pad_maximum_fusion), calls=%async_computation | async-start | bytes 655360 | tf_op jit(solution)/shard_map/all_to_all | solution.py:466
  20.6 1.6 %copy-start.5 = (bf16[384,128]{1,0:T(8,128)(2,1)S(1)}, bf16[384,128]{1,0:T(8,128)(2,1)}, u32[]{:S(2)}) copy-start(bf16[384,128]{1,0:T(8,128)(2,1)} %out_weight.1) | copy-start | bytes 294916
  20.6 1.6 %copy-start.6 = (s32[1,32,128]{2,1,0:T(8,128)S(1)}, s32[1,32,128]{2,1,0:T(8,128)}, u32[]{:S(2)}) copy-start(s32[1,32,128]{2,1,0:T(8,128)} %neighbours.1) | copy-start | bytes 49156
  20.6 1.6 %copy-start.7 = (s32[1,32,128]{2,1,0:T(8,128)S(1)}, s32[1,32,128]{2,1,0:T(8,128)}, u32[]{:S(2)}) copy-start(s32[1,32,128]{2,1,0:T(8,128)} %images.1) | copy-start | bytes 49156
  20.6 1.6 %copy-start.8 = (f32[3,8,128]{2,1,0:T(8,128)S(1)}, f32[3,8,128]{2,1,0:T(8,128)}, u32[]{:S(2)}) copy-start(f32[3,8,128]{2,1,0:T(8,128)} %radial_weight.1) | copy-start | bytes 36868
  20.7 1.6 %copy-start.9 = (s32[1,128]{1,0:T(1,128)S(1)}, s32[1,128]{1,0:T(1,128)}, u32[]{:S(2)}) copy-start(s32[1,128]{1,0:T(1,128)} %count.1) | copy-start | bytes 1540

commit v4 on v3

--- a/solution.py
+++ b/solution.py
@@ -37,6 +37,7 @@
 
 VMEM = pl.BlockSpec(memory_space=pltpu.VMEM)
 SMEM = pl.BlockSpec(memory_space=pltpu.SMEM)
+HBM = pl.BlockSpec(memory_space=pltpu.HBM)
 
 NN = (((1,), (0,)), ((), ()))
 NT = (((1,), (1,)), ((), ()))
@@ -66,11 +67,39 @@
     )(*[arg for _, arg in args])
 
 
-def coordinates(frac):
-    rows = jnp.concatenate([frac, frac, jnp.zeros((10, frac.shape[1]), F32)], axis=0)
-    first = jnp.floor(rows * 256.0) * (1.0 / 256.0)
-    top = lax.broadcasted_iota(I32, rows.shape, 0) < 3
-    return jnp.where(top, first, rows - first).astype(BF16)
+def pack_kernel(
+    feats_hbm, cot_hbm, frac_hbm, weight_hbm, halo, payload_hbm, feats, cot, frac, weight, payload, rows, sems
+):
+    pairs = ((frac_hbm, frac), (feats_hbm, feats), (weight_hbm, weight), (cot_hbm, cot))
+    copies = [
+        pltpu.make_async_copy(src, dst, sems.at[n]) for n, (src, dst) in enumerate(pairs)
+    ]
+    for copy in copies:
+        copy.start()
+    copies[0].wait()
+    rows[...] = jnp.zeros((16, ROWS), F32)
+    for d in range(3):
+        first = jnp.floor(frac[d] * 256.0) * (1.0 / 256.0)
+        rows[d : d + 1, :] = first
+        rows[d + 3 : d + 4, :] = frac[d] - first
+    where = rows[...]
+    halo[FRAC_AT:HALO] = where.astype(BF16)
+    copies[1].wait()
+    halo[0:CH] = feats[0]
+    for a in range(SLABS):
+        payload[a, 0:COT_AT] = feats[0, a % 4 * QUARTER : (a % 4 + 1) * QUARTER]
+    copies[2].wait()
+    hidden = dot(weight[...], feats[0], TN)
+    for a in range(SLABS):
+        payload[a, HID_AT:PAY] = jnp.concatenate(
+            [hidden[a * MINE : (a + 1) * MINE], where[0:8]], axis=0
+        ).astype(BF16)
+    copies[3].wait()
+    for a in range(SLABS):
+        payload[a, COT_AT:HID_AT] = cot[0, a // 4 * QUARTER : (a // 4 + 1) * QUARTER]
+    sent = pltpu.make_async_copy(payload, payload_hbm, sems.at[4])
+    sent.start()
+    sent.wait()
 
 
 def joined_frac(rows):
@@ -87,8 +116,8 @@
 def edge_kernel(
     place,
     own,
-    left,
-    right,
+    first_swap,
+    second_swap,
     neighbours,
     images,
     count,
@@ -114,8 +143,12 @@
     first, live_here, live_left, live_right = place[0], place[1], place[2], place[3]
     lane = lax.broadcasted_iota(I32, (CH, ROWS), 1)
     ext[:, 0:ROWS] = jnp.where(lane < live_here, own[0:CH].astype(F32), 0.0).astype(BF16)
-    near_right = jnp.where(lane < live_right, right[0:CH].astype(F32), 0.0)
-    near_left = jnp.where(lane < live_left, left[0:CH].astype(F32), 0.0)
+    even = place[6] == 0
+    swaps = first_swap[...].astype(F32), second_swap[...].astype(F32)
+    right = jnp.where(even, swaps[0], swaps[1])
+    left = jnp.where(even, swaps[1], swaps[0])
+    near_right = jnp.where(lane < live_right, right[0:CH], 0.0)
+    near_left = jnp.where(lane < live_left, left[0:CH], 0.0)
     ext[:, ROWS : 2 * ROWS] = jnp.where(lane < GHOST, near_right, near_left).astype(BF16)
     hidden = dot(in_weight[...], ext[...], TN).astype(BF16)
 
@@ -317,6 +350,19 @@
         folded[QUARTER : 2 * QUARTER, lanes] = sums[here] - sums[there]
 
 
+def by_lane_group(pieces):
+    group = lax.broadcasted_iota(I32, pieces[0].shape, 1) // 8
+    for bit in (1, 2, 4, 8):
+        low = group & bit == 0
+        pieces = [
+            jnp.where(low, piece, pltpu.roll(pieces[n + bit], 8 * bit, 1))
+            if n & bit == 0
+            else jnp.where(low, pltpu.roll(pieces[n - bit], CH - 8 * bit, 1), piece)
+            for n, piece in enumerate(pieces)
+        ]
+    return pieces
+
+
 def blocks(x, m):
     at = 2 * m * PLANE
     cc, cs = x[:, at : at + PLANE], x[:, at + PLANE : at + 2 * PLANE]
@@ -386,6 +432,7 @@
     for b in range(planes):
         value = found[b * MINE : (b + 1) * MINE] + found[(planes + b) * MINE : (planes + b + 1) * MINE]
         pair = jnp.where(around_plane == b, value, pair)
+    pair = by_lane_group([pair[:, d * ROWS : (d + 1) * ROWS] for d in range(SLABS)])
     grad = filtered(
         folded[0:QUARTER, :],
         folded[QUARTER : 2 * QUARTER, :],
@@ -397,7 +444,7 @@
     block = jnp.concatenate([block[8 * q : 8 * q + 8] for q in range(4)], axis=1)
     for d in range(STRUCTS):
         parts[d, 0:16, :] = jnp.concatenate(
-            [pair[:, d * KSHARE : (d + 1) * KSHARE], block], axis=0
+            [pair[d], block], axis=0
         ).astype(BF16)
         parts[d, 16:48, :] = early[d * SLOTS : (d + 1) * SLOTS, :].astype(BF16)
     coef = filtered(plus, minus, s)
@@ -485,42 +532,39 @@
     live = atom_count[0] - jnp.stack(
         [first, (first - ROWS) % ATOMS, (first + ROWS) % ATOMS]
     )
-    place = jnp.stack([slab * MINE, slab // 4 * QUARTER])
+    place = jnp.stack([slab * MINE, slab // 4 * QUARTER, slab % 2])
     place = jnp.concatenate([first[None], live, place]).astype(I32)
     struct = jax.ShapeDtypeStruct
 
-    feats = node_feats[0]
-    halo = jnp.concatenate([feats, coordinates(frac[0])], axis=0)
-    where = halo[FRAC_AT : FRAC_AT + 8]
-    ring = range(SLABS)
-    left = lax.ppermute(halo, "atom", [(i, (i + 1) % SLABS) for i in ring])
-    right = lax.ppermute(halo, "atom", [((i + 1) % SLABS, i) for i in ring])
-    hidden = dot(in_weight, feats, TN).astype(BF16)
-    square = (4, 4, QUARTER, ROWS)
-    payload = [
-        jnp.broadcast_to(feats.reshape(1, 4, QUARTER, ROWS), square),
-        jnp.broadcast_to(cotangent[0].reshape(4, 1, QUARTER, ROWS), square),
-        hidden.reshape(4, 4, MINE, ROWS),
-        jnp.broadcast_to(where, (4, 4, 8, ROWS)),
-    ]
-    payload = jnp.concatenate(payload, axis=2).reshape(SLABS, PAY, ROWS)
+    halo, payload = call(
+        pack_kernel,
+        [
+            (VMEM, struct((HALO, ROWS), BF16)),
+            (HBM, struct((SLABS, PAY, ROWS), BF16)),
+        ],
+        [
+            pltpu.VMEM((1, CH, ROWS), BF16),
+            pltpu.VMEM((1, CH, ROWS), BF16),
+            pltpu.VMEM((3, 1, ROWS), F32),
+            pltpu.VMEM((CH, CH), BF16),
+            pltpu.VMEM((SLABS, PAY, ROWS), BF16),
+            pltpu.VMEM((16, ROWS), F32),
+            pltpu.SemaphoreType.DMA((5,)),
+        ],
+        60,
+        10**6,
+        (HBM, node_feats),
+        (HBM, cotangent),
+        (HBM, frac.transpose(1, 0, 2)),
+        (HBM, in_weight),
+    )
+    evens = range(0, SLABS, 2)
+    pairs = [(n, n + 1) for n in evens], [(n + 1, (n + 2) % SLABS) for n in evens]
+    first_swap, second_swap = (
+        lax.ppermute(halo, "atom", [*pair, *((j, i) for i, j in pair)]) for pair in pairs
+    )
     gathered = exchange(payload, "atom")
 
-    (folded,) = call(
-        lattice_kernel,
-        [(VMEM, struct((2 * QUARTER, HALF), F32))],
-        [
-            pltpu.VMEM((CH, KVEC), F32),
-            pltpu.VMEM((2 * (TOP + 1) * QUARTER, KVEC), BF16),
-        ],
-        12,
-        10**8,
-        (SMEM, place),
-        (VMEM, miller),
-        (VMEM, filter_weight),
-    )
-    order = (3, SLABS, STRUCTS, KVEC // SLABS // STRUCTS)
-    miller = miller.reshape(order).transpose(0, 2, 1, 3).reshape(3, KVEC)
     early, local = call(
         edge_kernel,
         [(VMEM, struct((4 * CH, CH), F32)), (VMEM, struct((CH, ROWS), F32))],
@@ -542,8 +586,8 @@
         EDGE_COST,
         (SMEM, place),
         (VMEM, halo),
-        (VMEM, left),
-        (VMEM, right),
+        (VMEM, first_swap),
+        (VMEM, second_swap),
         (VMEM, neighbours),
         (VMEM, images),
         (VMEM, neighbour_count),
@@ -551,6 +595,20 @@
         (VMEM, radial_weight),
         (VMEM, out_weight),
         (VMEM, cotangent),
+    )
+    early, miller = lax.optimization_barrier((early, miller))
+    (folded,) = call(
+        lattice_kernel,
+        [(VMEM, struct((2 * QUARTER, HALF), F32))],
+        [
+            pltpu.VMEM((CH, KVEC), F32),
+            pltpu.VMEM((2 * (TOP + 1) * QUARTER, KVEC), BF16),
+        ],
+        12,
+        10**8,
+        (SMEM, place),
+        (VMEM, miller),
+        (VMEM, filter_weight),
     )
     parts, ewald = call(
         spectrum_kernel,

time: 78.8 us -> 76.4 us (0.970)
  Pallas kernels: 14.2 us -> 16.8 us
  local copies, waits for them, and re-layouts: 2.7 us -> 0.69 us
  other arithmetic: 1.87 us -> 0.13 us
  starting transfers between devices: 14.6 us -> 13.4 us
    pallas_call x5 -> x6, Pallas kernels: 14.2 us -> 16.8 us  [call(): pl.pallas_call(kernel, out_shape=[shape for _, shape in outs], in_specs=[...]
    concatenate x3 -> x0, other arithmetic: 1.65 us -> none  [the longest x1 0.81 us: shards(): halo = jnp.concatenate([feats, coordinates(frac[0])], axis=0)]
    all_to_all x1, starting transfers between devices: 5.52 us -> 4.31 us  [exchange(): return lax.all_to_all(x, axis, 0, 0)]
    unnamed x25 -> x22, local copies, waits for them, and re-layouts: 1.47 us -> 0.58 us
  transfers between devices with their start and end apart: 3 -> 3, of which waited for: 0 -> 0; matrix products, arithmetic and copies ran while one was open for 2% -> 0% of each run, Pallas kernels for 12% -> 12%
where the time goes in v4:
time: 76.4 us; the launch traced here: 75.9 us
  blocking collectives  43.3 us (57%)
  Pallas kernels  16.8 us (22%)
  starting transfers between devices  13.4 us (18%)
  between operations  1.49 us (2%)
    all_to_all x3, blocking collectives, exchange(): return lax.all_to_all(x, axis, 0, 0)  43.3 us
    pallas_call x6, Pallas kernels, call(): pl.pallas_call(kernel, out_shape=[shape for _, shape in outs], in_specs=[...  16.8 us
    ppermute x2, starting transfers between devices, shards(): lax.ppermute(halo, 'atom', [*pair, *((j, i) for i, j in pair)])  9.13 us
    all_to_all x1, starting transfers between devices, exchange(): return lax.all_to_all(x, axis, 0, 0)  4.31 us
  transfers between devices with their start and end apart: 3, of which 0 were waited for; matrix products, arithmetic and copies ran while one was open for 0% of the time, Pallas kernels for 12%

profile of v4, /device:TPU:1, one launch (start us, length us, event | category | flops | bytes accessed | tf_op | source)
XLA Modules:
  0.0 75.9 jit_solution(13041277382545384202)
XLA Ops:
  0.6 2.4 %shard_map.147 = (bf16[144,128]{1,0:T(8,128)(2,1)}, bf16[16,80,128]{2,1,0:T(8,128)(2,1)}) custom-call(bf16[1,128,128]{2,1,0:T(8,128)(2,1)} %feats.1, bf16[1,128,128]{2,1,0:T(8,128)(2,1)} %cot.1, f32[3,1,128]{2,1,0:T(1,128)} %bitcast.9, bf16[128,128]{1,0:T(8,128)(2,1)} %in_weight.1), custom_call_target="tpu_custom_call" | custom-call | flops 1000000 | bytes 65536 | tf_op jit(solution)/shard_map/pallas_call | solution.py:57
  3.0 9.1 %collective-permute-start.1 = (bf16[144,128]{1,0:T(8,128)(2,1)}, bf16[144,128]{1,0:T(8,128)(2,1)S(1)}, u32[]{:S(2)}, u32[]{:S(2)}) collective-permute-start(bf16[144,128]{1,0:T(8,128)(2,1)} %get-tuple-element.19.own), channel_id=1, source_target_pairs={{1,2},{3,4},{5,6},{7,8},{9,10},{11,12},{13,14},{15,0},{2,1},{4,3},... | collective-permute-start | bytes 110600 | tf_op jit(solution)/shard_map/ppermute | solution.py:564
  12.1 0.0 collective-permute-start
  12.2 4.3 %all-to-all-start = ((bf16[16,80,128]{2,1,0:T(8,128)(2,1)}), bf16[16,80,128]{2,1,0:T(8,128)(2,1)S(1)}, u32[]{:S(2)}, u32[]{:S(2)}) async-start(bf16[16,80,128]{2,1,0:T(8,128)(2,1)} %get-tuple-element.18), calls=%async_computation | async-start | bytes 655360 | tf_op jit(solution)/shard_map/all_to_all | solution.py:513
  16.5 0.0 copy-start.9
  16.5 0.0 copy-start.6
  17.2 0.0 copy-start.2
  17.2 0.0 copy-start.3
  17.2 0.1 add_subtract_fusion
  17.3 0.1 concatenate.6.place
  17.4 0.0 collective-permute-done.1.second_swap
  17.4 0.0 collective-permute-done.first_swap
  17.4 0.5 copy-done.2
  17.9 0.0 copy-done.3
  18.0 7.9 %shard_map.148 = (f32[512,128]{1,0:T(8,128)S(1)}, f32[128,128]{1,0:T(8,128)S(1)}) custom-call(s32[7]{0:T(128)S(1)} %concatenate.6.place, bf16[144,128]{1,0:T(8,128)(2,1)S(1)} %copy-done.6, bf16[144,128]{1,0:T(8,128)(2,1)S(1)} %collective-permute-done.first_swap, bf16[144,128]{1,0:T(8,128)(2,1)S(1)} %collective-permute-done.1.second_swap, ...), custom_call_target="tpu_custom_call" | custom-call | flops 10000000000 | bytes 65536 | tf_op jit(solution)/shard_map/pallas_call | solution.py:57
  25.8 1.5 %shard_map.149.folded = f32[64,896]{1,0:T(8,128)S(1)} custom-call(s32[7]{0:T(128)S(1)} %concatenate.6.place, s32[3,2048]{1,0:T(4,128)S(1)} %copy-done.4, f32[2048,128]{1,0:T(8,128)S(1)} %copy-done), custom_call_target="tpu_custom_call" | custom-call | flops 100000000 | bytes 65536 | tf_op jit(solution)/shard_map/pallas_call | solution.py:57
  27.3 0.0 all-to-all-done.gathered
  27.4 3.1 %shard_map.150 = (bf16[16,48,128]{2,1,0:T(8,128)(2,1)S(1)}, bf16[16,8,128]{2,1,0:T(8,128)(2,1)S(1)}) custom-call(s32[7]{0:T(128)S(1)} %concatenate.6.place, bf16[16,80,128]{2,1,0:T(8,128)(2,1)S(1)} %all-to-all-done.gathered, f32[64,896]{1,0:T(8,128)S(1)} %shard_map.149.folded, s32[3,2048]{1,0:T(4,128)S(1)} %copy-done.4, f32[512,128]{1,0:T(8,128)S(1)} %get-tuple-element.22.early), custom_call_target="tpu_custom_call" | custom-call | flops 10000000000 | bytes 65536 | tf_op jit(solution)/shard_map/pallas_call | solution.py:57
  30.5 13.9 %all_to_all.20 = bf16[16,48,128]{2,1,0:T(8,128)(2,1)S(1)} all-to-all(bf16[16,48,128]{2,1,0:T(8,128)(2,1)S(1)} %get-tuple-element.23), channel_id=1, replica_groups=mesh['dp'=16,'atom'=16] {'dp'}, dimensions={0} | all-to-all | bytes 393216 | tf_op jit(solution)/shard_map/all_to_all | solution.py:513
  44.4 0.0 copy-start.1
  44.5 17.7 %all_to_all.21.sums = bf16[16,56,128]{2,1,0:T(8,128)(2,1)S(1)} all-to-all(bf16[16,56,128]{2,1,0:T(8,128)(2,1)S(1)} %pad_maximum_fusion), channel_id=1, replica_groups=mesh['dp'=16,'atom'=16] {'atom'}, dimensions={0} | all-to-all | bytes 458752 | tf_op jit(solution)/shard_map/all_to_all | solution.py:513
  62.1 1.3 %shard_map.151 = (bf16[16,48,128]{2,1,0:T(8,128)(2,1)S(1)}, f32[128,128]{1,0:T(8,128)S(1)}, bf16[1,128,128]{2,1,0:T(8,128)(2,1)}) custom-call(s32[7]{0:T(128)S(1)} %concatenate.6.place, bf16[16,56,128]{2,1,0:T(8,128)(2,1)S(1)} %all_to_all.21.sums, bf16[1,128,128]{2,1,0:T(8,128)(2,1)S(1)} %copy-done.1, f32[128,128]{1,0:T(8,128)S(1)} %get-tuple-element.25.local), custom_call_target="tpu_custom_call" | custom-call | flops 1000000 | bytes 65536 | tf_op jit(solution)/shard_map/pallas_call | solution.py:57
  63.4 11.7 %all_to_all.22.sums = bf16[16,48,128]{2,1,0:T(8,128)(2,1)S(1)} all-to-all(bf16[16,48,128]{2,1,0:T(8,128)(2,1)S(1)} %get-tuple-element.27), channel_id=1, replica_groups=mesh['dp'=16,'atom'=16] {'dp'}, dimensions={0} | all-to-all | bytes 393216 | tf_op jit(solution)/shard_map/all_to_all | solution.py:513
  75.1 0.7 shard_map.152
  (18 shorter events, 0.1 us)
Async XLA Ops:
  3.0 14.4 %collective-permute-start.1 = (bf16[144,128]{1,0:T(8,128)(2,1)}, bf16[144,128]{1,0:T(8,128)(2,1)S(1)}, u32[]{:S(2)}, u32[]{:S(2)}) collective-permute-start(bf16[144,128]{1,0:T(8,128)(2,1)} %get-tuple-element.19.own), channel_id=1, source_target_pairs={{1,2},{3,4},{5,6},{7,8},{9,10},{11,12},{13,14},{15,0},{2,1},{4,3},... | collective-permute-start | bytes 110600 | tf_op jit(solution)/shard_map/ppermute | solution.py:564
  12.1 5.2 %collective-permute-start = (bf16[144,128]{1,0:T(8,128)(2,1)}, bf16[144,128]{1,0:T(8,128)(2,1)S(1)}, u32[]{:S(2)}, u32[]{:S(2)}) collective-permute-start(bf16[144,128]{1,0:T(8,128)(2,1)} %get-tuple-element.19.own), channel_id=1, source_target_pairs={{0,1},{2,3},{4,5},{6,7},{8,9},{10,11},{12,13},{14,15},{1,0},{3,2},... | collective-permute-start | bytes 110600 | tf_op jit(solution)/shard_map/ppermute | solution.py:564
  12.1 5.2 %copy-start.5 = (bf16[384,128]{1,0:T(8,128)(2,1)S(1)}, bf16[384,128]{1,0:T(8,128)(2,1)}, u32[]{:S(2)}) copy-start(bf16[384,128]{1,0:T(8,128)(2,1)} %out_weight.1) | copy-start | bytes 294916
  12.1 5.3 %copy-start.7 = (s32[1,32,128]{2,1,0:T(8,128)S(1)}, s32[1,32,128]{2,1,0:T(8,128)}, u32[]{:S(2)}) copy-start(s32[1,32,128]{2,1,0:T(8,128)} %neighbours.1) | copy-start | bytes 49156
  12.1 5.3 %copy-start.8 = (s32[1,32,128]{2,1,0:T(8,128)S(1)}, s32[1,32,128]{2,1,0:T(8,128)}, u32[]{:S(2)}) copy-start(s32[1,32,128]{2,1,0:T(8,128)} %images.1) | copy-start | bytes 49156
  12.2 15.2 %all-to-all-start = ((bf16[16,80,128]{2,1,0:T(8,128)(2,1)}), bf16[16,80,128]{2,1,0:T(8,128)(2,1)S(1)}, u32[]{:S(2)}, u32[]{:S(2)}) async-start(bf16[16,80,128]{2,1,0:T(8,128)(2,1)} %get-tuple-element.18), calls=%async_computation | async-start | bytes 655360 | tf_op jit(solution)/shard_map/all_to_all | solution.py:513
  16.5 0.9 %copy-start.9 = (f32[3,8,128]{2,1,0:T(8,128)S(1)}, f32[3,8,128]{2,1,0:T(8,128)}, u32[]{:S(2)}) copy-start(f32[3,8,128]{2,1,0:T(8,128)} %radial_weight.1) | copy-start | bytes 36868
  16.5 0.9 %copy-start.6 = (bf16[144,128]{1,0:T(8,128)(2,1)S(1)}, bf16[144,128]{1,0:T(8,128)(2,1)}, u32[]{:S(2)}) copy-start(bf16[144,128]{1,0:T(8,128)(2,1)} %get-tuple-element.19.own) | copy-start | bytes 110596
  17.2 0.8 %copy-start.2 = (bf16[1,128,128]{2,1,0:T(8,128)(2,1)S(1)}, bf16[1,128,128]{2,1,0:T(8,128)(2,1)}, u32[]{:S(2)}) copy-start(bf16[1,128,128]{2,1,0:T(8,128)(2,1)} %cot.1) | copy-start | bytes 98308
  17.2 0.8 %copy-start.3 = (bf16[128,128]{1,0:T(8,128)(2,1)S(1)}, bf16[128,128]{1,0:T(8,128)(2,1)}, u32[]{:S(2)}) copy-start(bf16[128,128]{1,0:T(8,128)(2,1)} %in_weight.1) | copy-start | bytes 98308
  17.3 0.7 copy-start.10
  17.4 8.5 %copy-start = (f32[2048,128]{1,0:T(8,128)S(1)}, f32[2048,128]{1,0:T(8,128)}, u32[]{:S(2)}) copy-start(f32[2048,128]{1,0:T(8,128)} %filter_weight.1) | copy-start | bytes 3145732
  17.4 8.5 %copy-start.4 = (s32[3,2048]{1,0:T(4,128)S(1)}, s32[3,2048]{1,0:T(4,128)}, u32[]{:S(2)}) copy-start(s32[3,2048]{1,0:T(4,128)} %miller.1) | copy-start | bytes 73732
  44.4 17.7 %copy-start.1 = (bf16[1,128,128]{2,1,0:T(8,128)(2,1)S(1)}, bf16[1,128,128]{2,1,0:T(8,128)(2,1)}, u32[]{:S(2)}) copy-start(bf16[1,128,128]{2,1,0:T(8,128)(2,1)} %feats.1) | copy-start | bytes 98308

commit v5 on v4

--- a/solution.py
+++ b/solution.py
@@ -36,7 +36,6 @@
 COT_AT, HID_AT, PAY = QUARTER, 2 * QUARTER, 2 * QUARTER + 16
 
 VMEM = pl.BlockSpec(memory_space=pltpu.VMEM)
-SMEM = pl.BlockSpec(memory_space=pltpu.SMEM)
 HBM = pl.BlockSpec(memory_space=pltpu.HBM)
 
 NN = (((1,), (0,)), ((), ()))
@@ -68,9 +67,15 @@
 
 
 def pack_kernel(
-    feats_hbm, cot_hbm, frac_hbm, weight_hbm, halo, payload_hbm, feats, cot, frac, weight, payload, rows, sems
+    feats_hbm, cot_hbm, frac_hbm, weight_hbm, count_hbm, halo, payload_hbm, feats, cot, frac, weight, count, payload, rows, sems
 ):
-    pairs = ((frac_hbm, frac), (feats_hbm, feats), (weight_hbm, weight), (cot_hbm, cot))
+    pairs = (
+        (frac_hbm, frac),
+        (feats_hbm, feats),
+        (weight_hbm, weight),
+        (cot_hbm, cot),
+        (count_hbm, count),
+    )
     copies = [
         pltpu.make_async_copy(src, dst, sems.at[n]) for n, (src, dst) in enumerate(pairs)
     ]
@@ -82,6 +87,9 @@
         first = jnp.floor(frac[d] * 256.0) * (1.0 / 256.0)
         rows[d : d + 1, :] = first
         rows[d + 3 : d + 4, :] = frac[d] - first
+    copies[4].wait()
+    rows[6:7, :] = jnp.broadcast_to((count[...] >> 4).astype(F32), (1, ROWS))
+    rows[7:8, :] = jnp.broadcast_to((count[...] & 15).astype(F32), (1, ROWS))
     where = rows[...]
     halo[FRAC_AT:HALO] = where.astype(BF16)
     copies[1].wait()
@@ -97,9 +105,14 @@
     copies[3].wait()
     for a in range(SLABS):
         payload[a, COT_AT:HID_AT] = cot[0, a // 4 * QUARTER : (a // 4 + 1) * QUARTER]
-    sent = pltpu.make_async_copy(payload, payload_hbm, sems.at[4])
+    sent = pltpu.make_async_copy(payload, payload_hbm, sems.at[5])
     sent.start()
     sent.wait()
+
+
+def joined_count(rows):
+    wide = rows.astype(F32)
+    return 16.0 * wide[6:7] + wide[7:8]
 
 
 def joined_frac(rows):
@@ -114,7 +127,6 @@
 
 
 def edge_kernel(
-    place,
     own,
     first_swap,
     second_swap,
@@ -140,10 +152,15 @@
     pulled,
     inv,
 ):
-    first, live_here, live_left, live_right = place[0], place[1], place[2], place[3]
+    slab = lax.axis_index("atom")
+    first = slab * ROWS
+    atoms = joined_count(own[FRAC_AT:HALO]).astype(I32)
+    live_here = atoms - first
+    live_left = atoms - ((first - ROWS) & (ATOMS - 1))
+    live_right = atoms - ((first + ROWS) & (ATOMS - 1))
     lane = lax.broadcasted_iota(I32, (CH, ROWS), 1)
     ext[:, 0:ROWS] = jnp.where(lane < live_here, own[0:CH].astype(F32), 0.0).astype(BF16)
-    even = place[6] == 0
+    even = (slab & 1) == 0
     swaps = first_swap[...].astype(F32), second_swap[...].astype(F32)
     right = jnp.where(even, swaps[0], swaps[1])
     left = jnp.where(even, swaps[1], swaps[0])
@@ -333,10 +350,11 @@
     ]
 
 
-def lattice_kernel(place, miller, filter_weight, folded, turned, wide):
+def lattice_kernel(miller, filter_weight, folded, turned, wide):
     plane, point = half_point(miller[...])
     turned[...] = filter_weight[...].T * (1.0 / math.sqrt(KVEC * ATOMS))
-    mine = turned[pl.ds(pl.multiple_of(place[5], QUARTER), QUARTER), :]
+    quarter = lax.axis_index("atom") >> 2
+    mine = turned[pl.ds(pl.multiple_of(quarter * QUARTER, QUARTER), QUARTER), :]
     for b in range(2 * (TOP + 1)):
         here = slice(b * QUARTER, (b + 1) * QUARTER)
         wide[here, :] = jnp.where(plane == b, mine, 0.0).astype(BF16)
@@ -388,7 +406,7 @@
 
 
 def spectrum_kernel(
-    place, gathered, folded, miller, early, parts, ewald, factor, frac, values, plane, wide
+    gathered, folded, miller, early, parts, ewald, factor, frac, values, plane, wide
 ):
     for p in range(SLABS):
         here = slice(p * ROWS, (p + 1) * ROWS)
@@ -396,7 +414,9 @@
         tail = gathered[p, HID_AT:PAY].astype(F32)
         frac[0:3, here] = tail[MINE : MINE + 3] + tail[MINE + 3 : MINE + 6]
     along = waves([frac[d : d + 1, :] for d in range(3)], plane)
-    live = (lax.broadcasted_iota(I32, (1, ATOMS), 1) < place[0] + place[1]).astype(F32)
+    atoms = joined_count(gathered[0, HID_AT:PAY].astype(F32)[MINE:16]).astype(I32)
+    live = lax.broadcasted_iota(I32, (1, ATOMS), 1) < atoms[:, 0:1]
+    live = jnp.where(live, 1.0, 0.0)
     around = plane[...].astype(BF16)
     for low, high in ((0, TOP + 1), (TOP + 1, WAVES)):
         for f in range(low, high):
@@ -408,7 +428,7 @@
             here = slice(f * 2 * PLANE, (f + 1) * 2 * PLANE)
             factor[:, here] = both[(f - low) * PAY : (f - low + 1) * PAY]
 
-    at = pl.multiple_of(place[4] - place[5], MINE)
+    at = pl.multiple_of((lax.axis_index("atom") & 3) * MINE, MINE)
     s = factor[HID_AT : HID_AT + MINE, :]
     g = factor[pl.ds(pl.multiple_of(COT_AT + at, MINE), MINE), :]
     plus = folded[pl.ds(at, MINE), :]
@@ -468,10 +488,10 @@
 ]
 
 
-def middle_kernel(place, sums, feats, local, last, grad_in, updated):
+def middle_kernel(sums, own, local, last, grad_in, field):
     row = lax.broadcasted_iota(I32, (8, KSHARE), 0)
     lane = lax.broadcasted_iota(I32, (8, KSHARE), 1)
-    pick = jnp.where(lane == row + place[4], 1.0, 0.0).astype(BF16)
+    pick = jnp.where(lane == row + MINE * lax.axis_index("atom"), 1.0, 0.0).astype(BF16)
     blocks = [sums[p].astype(F32) for p in range(SLABS)]
     pairs = jnp.concatenate([block[0:8] for block in blocks], axis=0)
     picked = dot(pick, pairs.astype(BF16), NT)
@@ -492,13 +512,15 @@
         grads.append(eight)
     grad_in[...] = jnp.concatenate(grads, axis=0).T
     ewald = jnp.concatenate([block[48:56] for block in blocks], axis=0)
-    here = lax.broadcasted_iota(I32, (CH, ROWS), 1) < place[1]
-    updated[0] = jnp.where(
-        here, feats[0].astype(F32) + local[...] + ewald, 0.0
-    ).astype(BF16)
-
-
-def finish_kernel(sums, ewald_in, grad_filter, grad_in, grad_out):
+    live = joined_count(own[FRAC_AT:HALO]).astype(I32) - lax.axis_index("atom") * ROWS
+    live = lax.broadcasted_iota(I32, (CH, ROWS), 1) < live
+    field[...] = jnp.where(live, own[0:CH].astype(F32) + local[...] + ewald, 0.0)
+
+
+def finish_kernel(
+    sums, ewald_in, field, updated, grad_filter, grad_in, grad_out
+):
+    updated[0] = field[...].astype(BF16)
     for d in range(STRUCTS):
         late = sums[d, 32:48].astype(F32)
         grad_filter[8 * d : 8 * d + 8, :] = late[0:8]
@@ -527,13 +549,6 @@
     filter_weight,
     cotangent,
 ):
-    slab = lax.axis_index("atom")
-    first = slab * ROWS
-    live = atom_count[0] - jnp.stack(
-        [first, (first - ROWS) % ATOMS, (first + ROWS) % ATOMS]
-    )
-    place = jnp.stack([slab * MINE, slab // 4 * QUARTER, slab % 2])
-    place = jnp.concatenate([first[None], live, place]).astype(I32)
     struct = jax.ShapeDtypeStruct
 
     halo, payload = call(
@@ -547,9 +562,10 @@
             pltpu.VMEM((1, CH, ROWS), BF16),
             pltpu.VMEM((3, 1, ROWS), F32),
             pltpu.VMEM((CH, CH), BF16),
+            pltpu.VMEM((1, 1), I32),
             pltpu.VMEM((SLABS, PAY, ROWS), BF16),
             pltpu.VMEM((16, ROWS), F32),
-            pltpu.SemaphoreType.DMA((5,)),
+            pltpu.SemaphoreType.DMA((6,)),
         ],
         60,
         10**6,
@@ -557,6 +573,7 @@
         (HBM, cotangent),
         (HBM, frac.transpose(1, 0, 2)),
         (HBM, in_weight),
+        (HBM, atom_count.reshape(1, 1)),
     )
     evens = range(0, SLABS, 2)
     pairs = [(n, n + 1) for n in evens], [(n + 1, (n + 2) % SLABS) for n in evens]
@@ -584,7 +601,6 @@
         ],
         20,
         EDGE_COST,
-        (SMEM, place),
         (VMEM, halo),
         (VMEM, first_swap),
         (VMEM, second_swap),
@@ -606,7 +622,6 @@
         ],
         12,
         10**8,
-        (SMEM, place),
         (VMEM, miller),
         (VMEM, filter_weight),
     )
@@ -619,7 +634,6 @@
         SPECTRUM_SCRATCH,
         20,
         10**10,
-        (SMEM, place),
         (VMEM, gathered),
         (VMEM, folded),
         (VMEM, miller),
@@ -627,24 +641,24 @@
     )
     sums = exchange(parts, "dp").astype(F32).sum(axis=0).astype(BF16)
     sums = jnp.broadcast_to(sums[None], (SLABS, 48, CH))
-    last, ewald_in, updated = call(
+    last, ewald_in, field = call(
         middle_kernel,
         [
             (VMEM, struct((STRUCTS, 48, CH), BF16)),
             (VMEM, struct((CH, CH), F32)),
-            (VMEM, struct((1, CH, ROWS), BF16)),
+            (VMEM, struct((CH, ROWS), F32)),
         ],
         [],
         16,
         10**6,
-        (SMEM, place),
         (VMEM, exchange(jnp.concatenate([sums, ewald], axis=1), "atom")),
-        (VMEM, node_feats),
+        (VMEM, halo),
         (VMEM, local),
     )
-    grads = call(
+    return tuple(call(
         finish_kernel,
         [
+            (VMEM, struct((1, CH, ROWS), BF16)),
             (VMEM, struct((KSHARE, CH), F32)),
             (VMEM, struct((CH, CH), F32)),
             (VMEM, struct((3 * CH, CH), F32)),
@@ -654,8 +668,8 @@
         10**6,
         (VMEM, exchange(last, "dp")),
         (VMEM, ewald_in),
-    )
-    return (updated, *grads)
+        (VMEM, field),
+    ))
 
 
 def solution(mesh):

time: 76.4 us -> 72.5 us (0.949)
  Pallas kernels: 16.8 us -> 13.8 us
  blocking collectives: 43.3 us -> 40.8 us
  waiting for transfers between devices: 0.01 us -> 2.47 us
    pallas_call x6, Pallas kernels: 16.8 us -> 13.8 us  [call(): pl.pallas_call(kernel, out_shape=[shape for _, shape in outs], in_specs=[...]
    all_to_all x1, waiting for transfers between devices: 0.01 us -> 2.47 us  [exchange(): return lax.all_to_all(x, axis, 0, 0)]
    all_to_all x3, blocking collectives: 43.3 us -> 40.8 us  [exchange(): return lax.all_to_all(x, axis, 0, 0)]
  transfers between devices with their start and end apart: 3 -> 3, of which waited for: 0 -> 1; matrix products, arithmetic and copies ran while one was open for 0% -> 0% of each run, Pallas kernels for 12% -> 11%
where the time goes in v5:
time: 72.5 us; the launch traced here: 72.2 us
  blocking collectives  40.8 us (56%)
  Pallas kernels  13.8 us (19%)
  starting transfers between devices  13.4 us (18%)
  waiting for transfers between devices  2.47 us (3%)
  between operations  1.49 us (2%)
    all_to_all x3, blocking collectives, exchange(): return lax.all_to_all(x, axis, 0, 0)  40.8 us
    pallas_call x6, Pallas kernels, call(): pl.pallas_call(kernel, out_shape=[shape for _, shape in outs], in_specs=[...  13.8 us
    ppermute x2, starting transfers between devices, shards(): lax.ppermute(halo, 'atom', [*pair, *((j, i) for i, j in pair)])  9.13 us
    all_to_all x1, starting transfers between devices, exchange(): return lax.all_to_all(x, axis, 0, 0)  4.32 us
    all_to_all x1, waiting for transfers between devices, exchange(): return lax.all_to_all(x, axis, 0, 0)  2.47 us
  transfers between devices with their start and end apart: 3, of which 1 were waited for; matrix products, arithmetic and copies ran while one was open for 0% of the time, Pallas kernels for 11%

profile of v5, /device:TPU:1, one launch (start us, length us, event | category | flops | bytes accessed | tf_op | source)
XLA Modules:
  0.0 72.2 jit_solution(724279510998501338)
XLA Ops:
  1.3 2.4 %shard_map.147 = (bf16[144,128]{1,0:T(8,128)(2,1)}, bf16[16,80,128]{2,1,0:T(8,128)(2,1)}) custom-call(bf16[1,128,128]{2,1,0:T(8,128)(2,1)} %feats_hbm.1, bf16[1,128,128]{2,1,0:T(8,128)(2,1)} %cot.1, f32[3,1,128]{2,1,0:T(1,128)} %bitcast.3, bf16[128,128]{1,0:T(8,128)(2,1)} %in_weight.1, s32[1,1]{1,0:T(1,128)} %bitcast.2.count_hbm), custom_call_target="tpu_custom_call" | custom-call | flops 1000000 | bytes 65536 | tf_op jit(solution)/shard_map/pallas_call | solution.py:56
  3.7 9.1 %collective-permute-start.1 = (bf16[144,128]{1,0:T(8,128)(2,1)}, bf16[144,128]{1,0:T(8,128)(2,1)S(1)}, u32[]{:S(2)}, u32[]{:S(2)}) collective-permute-start(bf16[144,128]{1,0:T(8,128)(2,1)} %get-tuple-element.16.own), channel_id=1, source_target_pairs={{1,2},{3,4},{5,6},{7,8},{9,10},{11,12},{13,14},{15,0},{2,1},{4,3},... | collective-permute-start | bytes 110600 | tf_op jit(solution)/shard_map/ppermute | solution.py:581
  12.8 0.0 collective-permute-start
  12.8 0.0 copy-start.5
  12.8 0.0 copy-start.6
  12.8 0.0 copy-start.7
  12.8 0.0 copy-start.8
  12.9 0.0 copy-start.9
  12.9 4.3 %all-to-all-start = ((bf16[16,80,128]{2,1,0:T(8,128)(2,1)}), bf16[16,80,128]{2,1,0:T(8,128)(2,1)S(1)}, u32[]{:S(2)}, u32[]{:S(2)}) async-start(bf16[16,80,128]{2,1,0:T(8,128)(2,1)} %get-tuple-element.15), calls=%async_computation | async-start | bytes 655360 | tf_op jit(solution)/shard_map/all_to_all | solution.py:535
  17.2 0.0 copy-start
  17.2 0.0 copy-start.4
  17.2 0.0 collective-permute-done.1.second_swap
  17.2 0.0 collective-permute-done.first_swap
  17.2 0.0 copy-done.1
  17.3 0.0 copy-done.2
  17.3 7.1 %shard_map.148 = (f32[512,128]{1,0:T(8,128)S(1)}, f32[128,128]{1,0:T(8,128)S(1)}) custom-call(bf16[144,128]{1,0:T(8,128)(2,1)S(1)} %copy-done.1, bf16[144,128]{1,0:T(8,128)(2,1)S(1)} %collective-permute-done.first_swap, bf16[144,128]{1,0:T(8,128)(2,1)S(1)} %collective-permute-done.1.second_swap, s32[1,32,128]{2,1,0:T(8,128)S(1)} %copy-done.6, ...), custom_call_target="tpu_custom_call" | custom-call | flops 10000000000 | bytes 65536 | tf_op jit(solution)/shard_map/pallas_call | solution.py:56
  24.4 0.8 %shard_map.149.folded = f32[64,896]{1,0:T(8,128)S(1)} custom-call(s32[3,2048]{1,0:T(4,128)S(1)} %copy-done.4, f32[2048,128]{1,0:T(8,128)S(1)} %copy-done), custom_call_target="tpu_custom_call" | custom-call | flops 100000000 | bytes 65536 | tf_op jit(solution)/shard_map/pallas_call | solution.py:56
  25.2 2.5 %all-to-all-done.gathered = bf16[16,80,128]{2,1,0:T(8,128)(2,1)S(1)} async-done(((bf16[16,80,128]{2,1,0:T(8,128)(2,1)}), bf16[16,80,128]{2,1,0:T(8,128)(2,1)S(1)}, u32[]{:S(2)}, u32[]{:S(2)}) %all-to-all-start) | async-done | bytes 327712 | tf_op jit(solution)/shard_map/all_to_all | solution.py:535
  27.7 2.6 %shard_map.150 = (bf16[16,48,128]{2,1,0:T(8,128)(2,1)S(1)}, bf16[16,8,128]{2,1,0:T(8,128)(2,1)S(1)}) custom-call(bf16[16,80,128]{2,1,0:T(8,128)(2,1)S(1)} %all-to-all-done.gathered, f32[64,896]{1,0:T(8,128)S(1)} %shard_map.149.folded, s32[3,2048]{1,0:T(4,128)S(1)} %copy-done.4, f32[512,128]{1,0:T(8,128)S(1)} %get-tuple-element.19.early), custom_call_target="tpu_custom_call" | custom-call | flops 10000000000 | bytes 65536 | tf_op jit(solution)/shard_map/pallas_call | solution.py:56
  30.3 14.3 %all_to_all.20 = bf16[16,48,128]{2,1,0:T(8,128)(2,1)S(1)} all-to-all(bf16[16,48,128]{2,1,0:T(8,128)(2,1)S(1)} %get-tuple-element.20), channel_id=1, replica_groups=mesh['dp'=16,'atom'=16] {'dp'}, dimensions={0} | all-to-all | bytes 393216 | tf_op jit(solution)/shard_map/all_to_all | solution.py:535
  44.7 14.8 %all_to_all.21.sums = bf16[16,56,128]{2,1,0:T(8,128)(2,1)S(1)} all-to-all(bf16[16,56,128]{2,1,0:T(8,128)(2,1)S(1)} %pad_maximum_fusion), channel_id=1, replica_groups=mesh['dp'=16,'atom'=16] {'atom'}, dimensions={0} | all-to-all | bytes 458752 | tf_op jit(solution)/shard_map/all_to_all | solution.py:535
  59.5 0.2 shard_map.151
  59.7 11.7 %all_to_all.22.sums = bf16[16,48,128]{2,1,0:T(8,128)(2,1)S(1)} all-to-all(bf16[16,48,128]{2,1,0:T(8,128)(2,1)S(1)} %get-tuple-element.23), channel_id=1, replica_groups=mesh['dp'=16,'atom'=16] {'dp'}, dimensions={0} | all-to-all | bytes 393216 | tf_op jit(solution)/shard_map/all_to_all | solution.py:535
  71.4 0.7 %shard_map.152 = (bf16[1,128,128]{2,1,0:T(8,128)(2,1)}, f32[128,128]{1,0:T(8,128)}, f32[128,128]{1,0:T(8,128)}, f32[384,128]{1,0:T(8,128)}) custom-call(bf16[16,48,128]{2,1,0:T(8,128)(2,1)S(1)} %all_to_all.22.sums, f32[128,128]{1,0:T(8,128)S(1)} %get-tuple-element.24.ewald_in, f32[128,128]{1,0:T(8,128)S(1)} %get-tuple-element.25.field), custom_call_target="tpu_custom_call" | custom-call | flops 1000000 | bytes 65536 | tf_op jit(solution)/shard_map/pallas_call | solution.py:56
  (14 shorter events, 0.1 us)
Async XLA Ops:
  3.7 13.6 %collective-permute-start.1 = (bf16[144,128]{1,0:T(8,128)(2,1)}, bf16[144,128]{1,0:T(8,128)(2,1)S(1)}, u32[]{:S(2)}, u32[]{:S(2)}) collective-permute-start(bf16[144,128]{1,0:T(8,128)(2,1)} %get-tuple-element.16.own), channel_id=1, source_target_pairs={{1,2},{3,4},{5,6},{7,8},{9,10},{11,12},{13,14},{15,0},{2,1},{4,3},... | collective-permute-start | bytes 110600 | tf_op jit(solution)/shard_map/ppermute | solution.py:581
  12.8 4.4 %collective-permute-start = (bf16[144,128]{1,0:T(8,128)(2,1)}, bf16[144,128]{1,0:T(8,128)(2,1)S(1)}, u32[]{:S(2)}, u32[]{:S(2)}) collective-permute-start(bf16[144,128]{1,0:T(8,128)(2,1)} %get-tuple-element.16.own), channel_id=1, source_target_pairs={{0,1},{2,3},{4,5},{6,7},{8,9},{10,11},{12,13},{14,15},{1,0},{3,2},... | collective-permute-start | bytes 110600 | tf_op jit(solution)/shard_map/ppermute | solution.py:581
  12.8 4.4 %copy-start.1 = (bf16[144,128]{1,0:T(8,128)(2,1)S(1)}, bf16[144,128]{1,0:T(8,128)(2,1)}, u32[]{:S(2)}) copy-start(bf16[144,128]{1,0:T(8,128)(2,1)} %get-tuple-element.16.own) | copy-start | bytes 110596
  12.8 4.5 %copy-start.2 = (bf16[1,128,128]{2,1,0:T(8,128)(2,1)S(1)}, bf16[1,128,128]{2,1,0:T(8,128)(2,1)}, u32[]{:S(2)}) copy-start(bf16[1,128,128]{2,1,0:T(8,128)(2,1)} %cot.1) | copy-start | bytes 98308
  12.8 4.5 %copy-start.3 = (bf16[128,128]{1,0:T(8,128)(2,1)S(1)}, bf16[128,128]{1,0:T(8,128)(2,1)}, u32[]{:S(2)}) copy-start(bf16[128,128]{1,0:T(8,128)(2,1)} %in_weight.1) | copy-start | bytes 98308
  12.8 4.5 %copy-start.5 = (bf16[384,128]{1,0:T(8,128)(2,1)S(1)}, bf16[384,128]{1,0:T(8,128)(2,1)}, u32[]{:S(2)}) copy-start(bf16[384,128]{1,0:T(8,128)(2,1)} %out_weight.1) | copy-start | bytes 294916
  12.8 4.5 %copy-start.6 = (s32[1,32,128]{2,1,0:T(8,128)S(1)}, s32[1,32,128]{2,1,0:T(8,128)}, u32[]{:S(2)}) copy-start(s32[1,32,128]{2,1,0:T(8,128)} %neighbours.1) | copy-start | bytes 49156
  12.8 4.5 %copy-start.7 = (s32[1,32,128]{2,1,0:T(8,128)S(1)}, s32[1,32,128]{2,1,0:T(8,128)}, u32[]{:S(2)}) copy-start(s32[1,32,128]{2,1,0:T(8,128)} %images.1) | copy-start | bytes 49156
  12.8 4.5 %copy-start.8 = (f32[3,8,128]{2,1,0:T(8,128)S(1)}, f32[3,8,128]{2,1,0:T(8,128)}, u32[]{:S(2)}) copy-start(f32[3,8,128]{2,1,0:T(8,128)} %radial_weight.1) | copy-start | bytes 36868
  12.9 4.5 %copy-start.9 = (s32[1,128]{1,0:T(1,128)S(1)}, s32[1,128]{1,0:T(1,128)}, u32[]{:S(2)}) copy-start(s32[1,128]{1,0:T(1,128)} %count.1) | copy-start | bytes 1540
  12.9 14.8 %all-to-all-start = ((bf16[16,80,128]{2,1,0:T(8,128)(2,1)}), bf16[16,80,128]{2,1,0:T(8,128)(2,1)S(1)}, u32[]{:S(2)}, u32[]{:S(2)}) async-start(bf16[16,80,128]{2,1,0:T(8,128)(2,1)} %get-tuple-element.15), calls=%async_computation | async-start | bytes 655360 | tf_op jit(solution)/shard_map/all_to_all | solution.py:535
  17.2 7.2 %copy-start = (f32[2048,128]{1,0:T(8,128)S(1)}, f32[2048,128]{1,0:T(8,128)}, u32[]{:S(2)}) copy-start(f32[2048,128]{1,0:T(8,128)} %filter_weight.1) | copy-start | bytes 3145732
  17.2 7.2 %copy-start.4 = (s32[3,2048]{1,0:T(4,128)S(1)}, s32[3,2048]{1,0:T(4,128)}, u32[]{:S(2)}) copy-start(s32[3,2048]{1,0:T(4,128)} %miller.1) | copy-start | bytes 73732

commit v6 on v5

--- a/solution.py
+++ b/solution.py
@@ -67,7 +67,7 @@
 
 
 def pack_kernel(
-    feats_hbm, cot_hbm, frac_hbm, weight_hbm, count_hbm, halo, payload_hbm, feats, cot, frac, weight, count, payload, rows, sems
+    feats_hbm, cot_hbm, frac_hbm, weight_hbm, count_hbm, halo_hbm, payload_hbm, feats, cot, frac, weight, count, halo, payload, rows, sems
 ):
     pairs = (
         (frac_hbm, frac),
@@ -94,20 +94,28 @@
     halo[FRAC_AT:HALO] = where.astype(BF16)
     copies[1].wait()
     halo[0:CH] = feats[0]
+    sent = [pltpu.make_async_copy(halo, halo_hbm, sems.at[5])]
+    sent[0].start()
     for a in range(SLABS):
         payload[a, 0:COT_AT] = feats[0, a % 4 * QUARTER : (a % 4 + 1) * QUARTER]
+    copies[3].wait()
+    for a in range(SLABS):
+        payload[a, COT_AT:HID_AT] = cot[0, a // 4 * QUARTER : (a // 4 + 1) * QUARTER]
+    parts = slice(0, HID_AT), slice(HID_AT, PAY)
+    sent += [
+        pltpu.make_async_copy(payload.at[:, part], payload_hbm.at[:, part], sems.at[6 + n])
+        for n, part in enumerate(parts)
+    ]
+    sent[1].start()
     copies[2].wait()
     hidden = dot(weight[...], feats[0], TN)
     for a in range(SLABS):
         payload[a, HID_AT:PAY] = jnp.concatenate(
             [hidden[a * MINE : (a + 1) * MINE], where[0:8]], axis=0
         ).astype(BF16)
-    copies[3].wait()
-    for a in range(SLABS):
-        payload[a, COT_AT:HID_AT] = cot[0, a // 4 * QUARTER : (a // 4 + 1) * QUARTER]
-    sent = pltpu.make_async_copy(payload, payload_hbm, sems.at[5])
-    sent.start()
-    sent.wait()
+    sent[2].start()
+    for copy in sent:
+        copy.wait()
 
 
 def joined_count(rows):
@@ -198,19 +206,18 @@
     slot = lax.broadcasted_iota(I32, (SLOTS, ROWS), 0)
     lane32 = lax.broadcasted_iota(I32, (SLOTS, ROWS), 1)
     used = (slot < count[...]) & (lane32 < live_here)
-    weight = jnp.where(used, SLOTS**-0.5, 0.0)
+    column = jnp.where(used, column, -1)
     harmonics = (
-        weight,
-        weight * (ROOT3 * x),
-        weight * (ROOT3 * y),
-        weight * (ROOT3 * z),
-        weight * (ROOT15 * x * y),
-        weight * (ROOT15 * y * z),
-        weight * (0.5 * ROOT5 * (3.0 * z * z - square)),
-        weight * (ROOT15 * x * z),
-        weight * (0.5 * ROOT15 * (x * x - y * y)),
-    )
-    for m in range(9):
+        ROOT3 * x,
+        ROOT3 * y,
+        ROOT3 * z,
+        ROOT15 * x * y,
+        ROOT15 * y * z,
+        0.5 * ROOT5 * (3.0 * z * z - square),
+        ROOT15 * x * z,
+        0.5 * ROOT15 * (x * x - y * y),
+    )
+    for m in range(8):
         shape_w[m] = harmonics[m]
     length[...] = jnp.sqrt(square)
 
@@ -228,7 +235,7 @@
         basis[16:24, here] = hi.astype(F32)
     weights[...] = jnp.zeros((32, 3 * CH), F32)
     for l in range(3):
-        hi, lo = split(radial_weight[l])
+        hi, lo = split(radial_weight[l] * SLOTS**-0.5)
         part = slice(l * CH, (l + 1) * CH)
         weights[0:8, part] = hi.astype(F32)
         weights[8:16, part] = hi.astype(F32)
@@ -246,9 +253,10 @@
                 radial[pl.ds(pl.multiple_of(l * CH + top, BAND), BAND), here] * value
                 for l in range(3)
             ]
-            for m in range(9):
-                l = 0 if m == 0 else (1 if m < 4 else 2)
-                total[m] = total[m] + shape_w[m, e : e + 1, :] * parts[l]
+            total[0] = total[0] + parts[0]
+            for m in range(1, 9):
+                l = 1 if m < 4 else 2
+                total[m] = total[m] + shape_w[m - 1, e : e + 1, :] * parts[l]
         for m in range(9):
             feats9[m, pl.ds(top, BAND), :] = total[m]
         squares = [t * t for t in total]
@@ -282,7 +290,9 @@
             upstream.append(feats9[m, pl.ds(top, BAND), :] * up[l])
         for e in range(SLOTS):
             here = slice(e * ROWS, (e + 1) * ROWS)
-            term = [shape_w[m, e : e + 1, :] * upstream[m] for m in range(9)]
+            term = [upstream[0]] + [
+                shape_w[m - 1, e : e + 1, :] * upstream[m] for m in range(1, 9)
+            ]
             pull = (
                 radial[pl.ds(top, BAND), here] * term[0]
                 + radial[pl.ds(pl.multiple_of(CH + top, BAND), BAND), here]
@@ -554,7 +564,7 @@
     halo, payload = call(
         pack_kernel,
         [
-            (VMEM, struct((HALO, ROWS), BF16)),
+            (HBM, struct((HALO, ROWS), BF16)),
             (HBM, struct((SLABS, PAY, ROWS), BF16)),
         ],
         [
@@ -563,9 +573,10 @@
             pltpu.VMEM((3, 1, ROWS), F32),
             pltpu.VMEM((CH, CH), BF16),
             pltpu.VMEM((1, 1), I32),
+            pltpu.VMEM((HALO, ROWS), BF16),
             pltpu.VMEM((SLABS, PAY, ROWS), BF16),
             pltpu.VMEM((16, ROWS), F32),
-            pltpu.SemaphoreType.DMA((6,)),
+            pltpu.SemaphoreType.DMA((8,)),
         ],
         60,
         10**6,
@@ -592,7 +603,7 @@
             pltpu.VMEM((32, EDGES), F32),
             pltpu.VMEM((3 * CH, EDGES), F32),
             pltpu.VMEM((CH, EDGES), F32),
-            pltpu.VMEM((9, SLOTS, ROWS), F32),
+            pltpu.VMEM((8, SLOTS, ROWS), F32),
             pltpu.VMEM((SLOTS, ROWS), F32),
             pltpu.VMEM((9, CH, ROWS), F32),
             pltpu.VMEM((3 * CH, ROWS), F32),

time: 72.5 us -> 71.7 us (0.989)
  Pallas kernels: 13.8 us -> 12.9 us
    pallas_call x6, Pallas kernels: 13.8 us -> 12.9 us  [call(): pl.pallas_call(kernel, out_shape=[shape for _, shape in outs], in_specs=[...]
where the time goes in v6:
time: 71.7 us; the launch traced here: 71.3 us
  blocking collectives  40.6 us (57%)
  starting transfers between devices  13.4 us (19%)
  Pallas kernels  12.9 us (18%)
  waiting for transfers between devices  2.65 us (4%)
  between operations  1.49 us (2%)
    all_to_all x3, blocking collectives, exchange(): return lax.all_to_all(x, axis, 0, 0)  40.6 us
    pallas_call x6, Pallas kernels, call(): pl.pallas_call(kernel, out_shape=[shape for _, shape in outs], in_specs=[...  12.9 us
    ppermute x2, starting transfers between devices, shards(): lax.ppermute(halo, 'atom', [*pair, *((j, i) for i, j in pair)])  9.13 us
    all_to_all x1, starting transfers between devices, exchange(): return lax.all_to_all(x, axis, 0, 0)  4.32 us
    all_to_all x1, waiting for transfers between devices, exchange(): return lax.all_to_all(x, axis, 0, 0)  2.64 us
  transfers between devices with their start and end apart: 3, of which 1 were waited for; matrix products, arithmetic and copies ran while one was open for 0% of the time, Pallas kernels for 11%

profile of v6, /device:TPU:1, one launch (start us, length us, event | category | flops | bytes accessed | tf_op | source)
XLA Modules:
  0.0 71.3 jit_solution(343983745331120363)
XLA Ops:
  1.3 1.7 %shard_map.147 = (bf16[144,128]{1,0:T(8,128)(2,1)}, bf16[16,80,128]{2,1,0:T(8,128)(2,1)}) custom-call(bf16[1,128,128]{2,1,0:T(8,128)(2,1)} %feats_hbm.1, bf16[1,128,128]{2,1,0:T(8,128)(2,1)} %cot.1, f32[3,1,128]{2,1,0:T(1,128)} %bitcast.3, bf16[128,128]{1,0:T(8,128)(2,1)} %in_weight.1, s32[1,1]{1,0:T(1,128)} %bitcast.2.count_hbm), custom_call_target="tpu_custom_call" | custom-call | flops 1000000 | bytes 65536 | tf_op jit(solution)/shard_map/pallas_call | solution.py:56
  3.0 9.1 %collective-permute-start.1 = (bf16[144,128]{1,0:T(8,128)(2,1)}, bf16[144,128]{1,0:T(8,128)(2,1)S(1)}, u32[]{:S(2)}, u32[]{:S(2)}) collective-permute-start(bf16[144,128]{1,0:T(8,128)(2,1)} %get-tuple-element.16.own), channel_id=1, source_target_pairs={{1,2},{3,4},{5,6},{7,8},{9,10},{11,12},{13,14},{15,0},{2,1},{4,3},... | collective-permute-start | bytes 110600 | tf_op jit(solution)/shard_map/ppermute | solution.py:592
  12.1 0.0 collective-permute-start
  12.1 0.0 copy-start.5
  12.1 0.0 copy-start.6
  12.2 0.0 copy-start.7
  12.2 0.0 copy-start.8
  12.2 0.0 copy-start.9
  12.2 4.3 %all-to-all-start = ((bf16[16,80,128]{2,1,0:T(8,128)(2,1)}), bf16[16,80,128]{2,1,0:T(8,128)(2,1)S(1)}, u32[]{:S(2)}, u32[]{:S(2)}) async-start(bf16[16,80,128]{2,1,0:T(8,128)(2,1)} %get-tuple-element.15), calls=%async_computation | async-start | bytes 655360 | tf_op jit(solution)/shard_map/all_to_all | solution.py:545
  16.5 0.0 copy-start
  16.5 0.0 copy-start.4
  16.5 0.0 collective-permute-done.1.second_swap
  16.6 0.0 collective-permute-done.first_swap
  16.6 0.0 copy-done.1
  16.6 0.0 copy-done.2
  16.6 6.9 %shard_map.148 = (f32[512,128]{1,0:T(8,128)S(1)}, f32[128,128]{1,0:T(8,128)S(1)}) custom-call(bf16[144,128]{1,0:T(8,128)(2,1)S(1)} %copy-done.1, bf16[144,128]{1,0:T(8,128)(2,1)S(1)} %collective-permute-done.first_swap, bf16[144,128]{1,0:T(8,128)(2,1)S(1)} %collective-permute-done.1.second_swap, s32[1,32,128]{2,1,0:T(8,128)S(1)} %copy-done.6, ...), custom_call_target="tpu_custom_call" | custom-call | flops 10000000000 | bytes 65536 | tf_op jit(solution)/shard_map/pallas_call | solution.py:56
  23.6 0.8 %shard_map.149.folded = f32[64,896]{1,0:T(8,128)S(1)} custom-call(s32[3,2048]{1,0:T(4,128)S(1)} %copy-done.4, f32[2048,128]{1,0:T(8,128)S(1)} %copy-done), custom_call_target="tpu_custom_call" | custom-call | flops 100000000 | bytes 65536 | tf_op jit(solution)/shard_map/pallas_call | solution.py:56
  24.4 2.6 %all-to-all-done.gathered = bf16[16,80,128]{2,1,0:T(8,128)(2,1)S(1)} async-done(((bf16[16,80,128]{2,1,0:T(8,128)(2,1)}), bf16[16,80,128]{2,1,0:T(8,128)(2,1)S(1)}, u32[]{:S(2)}, u32[]{:S(2)}) %all-to-all-start) | async-done | bytes 327712 | tf_op jit(solution)/shard_map/all_to_all | solution.py:545
  27.0 2.6 %shard_map.150 = (bf16[16,48,128]{2,1,0:T(8,128)(2,1)S(1)}, bf16[16,8,128]{2,1,0:T(8,128)(2,1)S(1)}) custom-call(bf16[16,80,128]{2,1,0:T(8,128)(2,1)S(1)} %all-to-all-done.gathered, f32[64,896]{1,0:T(8,128)S(1)} %shard_map.149.folded, s32[3,2048]{1,0:T(4,128)S(1)} %copy-done.4, f32[512,128]{1,0:T(8,128)S(1)} %get-tuple-element.19.early), custom_call_target="tpu_custom_call" | custom-call | flops 10000000000 | bytes 65536 | tf_op jit(solution)/shard_map/pallas_call | solution.py:56
  29.6 14.3 %all_to_all.20 = bf16[16,48,128]{2,1,0:T(8,128)(2,1)S(1)} all-to-all(bf16[16,48,128]{2,1,0:T(8,128)(2,1)S(1)} %get-tuple-element.20), channel_id=1, replica_groups=mesh['dp'=16,'atom'=16] {'dp'}, dimensions={0} | all-to-all | bytes 393216 | tf_op jit(solution)/shard_map/all_to_all | solution.py:545
  44.0 14.7 %all_to_all.21.sums = bf16[16,56,128]{2,1,0:T(8,128)(2,1)S(1)} all-to-all(bf16[16,56,128]{2,1,0:T(8,128)(2,1)S(1)} %pad_maximum_fusion), channel_id=1, replica_groups=mesh['dp'=16,'atom'=16] {'atom'}, dimensions={0} | all-to-all | bytes 458752 | tf_op jit(solution)/shard_map/all_to_all | solution.py:545
  58.6 0.2 shard_map.151
  58.8 11.7 %all_to_all.22.sums = bf16[16,48,128]{2,1,0:T(8,128)(2,1)S(1)} all-to-all(bf16[16,48,128]{2,1,0:T(8,128)(2,1)S(1)} %get-tuple-element.23), channel_id=1, replica_groups=mesh['dp'=16,'atom'=16] {'dp'}, dimensions={0} | all-to-all | bytes 393216 | tf_op jit(solution)/shard_map/all_to_all | solution.py:545
  70.6 0.7 %shard_map.152 = (bf16[1,128,128]{2,1,0:T(8,128)(2,1)}, f32[128,128]{1,0:T(8,128)}, f32[128,128]{1,0:T(8,128)}, f32[384,128]{1,0:T(8,128)}) custom-call(bf16[16,48,128]{2,1,0:T(8,128)(2,1)S(1)} %all_to_all.22.sums, f32[128,128]{1,0:T(8,128)S(1)} %get-tuple-element.24.ewald_in, f32[128,128]{1,0:T(8,128)S(1)} %get-tuple-element.25.field), custom_call_target="tpu_custom_call" | custom-call | flops 1000000 | bytes 65536 | tf_op jit(solution)/shard_map/pallas_call | solution.py:56
  (14 shorter events, 0.1 us)
Async XLA Ops:
  3.0 13.6 %collective-permute-start.1 = (bf16[144,128]{1,0:T(8,128)(2,1)}, bf16[144,128]{1,0:T(8,128)(2,1)S(1)}, u32[]{:S(2)}, u32[]{:S(2)}) collective-permute-start(bf16[144,128]{1,0:T(8,128)(2,1)} %get-tuple-element.16.own), channel_id=1, source_target_pairs={{1,2},{3,4},{5,6},{7,8},{9,10},{11,12},{13,14},{15,0},{2,1},{4,3},... | collective-permute-start | bytes 110600 | tf_op jit(solution)/shard_map/ppermute | solution.py:592
  12.1 4.4 %collective-permute-start = (bf16[144,128]{1,0:T(8,128)(2,1)}, bf16[144,128]{1,0:T(8,128)(2,1)S(1)}, u32[]{:S(2)}, u32[]{:S(2)}) collective-permute-start(bf16[144,128]{1,0:T(8,128)(2,1)} %get-tuple-element.16.own), channel_id=1, source_target_pairs={{0,1},{2,3},{4,5},{6,7},{8,9},{10,11},{12,13},{14,15},{1,0},{3,2},... | collective-permute-start | bytes 110600 | tf_op jit(solution)/shard_map/ppermute | solution.py:592
  12.1 4.4 %copy-start.1 = (bf16[144,128]{1,0:T(8,128)(2,1)S(1)}, bf16[144,128]{1,0:T(8,128)(2,1)}, u32[]{:S(2)}) copy-start(bf16[144,128]{1,0:T(8,128)(2,1)} %get-tuple-element.16.own) | copy-start | bytes 110596
  12.1 4.5 %copy-start.2 = (bf16[1,128,128]{2,1,0:T(8,128)(2,1)S(1)}, bf16[1,128,128]{2,1,0:T(8,128)(2,1)}, u32[]{:S(2)}) copy-start(bf16[1,128,128]{2,1,0:T(8,128)(2,1)} %cot.1) | copy-start | bytes 98308
  12.1 4.5 %copy-start.3 = (bf16[128,128]{1,0:T(8,128)(2,1)S(1)}, bf16[128,128]{1,0:T(8,128)(2,1)}, u32[]{:S(2)}) copy-start(bf16[128,128]{1,0:T(8,128)(2,1)} %in_weight.1) | copy-start | bytes 98308
  12.1 4.5 %copy-start.5 = (bf16[384,128]{1,0:T(8,128)(2,1)S(1)}, bf16[384,128]{1,0:T(8,128)(2,1)}, u32[]{:S(2)}) copy-start(bf16[384,128]{1,0:T(8,128)(2,1)} %out_weight.1) | copy-start | bytes 294916
  12.1 4.5 %copy-start.6 = (s32[1,32,128]{2,1,0:T(8,128)S(1)}, s32[1,32,128]{2,1,0:T(8,128)}, u32[]{:S(2)}) copy-start(s32[1,32,128]{2,1,0:T(8,128)} %neighbours.1) | copy-start | bytes 49156
  12.2 4.5 %copy-start.7 = (s32[1,32,128]{2,1,0:T(8,128)S(1)}, s32[1,32,128]{2,1,0:T(8,128)}, u32[]{:S(2)}) copy-start(s32[1,32,128]{2,1,0:T(8,128)} %images.1) | copy-start | bytes 49156
  12.2 4.5 %copy-start.8 = (f32[3,8,128]{2,1,0:T(8,128)S(1)}, f32[3,8,128]{2,1,0:T(8,128)}, u32[]{:S(2)}) copy-start(f32[3,8,128]{2,1,0:T(8,128)} %radial_weight.1) | copy-start | bytes 36868
  12.2 4.5 %copy-start.9 = (s32[1,128]{1,0:T(1,128)S(1)}, s32[1,128]{1,0:T(1,128)}, u32[]{:S(2)}) copy-start(s32[1,128]{1,0:T(1,128)} %count.1) | copy-start | bytes 1540
  12.2 14.8 %all-to-all-start = ((bf16[16,80,128]{2,1,0:T(8,128)(2,1)}), bf16[16,80,128]{2,1,0:T(8,128)(2,1)S(1)}, u32[]{:S(2)}, u32[]{:S(2)}) async-start(bf16[16,80,128]{2,1,0:T(8,128)(2,1)} %get-tuple-element.15), calls=%async_computation | async-start | bytes 655360 | tf_op jit(solution)/shard_map/all_to_all | solution.py:545
  16.5 7.0 %copy-start = (f32[2048,128]{1,0:T(8,128)S(1)}, f32[2048,128]{1,0:T(8,128)}, u32[]{:S(2)}) copy-start(f32[2048,128]{1,0:T(8,128)} %filter_weight.1) | copy-start | bytes 3145732
  16.5 7.0 %copy-start.4 = (s32[3,2048]{1,0:T(4,128)S(1)}, s32[3,2048]{1,0:T(4,128)}, u32[]{:S(2)}) copy-start(s32[3,2048]{1,0:T(4,128)} %miller.1) | copy-start | bytes 73732

commit v7 on v6

--- a/solution.py
+++ b/solution.py
@@ -486,7 +486,7 @@
     for f in range(1, WAVES):
         total = total + field[f * MINE : (f + 1) * MINE] * along[f]
     for p in range(SLABS):
-        ewald[p] = total[:, p * ROWS : (p + 1) * ROWS].astype(BF16)
+        ewald[p] = total[:, p * ROWS : (p + 1) * ROWS]
 
 
 SPECTRUM_SCRATCH = [
@@ -498,45 +498,63 @@
 ]
 
 
-def middle_kernel(sums, own, local, last, grad_in, field):
-    row = lax.broadcasted_iota(I32, (8, KSHARE), 0)
-    lane = lax.broadcasted_iota(I32, (8, KSHARE), 1)
-    pick = jnp.where(lane == row + MINE * lax.axis_index("atom"), 1.0, 0.0).astype(BF16)
+def turn_kernel(sums, ewald, out):
+    total = sums[0].astype(F32)
+    for d in range(1, STRUCTS):
+        total = total + sums[d].astype(F32)
+    lane = lax.broadcasted_iota(I32, (MINE, CH), 1)
+    share = pltpu.roll(total[8:16], (8 - 8 * lax.axis_index("dp")) & (CH - 1), 1)
+    for p in range(SLABS):
+        picked = pltpu.roll(total[0:8], (CH - 8 * p) % CH, 1)
+        out[p] = jnp.concatenate(
+            [total[16:48], jnp.where(lane < 8, picked, share), ewald[p]], axis=0
+        ).astype(BF16)
+
+
+def middle_kernel(sums, own, local, last, field):
+    row = lax.broadcasted_iota(I32, (8, CH), 0)
+    lane = lax.broadcasted_iota(I32, (8, CH), 1)
+    pick = jnp.where(lane == row, 1.0, 0.0).astype(BF16)
     blocks = [sums[p].astype(F32) for p in range(SLABS)]
-    pairs = jnp.concatenate([block[0:8] for block in blocks], axis=0)
+    pairs = jnp.concatenate([block[32:40] for block in blocks], axis=0)
     picked = dot(pick, pairs.astype(BF16), NT)
-    total = blocks[0][16:48]
+    total, share = blocks[0][0:32], jnp.zeros((8, CH), F32)
     for block in blocks[1:]:
-        total = total + block[16:48]
-    out = jnp.concatenate([total, picked, picked], axis=0).astype(BF16)
+        total = total + block[0:32]
+    for p, block in enumerate(blocks):
+        turned = pltpu.roll(block[32:40], (8 * p - 8) % CH, 1)
+        share = jnp.where(lane >> 3 == p, turned, share)
+    out = jnp.concatenate([total, picked, share], axis=0).astype(BF16)
     for d in range(STRUCTS):
         last[d] = out
-    grads = []
-    for c in range(0, CH, 8):
-        at, g = c % QUARTER // 8, c // QUARTER
-        eight = blocks[4 * g][8:16]
-        eight = pltpu.roll(eight, (0 - at) * QUARTER % CH, 1)
-        for q in range(1, 4):
-            turned = pltpu.roll(blocks[4 * g + q][8:16], (q - at) * QUARTER % CH, 1)
-            eight = jnp.where(lane < q * QUARTER, eight, turned)
-        grads.append(eight)
-    grad_in[...] = jnp.concatenate(grads, axis=0).T
-    ewald = jnp.concatenate([block[48:56] for block in blocks], axis=0)
+    ewald = jnp.concatenate([block[40:48] for block in blocks], axis=0)
     live = joined_count(own[FRAC_AT:HALO]).astype(I32) - lax.axis_index("atom") * ROWS
     live = lax.broadcasted_iota(I32, (CH, ROWS), 1) < live
     field[...] = jnp.where(live, own[0:CH].astype(F32) + local[...] + ewald, 0.0)
 
 
-def finish_kernel(
-    sums, ewald_in, field, updated, grad_filter, grad_in, grad_out
-):
+def finish_kernel(sums, field, updated, grad_filter, grad_in, grad_out):
     updated[0] = field[...].astype(BF16)
+    lane8 = lax.broadcasted_iota(I32, (8, CH), 1)
+    heads = [sums[d, 32:48].astype(F32) for d in range(STRUCTS)]
     for d in range(STRUCTS):
-        late = sums[d, 32:48].astype(F32)
-        grad_filter[8 * d : 8 * d + 8, :] = late[0:8]
+        grad_filter[8 * d : 8 * d + 8, :] = heads[d][0:8]
+    grads = []
+    for c in range(0, CH, 8):
+        g, q = c // QUARTER, c % QUARTER // 8
+        eight = pltpu.roll(heads[4 * q][8:16], (0 - g) * QUARTER % CH, 1)
+        for u in range(1, 4):
+            turned = pltpu.roll(heads[4 * q + u][8:16], (u - g) * QUARTER % CH, 1)
+            eight = jnp.where(lane8 < u * QUARTER, eight, turned)
+        grads.append(eight)
+    row = lax.broadcasted_iota(I32, (CH, CH), 0)
+    lane = lax.broadcasted_iota(I32, (CH, CH), 1)
+    channel = 32 * ((lane >> 3) & 3) + 8 * (lane >> 5) + (lane & 7)
+    order = jnp.where(row == channel, 1.0, 0.0).astype(BF16)
+    ewald_in = dot(order, jnp.concatenate(grads, axis=0).astype(BF16), NT)
     for d in range(4):
         here = slice(d * SLOTS, (d + 1) * SLOTS)
-        grad_in[here, :] = ewald_in[here, :] + sums[d, 0:32].astype(F32)
+        grad_in[here, :] = ewald_in[here] + sums[d, 0:32].astype(F32)
     for d in range(4, STRUCTS):
         grad_out[(d - 4) * SLOTS : (d - 3) * SLOTS, :] = sums[d, 0:32].astype(F32)
 
@@ -640,7 +658,7 @@
         spectrum_kernel,
         [
             (VMEM, struct((STRUCTS, 48, CH), BF16)),
-            (VMEM, struct((SLABS, MINE, ROWS), BF16)),
+            (VMEM, struct((SLABS, MINE, ROWS), F32)),
         ],
         SPECTRUM_SCRATCH,
         20,
@@ -650,37 +668,44 @@
         (VMEM, miller),
         (VMEM, early),
     )
-    sums = exchange(parts, "dp").astype(F32).sum(axis=0).astype(BF16)
-    sums = jnp.broadcast_to(sums[None], (SLABS, 48, CH))
-    last, ewald_in, field = call(
+    (sums,) = call(
+        turn_kernel,
+        [(VMEM, struct((SLABS, 48, CH), BF16))],
+        [],
+        16,
+        10**6,
+        (VMEM, exchange(parts, "dp")),
+        (VMEM, ewald),
+    )
+    last, field = call(
         middle_kernel,
         [
             (VMEM, struct((STRUCTS, 48, CH), BF16)),
-            (VMEM, struct((CH, CH), F32)),
             (VMEM, struct((CH, ROWS), F32)),
         ],
         [],
         16,
         10**6,
-        (VMEM, exchange(jnp.concatenate([sums, ewald], axis=1), "atom")),
+        (VMEM, exchange(sums, "atom")),
         (VMEM, halo),
         (VMEM, local),
     )
-    return tuple(call(
-        finish_kernel,
-        [
-            (VMEM, struct((1, CH, ROWS), BF16)),
-            (VMEM, struct((KSHARE, CH), F32)),
-            (VMEM, struct((CH, CH), F32)),
-            (VMEM, struct((3 * CH, CH), F32)),
-        ],
-        [],
-        16,
-        10**6,
-        (VMEM, exchange(last, "dp")),
-        (VMEM, ewald_in),
-        (VMEM, field),
-    ))
+    return tuple(
+        call(
+            finish_kernel,
+            [
+                (VMEM, struct((1, CH, ROWS), BF16)),
+                (VMEM, struct((KSHARE, CH), F32)),
+                (VMEM, struct((CH, CH), F32)),
+                (VMEM, struct((3 * CH, CH), F32)),
+            ],
+            [],
+            16,
+            10**6,
+            (VMEM, exchange(last, "dp")),
+            (VMEM, field),
+        )
+    )
 
 
 def solution(mesh):

time: 71.7 us -> 71.2 us (level)
    pallas_call x6 -> x7, Pallas kernels: 12.9 us -> 13.1 us  [call(): pl.pallas_call(kernel, out_shape=[shape for _, shape in outs], in_specs=[...]
where the time goes in v7:
time: 71.2 us; the launch traced here: 70.8 us
  blocking collectives  40 us (56%)
  starting transfers between devices  13.4 us (19%)
  Pallas kernels  13.1 us (18%)
  waiting for transfers between devices  2.66 us (4%)
  between operations  1.48 us (2%)
    all_to_all x3, blocking collectives, exchange(): return lax.all_to_all(x, axis, 0, 0)  40 us
    pallas_call x7, Pallas kernels, call(): pl.pallas_call(kernel, out_shape=[shape for _, shape in outs], in_specs=[...  13.1 us
    ppermute x2, starting transfers between devices, shards(): lax.ppermute(halo, 'atom', [*pair, *((j, i) for i, j in pair)])  9.13 us
    all_to_all x1, starting transfers between devices, exchange(): return lax.all_to_all(x, axis, 0, 0)  4.32 us
    all_to_all x1, waiting for transfers between devices, exchange(): return lax.all_to_all(x, axis, 0, 0)  2.65 us
  transfers between devices with their start and end apart: 3, of which 1 were waited for; matrix products, arithmetic and copies ran while one was open for 0% of the time, Pallas kernels for 11%

profile of v7, /device:TPU:1, one launch (start us, length us, event | category | flops | bytes accessed | tf_op | source)
XLA Modules:
  0.0 70.8 jit_solution(17880768436588144725)
XLA Ops:
  1.3 1.7 %shard_map.147 = (bf16[144,128]{1,0:T(8,128)(2,1)}, bf16[16,80,128]{2,1,0:T(8,128)(2,1)}) custom-call(bf16[1,128,128]{2,1,0:T(8,128)(2,1)} %feats_hbm.1, bf16[1,128,128]{2,1,0:T(8,128)(2,1)} %cot.1, f32[3,1,128]{2,1,0:T(1,128)} %bitcast.3, bf16[128,128]{1,0:T(8,128)(2,1)} %in_weight.1, s32[1,1]{1,0:T(1,128)} %bitcast.2.count_hbm), custom_call_target="tpu_custom_call" | custom-call | flops 1000000 | bytes 65536 | tf_op jit(solution)/shard_map/pallas_call | solution.py:56
  3.0 9.1 %collective-permute-start.1 = (bf16[144,128]{1,0:T(8,128)(2,1)}, bf16[144,128]{1,0:T(8,128)(2,1)S(1)}, u32[]{:S(2)}, u32[]{:S(2)}) collective-permute-start(bf16[144,128]{1,0:T(8,128)(2,1)} %get-tuple-element.15.own), channel_id=1, source_target_pairs={{1,2},{3,4},{5,6},{7,8},{9,10},{11,12},{13,14},{15,0},{2,1},{4,3},... | collective-permute-start | bytes 110600 | tf_op jit(solution)/shard_map/ppermute | solution.py:610
  12.1 0.0 collective-permute-start
  12.1 0.0 copy-start.5
  12.2 0.0 copy-start.6
  12.2 0.0 copy-start.7
  12.2 0.0 copy-start.8
  12.2 0.0 copy-start.9
  12.2 4.3 %all-to-all-start = ((bf16[16,80,128]{2,1,0:T(8,128)(2,1)}), bf16[16,80,128]{2,1,0:T(8,128)(2,1)S(1)}, u32[]{:S(2)}, u32[]{:S(2)}) async-start(bf16[16,80,128]{2,1,0:T(8,128)(2,1)} %get-tuple-element.14), calls=%async_computation | async-start | bytes 655360 | tf_op jit(solution)/shard_map/all_to_all | solution.py:563
  16.5 0.0 copy-start
  16.5 0.0 copy-start.4
  16.6 0.0 collective-permute-done.1.second_swap
  16.6 0.0 collective-permute-done.first_swap
  16.6 0.0 copy-done.1
  16.7 6.9 %shard_map.148 = (f32[512,128]{1,0:T(8,128)S(1)}, f32[128,128]{1,0:T(8,128)S(1)}) custom-call(bf16[144,128]{1,0:T(8,128)(2,1)S(1)} %copy-done.1, bf16[144,128]{1,0:T(8,128)(2,1)S(1)} %collective-permute-done.first_swap, bf16[144,128]{1,0:T(8,128)(2,1)S(1)} %collective-permute-done.1.second_swap, s32[1,32,128]{2,1,0:T(8,128)S(1)} %copy-done.6, ...), custom_call_target="tpu_custom_call" | custom-call | flops 10000000000 | bytes 65536 | tf_op jit(solution)/shard_map/pallas_call | solution.py:56
  23.6 0.8 %shard_map.149.folded = f32[64,896]{1,0:T(8,128)S(1)} custom-call(s32[3,2048]{1,0:T(4,128)S(1)} %copy-done.4, f32[2048,128]{1,0:T(8,128)S(1)} %copy-done), custom_call_target="tpu_custom_call" | custom-call | flops 100000000 | bytes 65536 | tf_op jit(solution)/shard_map/pallas_call | solution.py:56
  24.4 2.7 %all-to-all-done.gathered = bf16[16,80,128]{2,1,0:T(8,128)(2,1)S(1)} async-done(((bf16[16,80,128]{2,1,0:T(8,128)(2,1)}), bf16[16,80,128]{2,1,0:T(8,128)(2,1)S(1)}, u32[]{:S(2)}, u32[]{:S(2)}) %all-to-all-start) | async-done | bytes 327712 | tf_op jit(solution)/shard_map/all_to_all | solution.py:563
  27.0 2.6 %shard_map.150 = (bf16[16,48,128]{2,1,0:T(8,128)(2,1)S(1)}, f32[16,8,128]{2,1,0:T(8,128)S(1)}) custom-call(bf16[16,80,128]{2,1,0:T(8,128)(2,1)S(1)} %all-to-all-done.gathered, f32[64,896]{1,0:T(8,128)S(1)} %shard_map.149.folded, s32[3,2048]{1,0:T(4,128)S(1)} %copy-done.4, f32[512,128]{1,0:T(8,128)S(1)} %get-tuple-element.18.early), custom_call_target="tpu_custom_call" | custom-call | flops 10000000000 | bytes 65536 | tf_op jit(solution)/shard_map/pallas_call | solution.py:56
  29.6 14.3 %all_to_all.20.sums = bf16[16,48,128]{2,1,0:T(8,128)(2,1)S(1)} all-to-all(bf16[16,48,128]{2,1,0:T(8,128)(2,1)S(1)} %get-tuple-element.19), channel_id=1, replica_groups=mesh['dp'=16,'atom'=16] {'dp'}, dimensions={0} | all-to-all | bytes 393216 | tf_op jit(solution)/shard_map/all_to_all | solution.py:563
  43.9 0.1 shard_map.151
  44.0 14.4 %all_to_all.21.sums = bf16[16,48,128]{2,1,0:T(8,128)(2,1)S(1)} all-to-all(bf16[16,48,128]{2,1,0:T(8,128)(2,1)S(1)} %shard_map.151), channel_id=1, replica_groups=mesh['dp'=16,'atom'=16] {'atom'}, dimensions={0} | all-to-all | bytes 393216 | tf_op jit(solution)/shard_map/all_to_all | solution.py:563
  58.4 0.2 shard_map.152
  58.5 11.4 %all_to_all.22.sums = bf16[16,48,128]{2,1,0:T(8,128)(2,1)S(1)} all-to-all(bf16[16,48,128]{2,1,0:T(8,128)(2,1)S(1)} %get-tuple-element.22), channel_id=1, replica_groups=mesh['dp'=16,'atom'=16] {'dp'}, dimensions={0} | all-to-all | bytes 393216 | tf_op jit(solution)/shard_map/all_to_all | solution.py:563
  70.0 0.9 %shard_map.153 = (bf16[1,128,128]{2,1,0:T(8,128)(2,1)}, f32[128,128]{1,0:T(8,128)}, f32[128,128]{1,0:T(8,128)}, f32[384,128]{1,0:T(8,128)}) custom-call(bf16[16,48,128]{2,1,0:T(8,128)(2,1)S(1)} %all_to_all.22.sums, f32[128,128]{1,0:T(8,128)S(1)} %get-tuple-element.23.field), custom_call_target="tpu_custom_call" | custom-call | flops 1000000 | bytes 65536 | tf_op jit(solution)/shard_map/pallas_call | solution.py:56
  (12 shorter events, 0.0 us)
Async XLA Ops:
  3.0 13.6 %collective-permute-start.1 = (bf16[144,128]{1,0:T(8,128)(2,1)}, bf16[144,128]{1,0:T(8,128)(2,1)S(1)}, u32[]{:S(2)}, u32[]{:S(2)}) collective-permute-start(bf16[144,128]{1,0:T(8,128)(2,1)} %get-tuple-element.15.own), channel_id=1, source_target_pairs={{1,2},{3,4},{5,6},{7,8},{9,10},{11,12},{13,14},{15,0},{2,1},{4,3},... | collective-permute-start | bytes 110600 | tf_op jit(solution)/shard_map/ppermute | solution.py:610
  12.1 4.4 %collective-permute-start = (bf16[144,128]{1,0:T(8,128)(2,1)}, bf16[144,128]{1,0:T(8,128)(2,1)S(1)}, u32[]{:S(2)}, u32[]{:S(2)}) collective-permute-start(bf16[144,128]{1,0:T(8,128)(2,1)} %get-tuple-element.15.own), channel_id=1, source_target_pairs={{0,1},{2,3},{4,5},{6,7},{8,9},{10,11},{12,13},{14,15},{1,0},{3,2},... | collective-permute-start | bytes 110600 | tf_op jit(solution)/shard_map/ppermute | solution.py:610
  12.1 4.4 %copy-start.1 = (bf16[144,128]{1,0:T(8,128)(2,1)S(1)}, bf16[144,128]{1,0:T(8,128)(2,1)}, u32[]{:S(2)}) copy-start(bf16[144,128]{1,0:T(8,128)(2,1)} %get-tuple-element.15.own) | copy-start | bytes 110596
  12.1 4.5 %copy-start.2 = (bf16[1,128,128]{2,1,0:T(8,128)(2,1)S(1)}, bf16[1,128,128]{2,1,0:T(8,128)(2,1)}, u32[]{:S(2)}) copy-start(bf16[1,128,128]{2,1,0:T(8,128)(2,1)} %cot.1) | copy-start | bytes 98308
  12.1 4.5 %copy-start.3 = (bf16[128,128]{1,0:T(8,128)(2,1)S(1)}, bf16[128,128]{1,0:T(8,128)(2,1)}, u32[]{:S(2)}) copy-start(bf16[128,128]{1,0:T(8,128)(2,1)} %in_weight.1) | copy-start | bytes 98308
  12.1 4.5 %copy-start.5 = (bf16[384,128]{1,0:T(8,128)(2,1)S(1)}, bf16[384,128]{1,0:T(8,128)(2,1)}, u32[]{:S(2)}) copy-start(bf16[384,128]{1,0:T(8,128)(2,1)} %out_weight.1) | copy-start | bytes 294916
  12.2 4.5 %copy-start.6 = (s32[1,32,128]{2,1,0:T(8,128)S(1)}, s32[1,32,128]{2,1,0:T(8,128)}, u32[]{:S(2)}) copy-start(s32[1,32,128]{2,1,0:T(8,128)} %neighbours.1) | copy-start | bytes 49156
  12.2 4.5 %copy-start.7 = (s32[1,32,128]{2,1,0:T(8,128)S(1)}, s32[1,32,128]{2,1,0:T(8,128)}, u32[]{:S(2)}) copy-start(s32[1,32,128]{2,1,0:T(8,128)} %images.1) | copy-start | bytes 49156
  12.2 4.5 %copy-start.8 = (f32[3,8,128]{2,1,0:T(8,128)S(1)}, f32[3,8,128]{2,1,0:T(8,128)}, u32[]{:S(2)}) copy-start(f32[3,8,128]{2,1,0:T(8,128)} %radial_weight.1) | copy-start | bytes 36868
  12.2 4.5 %copy-start.9 = (s32[1,128]{1,0:T(1,128)S(1)}, s32[1,128]{1,0:T(1,128)}, u32[]{:S(2)}) copy-start(s32[1,128]{1,0:T(1,128)} %count.1) | copy-start | bytes 1540
  12.2 14.8 %all-to-all-start = ((bf16[16,80,128]{2,1,0:T(8,128)(2,1)}), bf16[16,80,128]{2,1,0:T(8,128)(2,1)S(1)}, u32[]{:S(2)}, u32[]{:S(2)}) async-start(bf16[16,80,128]{2,1,0:T(8,128)(2,1)} %get-tuple-element.14), calls=%async_computation | async-start | bytes 655360 | tf_op jit(solution)/shard_map/all_to_all | solution.py:563
  16.5 7.0 %copy-start = (f32[2048,128]{1,0:T(8,128)S(1)}, f32[2048,128]{1,0:T(8,128)}, u32[]{:S(2)}) copy-start(f32[2048,128]{1,0:T(8,128)} %filter_weight.1) | copy-start | bytes 3145732
  16.5 7.0 %copy-start.4 = (s32[3,2048]{1,0:T(4,128)S(1)}, s32[3,2048]{1,0:T(4,128)}, u32[]{:S(2)}) copy-start(s32[3,2048]{1,0:T(4,128)} %miller.1) | copy-start | bytes 73732

commit v8 on v7

--- a/solution.py
+++ b/solution.py
@@ -33,10 +33,12 @@
 QUARTER = CH // 4
 FRAC_AT = CH
 HALO = CH + 16
+THIRD = HALO // 3
 COT_AT, HID_AT, PAY = QUARTER, 2 * QUARTER, 2 * QUARTER + 16
 
 VMEM = pl.BlockSpec(memory_space=pltpu.VMEM)
 HBM = pl.BlockSpec(memory_space=pltpu.HBM)
+SMEM = pl.BlockSpec(memory_space=pltpu.SMEM)
 
 NN = (((1,), (0,)), ((), ()))
 NT = (((1,), (1,)), ((), ()))
@@ -67,14 +69,13 @@
 
 
 def pack_kernel(
-    feats_hbm, cot_hbm, frac_hbm, weight_hbm, count_hbm, halo_hbm, payload_hbm, feats, cot, frac, weight, count, halo, payload, rows, sems
+    feats_hbm, cot_hbm, frac_hbm, weight_hbm, halo_hbm, first_hbm, second_hbm, payload_hbm, feats, cot, frac, weight, halo, first_end, second_end, payload, rows, sems
 ):
     pairs = (
         (frac_hbm, frac),
         (feats_hbm, feats),
         (weight_hbm, weight),
         (cot_hbm, cot),
-        (count_hbm, count),
     )
     copies = [
         pltpu.make_async_copy(src, dst, sems.at[n]) for n, (src, dst) in enumerate(pairs)
@@ -87,15 +88,29 @@
         first = jnp.floor(frac[d] * 256.0) * (1.0 / 256.0)
         rows[d : d + 1, :] = first
         rows[d + 3 : d + 4, :] = frac[d] - first
-    copies[4].wait()
-    rows[6:7, :] = jnp.broadcast_to((count[...] >> 4).astype(F32), (1, ROWS))
-    rows[7:8, :] = jnp.broadcast_to((count[...] & 15).astype(F32), (1, ROWS))
     where = rows[...]
     halo[FRAC_AT:HALO] = where.astype(BF16)
     copies[1].wait()
     halo[0:CH] = feats[0]
-    sent = [pltpu.make_async_copy(halo, halo_hbm, sems.at[5])]
-    sent[0].start()
+    wide = jnp.concatenate([feats[0].astype(F32), where], axis=0)
+    bands = [wide[n * THIRD : (n + 1) * THIRD] for n in range(3)]
+    lane = lax.broadcasted_iota(I32, (THIRD, ROWS), 1)
+
+    def dense(shift):
+        turned = [pltpu.roll(b, shift + GHOST * n, 1) if shift + n else b for n, b in enumerate(bands)]
+        return jnp.where(lane < GHOST, turned[0], jnp.where(lane < 2 * GHOST, turned[1], turned[2]))
+
+    low, high = dense(0), dense(GHOST)
+    even = (lax.axis_index("atom") & 1) == 0
+    first_end[...] = jnp.where(even, high, low).astype(BF16)
+    second_end[...] = jnp.where(even, low, high).astype(BF16)
+    sent = [
+        pltpu.make_async_copy(first_end, first_hbm, sems.at[8]),
+        pltpu.make_async_copy(second_end, second_hbm, sems.at[9]),
+        pltpu.make_async_copy(halo, halo_hbm, sems.at[5]),
+    ]
+    for copy in sent:
+        copy.start()
     for a in range(SLABS):
         payload[a, 0:COT_AT] = feats[0, a % 4 * QUARTER : (a % 4 + 1) * QUARTER]
     copies[3].wait()
@@ -106,21 +121,16 @@
         pltpu.make_async_copy(payload.at[:, part], payload_hbm.at[:, part], sems.at[6 + n])
         for n, part in enumerate(parts)
     ]
-    sent[1].start()
+    sent[3].start()
     copies[2].wait()
     hidden = dot(weight[...], feats[0], TN)
     for a in range(SLABS):
         payload[a, HID_AT:PAY] = jnp.concatenate(
             [hidden[a * MINE : (a + 1) * MINE], where[0:8]], axis=0
         ).astype(BF16)
-    sent[2].start()
+    sent[4].start()
     for copy in sent:
         copy.wait()
-
-
-def joined_count(rows):
-    wide = rows.astype(F32)
-    return 16.0 * wide[6:7] + wide[7:8]
 
 
 def joined_frac(rows):
@@ -135,6 +145,7 @@
 
 
 def edge_kernel(
+    atom_count,
     own,
     first_swap,
     second_swap,
@@ -162,7 +173,7 @@
 ):
     slab = lax.axis_index("atom")
     first = slab * ROWS
-    atoms = joined_count(own[FRAC_AT:HALO]).astype(I32)
+    atoms = atom_count[0]
     live_here = atoms - first
     live_left = atoms - ((first - ROWS) & (ATOMS - 1))
     live_right = atoms - ((first + ROWS) & (ATOMS - 1))
@@ -172,6 +183,12 @@
     swaps = first_swap[...].astype(F32), second_swap[...].astype(F32)
     right = jnp.where(even, swaps[0], swaps[1])
     left = jnp.where(even, swaps[1], swaps[0])
+    right = jnp.concatenate(
+        [right] + [pltpu.roll(right, ROWS - GHOST * n, 1) for n in (1, 2)], axis=0
+    )
+    left = jnp.concatenate(
+        [pltpu.roll(left, ROWS - GHOST * (n + 1), 1) for n in range(3)], axis=0
+    )
     near_right = jnp.where(lane < live_right, right[0:CH], 0.0)
     near_left = jnp.where(lane < live_left, left[0:CH], 0.0)
     ext[:, ROWS : 2 * ROWS] = jnp.where(lane < GHOST, near_right, near_left).astype(BF16)
@@ -416,7 +433,7 @@
 
 
 def spectrum_kernel(
-    gathered, folded, miller, early, parts, ewald, factor, frac, values, plane, wide
+    atom_count, gathered, folded, miller, early, parts, ewald, factor, frac, values, plane, wide
 ):
     for p in range(SLABS):
         here = slice(p * ROWS, (p + 1) * ROWS)
@@ -424,8 +441,7 @@
         tail = gathered[p, HID_AT:PAY].astype(F32)
         frac[0:3, here] = tail[MINE : MINE + 3] + tail[MINE + 3 : MINE + 6]
     along = waves([frac[d : d + 1, :] for d in range(3)], plane)
-    atoms = joined_count(gathered[0, HID_AT:PAY].astype(F32)[MINE:16]).astype(I32)
-    live = lax.broadcasted_iota(I32, (1, ATOMS), 1) < atoms[:, 0:1]
+    live = lax.broadcasted_iota(I32, (1, ATOMS), 1) < atom_count[0]
     live = jnp.where(live, 1.0, 0.0)
     around = plane[...].astype(BF16)
     for low, high in ((0, TOP + 1), (TOP + 1, WAVES)):
@@ -511,7 +527,7 @@
         ).astype(BF16)
 
 
-def middle_kernel(sums, own, local, last, field):
+def middle_kernel(atom_count, sums, own, local, last, field):
     row = lax.broadcasted_iota(I32, (8, CH), 0)
     lane = lax.broadcasted_iota(I32, (8, CH), 1)
     pick = jnp.where(lane == row, 1.0, 0.0).astype(BF16)
@@ -528,7 +544,7 @@
     for d in range(STRUCTS):
         last[d] = out
     ewald = jnp.concatenate([block[40:48] for block in blocks], axis=0)
-    live = joined_count(own[FRAC_AT:HALO]).astype(I32) - lax.axis_index("atom") * ROWS
+    live = atom_count[0] - lax.axis_index("atom") * ROWS
     live = lax.broadcasted_iota(I32, (CH, ROWS), 1) < live
     field[...] = jnp.where(live, own[0:CH].astype(F32) + local[...] + ewald, 0.0)
 
@@ -579,10 +595,12 @@
 ):
     struct = jax.ShapeDtypeStruct
 
-    halo, payload = call(
+    halo, *ends, payload = call(
         pack_kernel,
         [
             (HBM, struct((HALO, ROWS), BF16)),
+            (HBM, struct((THIRD, ROWS), BF16)),
+            (HBM, struct((THIRD, ROWS), BF16)),
             (HBM, struct((SLABS, PAY, ROWS), BF16)),
         ],
         [
@@ -590,11 +608,12 @@
             pltpu.VMEM((1, CH, ROWS), BF16),
             pltpu.VMEM((3, 1, ROWS), F32),
             pltpu.VMEM((CH, CH), BF16),
-            pltpu.VMEM((1, 1), I32),
             pltpu.VMEM((HALO, ROWS), BF16),
+            pltpu.VMEM((THIRD, ROWS), BF16),
+            pltpu.VMEM((THIRD, ROWS), BF16),
             pltpu.VMEM((SLABS, PAY, ROWS), BF16),
             pltpu.VMEM((16, ROWS), F32),
-            pltpu.SemaphoreType.DMA((8,)),
+            pltpu.SemaphoreType.DMA((10,)),
         ],
         60,
         10**6,
@@ -602,12 +621,12 @@
         (HBM, cotangent),
         (HBM, frac.transpose(1, 0, 2)),
         (HBM, in_weight),
-        (HBM, atom_count.reshape(1, 1)),
     )
     evens = range(0, SLABS, 2)
     pairs = [(n, n + 1) for n in evens], [(n + 1, (n + 2) % SLABS) for n in evens]
     first_swap, second_swap = (
-        lax.ppermute(halo, "atom", [*pair, *((j, i) for i, j in pair)]) for pair in pairs
+        lax.ppermute(end, "atom", [*pair, *((j, i) for i, j in pair)])
+        for end, pair in zip(ends, pairs)
     )
     gathered = exchange(payload, "atom")
 
@@ -630,6 +649,7 @@
         ],
         20,
         EDGE_COST,
+        (SMEM, atom_count),
         (VMEM, halo),
         (VMEM, first_swap),
         (VMEM, second_swap),
@@ -663,6 +683,7 @@
         SPECTRUM_SCRATCH,
         20,
         10**10,
+        (SMEM, atom_count),
         (VMEM, gathered),
         (VMEM, folded),
         (VMEM, miller),
@@ -686,6 +707,7 @@
         [],
         16,
         10**6,
+        (SMEM, atom_count),
         (VMEM, exchange(sums, "atom")),
         (VMEM, halo),
         (VMEM, local),

time: 71.2 us -> 71.6 us (level)
  waiting for transfers between devices: 2.66 us -> 1.74 us
    all_to_all x1, waiting for transfers between devices: 2.65 us -> 1.74 us  [exchange(): return lax.all_to_all(x, axis, 0, 0)]
    ppermute x2, starting transfers between devices: 9.13 us -> 9.85 us  [shards(): lax.ppermute(end, 'atom', [*pair, *((j, i) for i, j in pair)])]
where the time goes in v8:
time: 71.6 us; the launch traced here: 71.2 us
  blocking collectives  40.6 us (57%)
  starting transfers between devices  13.5 us (19%)
  Pallas kernels  13.2 us (18%)
  waiting for transfers between devices  1.74 us (2%)
  between operations  1.45 us (2%)
    all_to_all x3, blocking collectives, exchange(): return lax.all_to_all(x, axis, 0, 0)  40.6 us
    pallas_call x7, Pallas kernels, call(): pl.pallas_call(kernel, out_shape=[shape for _, shape in outs], in_specs=[...  13.2 us
    ppermute x2, starting transfers between devices, shards(): lax.ppermute(end, 'atom', [*pair, *((j, i) for i, j in pair)])  9.85 us
    all_to_all x1, starting transfers between devices, exchange(): return lax.all_to_all(x, axis, 0, 0)  3.69 us
    all_to_all x1, waiting for transfers between devices, exchange(): return lax.all_to_all(x, axis, 0, 0)  1.74 us
  transfers between devices with their start and end apart: 3, of which 1 were waited for; matrix products, arithmetic and copies ran while one was open for 0% of the time, Pallas kernels for 11%

profile of v8, /device:TPU:1, one launch (start us, length us, event | category | flops | bytes accessed | tf_op | source)
XLA Modules:
  0.0 71.2 jit_solution(9320843009023327457)
XLA Ops:
  0.6 1.8 %shard_map.147 = (bf16[144,128]{1,0:T(8,128)(2,1)}, bf16[48,128]{1,0:T(8,128)(2,1)}, bf16[48,128]{1,0:T(8,128)(2,1)}, bf16[16,80,128]{2,1,0:T(8,128)(2,1)}) custom-call(bf16[1,128,128]{2,1,0:T(8,128)(2,1)} %feats_hbm.1, bf16[1,128,128]{2,1,0:T(8,128)(2,1)} %cot.1, f32[3,1,128]{2,1,0:T(1,128)} %bitcast.1, bf16[128,128]{1,0:T(8,128)(2,1)} %in_weight.1), custom_call_target="tpu_custom_call" | custom-call | flops 1000000 | bytes 65536 | tf_op jit(solution)/shard_map/pallas_call | solution.py:58
  2.4 2.6 %collective-permute-start = (bf16[48,128]{1,0:T(8,128)(2,1)}, bf16[48,128]{1,0:T(8,128)(2,1)S(1)}, u32[]{:S(2)}, u32[]{:S(2)}) collective-permute-start(bf16[48,128]{1,0:T(8,128)(2,1)} %get-tuple-element.18), channel_id=1, source_target_pairs={{0,1},{2,3},{4,5},{6,7},{8,9},{10,11},{12,13},{14,15},{1,0},{3,2},... | collective-permute-start | bytes 36872 | tf_op jit(solution)/shard_map/ppermute | solution.py:628
  5.0 7.3 %collective-permute-start.1 = (bf16[48,128]{1,0:T(8,128)(2,1)}, bf16[48,128]{1,0:T(8,128)(2,1)S(1)}, u32[]{:S(2)}, u32[]{:S(2)}) collective-permute-start(bf16[48,128]{1,0:T(8,128)(2,1)} %get-tuple-element.19), channel_id=1, source_target_pairs={{1,2},{3,4},{5,6},{7,8},{9,10},{11,12},{13,14},{15,0},{2,1},{4,3},... | collective-permute-start | bytes 36872 | tf_op jit(solution)/shard_map/ppermute | solution.py:628
  12.3 0.0 copy-start.6
  12.3 0.0 copy-start.7
  12.3 0.0 copy-start.8
  12.3 3.7 %all-to-all-start = ((bf16[16,80,128]{2,1,0:T(8,128)(2,1)}), bf16[16,80,128]{2,1,0:T(8,128)(2,1)S(1)}, u32[]{:S(2)}, u32[]{:S(2)}) async-start(bf16[16,80,128]{2,1,0:T(8,128)(2,1)} %get-tuple-element.16), calls=%async_computation | async-start | bytes 655360 | tf_op jit(solution)/shard_map/all_to_all | solution.py:579
  16.7 0.0 copy-start.9
  16.7 0.0 collective-permute-done.first_swap
  16.7 0.0 collective-permute-done.1.second_swap
  16.7 0.0 copy-done.1
  16.7 0.0 copy-done.2
  16.7 0.0 copy-done.3
  16.8 0.6 copy-done.9
  17.3 6.9 %shard_map.148 = (f32[512,128]{1,0:T(8,128)S(1)}, f32[128,128]{1,0:T(8,128)S(1)}) custom-call(s32[1]{0:T(128)S(6)} %copy.16.atom_count, bf16[144,128]{1,0:T(8,128)(2,1)S(1)} %copy-done.1, bf16[48,128]{1,0:T(8,128)(2,1)S(1)} %collective-permute-done.first_swap, bf16[48,128]{1,0:T(8,128)(2,1)S(1)} %collective-permute-done.1.second_swap, ...), custom_call_target="tpu_custom_call" | custom-call | flops 10000000000 | bytes 65536 | tf_op jit(solution)/shard_map/pallas_call | solution.py:58
  24.3 0.8 %shard_map.149.folded = f32[64,896]{1,0:T(8,128)S(1)} custom-call(s32[3,2048]{1,0:T(4,128)S(1)} %copy-done.4, f32[2048,128]{1,0:T(8,128)S(1)} %copy-done), custom_call_target="tpu_custom_call" | custom-call | flops 100000000 | bytes 65536 | tf_op jit(solution)/shard_map/pallas_call | solution.py:58
  25.1 1.7 %all-to-all-done.gathered = bf16[16,80,128]{2,1,0:T(8,128)(2,1)S(1)} async-done(((bf16[16,80,128]{2,1,0:T(8,128)(2,1)}), bf16[16,80,128]{2,1,0:T(8,128)(2,1)S(1)}, u32[]{:S(2)}, u32[]{:S(2)}) %all-to-all-start) | async-done | bytes 327712 | tf_op jit(solution)/shard_map/all_to_all | solution.py:579
  26.8 2.6 %shard_map.150 = (bf16[16,48,128]{2,1,0:T(8,128)(2,1)S(1)}, f32[16,8,128]{2,1,0:T(8,128)S(1)}) custom-call(s32[1]{0:T(128)S(6)} %copy.16.atom_count, bf16[16,80,128]{2,1,0:T(8,128)(2,1)S(1)} %all-to-all-done.gathered, f32[64,896]{1,0:T(8,128)S(1)} %shard_map.149.folded, s32[3,2048]{1,0:T(4,128)S(1)} %copy-done.4, f32[512,128]{1,0:T(8,128)S(1)} %get-tuple-element.22.early), custom_call_target="tpu_custom_call" | custom-call | flops 10000000000 | bytes 65536 | tf_op jit(solution)/shard_map/pallas_call | solution.py:58
  29.4 14.0 %all_to_all.20.sums = bf16[16,48,128]{2,1,0:T(8,128)(2,1)S(1)} all-to-all(bf16[16,48,128]{2,1,0:T(8,128)(2,1)S(1)} %get-tuple-element.23), channel_id=1, replica_groups=mesh['dp'=16,'atom'=16] {'dp'}, dimensions={0} | all-to-all | bytes 393216 | tf_op jit(solution)/shard_map/all_to_all | solution.py:579
  43.4 0.1 shard_map.151
  43.5 15.2 %all_to_all.21.sums = bf16[16,48,128]{2,1,0:T(8,128)(2,1)S(1)} all-to-all(bf16[16,48,128]{2,1,0:T(8,128)(2,1)S(1)} %shard_map.151), channel_id=1, replica_groups=mesh['dp'=16,'atom'=16] {'atom'}, dimensions={0} | all-to-all | bytes 393216 | tf_op jit(solution)/shard_map/all_to_all | solution.py:579
  58.7 0.2 shard_map.152
  58.9 11.4 %all_to_all.22.sums = bf16[16,48,128]{2,1,0:T(8,128)(2,1)S(1)} all-to-all(bf16[16,48,128]{2,1,0:T(8,128)(2,1)S(1)} %get-tuple-element.26), channel_id=1, replica_groups=mesh['dp'=16,'atom'=16] {'dp'}, dimensions={0} | all-to-all | bytes 393216 | tf_op jit(solution)/shard_map/all_to_all | solution.py:579
  70.3 0.9 %shard_map.153 = (bf16[1,128,128]{2,1,0:T(8,128)(2,1)}, f32[128,128]{1,0:T(8,128)}, f32[128,128]{1,0:T(8,128)}, f32[384,128]{1,0:T(8,128)}) custom-call(bf16[16,48,128]{2,1,0:T(8,128)(2,1)S(1)} %all_to_all.22.sums, f32[128,128]{1,0:T(8,128)S(1)} %get-tuple-element.27.field), custom_call_target="tpu_custom_call" | custom-call | flops 1000000 | bytes 65536 | tf_op jit(solution)/shard_map/pallas_call | solution.py:58
  (12 shorter events, 0.0 us)
Async XLA Ops:
  2.4 14.3 %collective-permute-start = (bf16[48,128]{1,0:T(8,128)(2,1)}, bf16[48,128]{1,0:T(8,128)(2,1)S(1)}, u32[]{:S(2)}, u32[]{:S(2)}) collective-permute-start(bf16[48,128]{1,0:T(8,128)(2,1)} %get-tuple-element.18), channel_id=1, source_target_pairs={{0,1},{2,3},{4,5},{6,7},{8,9},{10,11},{12,13},{14,15},{1,0},{3,2},... | collective-permute-start | bytes 36872 | tf_op jit(solution)/shard_map/ppermute | solution.py:628
  5.0 11.7 %collective-permute-start.1 = (bf16[48,128]{1,0:T(8,128)(2,1)}, bf16[48,128]{1,0:T(8,128)(2,1)S(1)}, u32[]{:S(2)}, u32[]{:S(2)}) collective-permute-start(bf16[48,128]{1,0:T(8,128)(2,1)} %get-tuple-element.19), channel_id=1, source_target_pairs={{1,2},{3,4},{5,6},{7,8},{9,10},{11,12},{13,14},{15,0},{2,1},{4,3},... | collective-permute-start | bytes 36872 | tf_op jit(solution)/shard_map/ppermute | solution.py:628
  12.3 4.4 %copy-start.1 = (bf16[144,128]{1,0:T(8,128)(2,1)S(1)}, bf16[144,128]{1,0:T(8,128)(2,1)}, u32[]{:S(2)}) copy-start(bf16[144,128]{1,0:T(8,128)(2,1)} %get-tuple-element.17.own) | copy-start | bytes 110596
  12.3 4.4 %copy-start.2 = (bf16[1,128,128]{2,1,0:T(8,128)(2,1)S(1)}, bf16[1,128,128]{2,1,0:T(8,128)(2,1)}, u32[]{:S(2)}) copy-start(bf16[1,128,128]{2,1,0:T(8,128)(2,1)} %cot.1) | copy-start | bytes 98308
  12.3 4.4 %copy-start.3 = (bf16[128,128]{1,0:T(8,128)(2,1)S(1)}, bf16[128,128]{1,0:T(8,128)(2,1)}, u32[]{:S(2)}) copy-start(bf16[128,128]{1,0:T(8,128)(2,1)} %in_weight.1) | copy-start | bytes 98308
  12.3 4.4 %copy-start.5 = (bf16[384,128]{1,0:T(8,128)(2,1)S(1)}, bf16[384,128]{1,0:T(8,128)(2,1)}, u32[]{:S(2)}) copy-start(bf16[384,128]{1,0:T(8,128)(2,1)} %out_weight.1) | copy-start | bytes 294916
  12.3 4.5 %copy-start.6 = (s32[1,32,128]{2,1,0:T(8,128)S(1)}, s32[1,32,128]{2,1,0:T(8,128)}, u32[]{:S(2)}) copy-start(s32[1,32,128]{2,1,0:T(8,128)} %neighbours.1) | copy-start | bytes 49156
  12.3 4.5 %copy-start.7 = (s32[1,32,128]{2,1,0:T(8,128)S(1)}, s32[1,32,128]{2,1,0:T(8,128)}, u32[]{:S(2)}) copy-start(s32[1,32,128]{2,1,0:T(8,128)} %images.1) | copy-start | bytes 49156
  12.3 4.4 %copy-start.8 = (f32[3,8,128]{2,1,0:T(8,128)S(1)}, f32[3,8,128]{2,1,0:T(8,128)}, u32[]{:S(2)}) copy-start(f32[3,8,128]{2,1,0:T(8,128)} %radial_weight.1) | copy-start | bytes 36868
  12.3 14.5 %all-to-all-start = ((bf16[16,80,128]{2,1,0:T(8,128)(2,1)}), bf16[16,80,128]{2,1,0:T(8,128)(2,1)S(1)}, u32[]{:S(2)}, u32[]{:S(2)}) async-start(bf16[16,80,128]{2,1,0:T(8,128)(2,1)} %get-tuple-element.16), calls=%async_computation | async-start | bytes 655360 | tf_op jit(solution)/shard_map/all_to_all | solution.py:579
  16.7 0.7 copy-start.9
  17.3 7.0 %copy-start = (f32[2048,128]{1,0:T(8,128)S(1)}, f32[2048,128]{1,0:T(8,128)}, u32[]{:S(2)}) copy-start(f32[2048,128]{1,0:T(8,128)} %filter_weight.1) | copy-start | bytes 3145732
  17.3 7.0 %copy-start.4 = (s32[3,2048]{1,0:T(4,128)S(1)}, s32[3,2048]{1,0:T(4,128)}, u32[]{:S(2)}) copy-start(s32[3,2048]{1,0:T(4,128)} %miller.1) | copy-start | bytes 73732

commit v9 on v7

--- a/solution.py
+++ b/solution.py
@@ -269,7 +269,7 @@
         ).astype(BF16)
         return carry
 
-    lax.fori_loop(0, CH // BAND, forward, 0)
+    lax.fori_loop(0, CH // BAND, forward, 0, unroll=2)
 
     masked = jnp.where(lane < live_here, cot[0].astype(F32), 0.0).astype(BF16)
     local[...] = dot(out_weight[...], inv[...], TN)
@@ -303,7 +303,7 @@
             pulled[pl.ds(top, BAND), here] = pull.astype(BF16)
         return carry
 
-    lax.fori_loop(0, CH // BAND, backward, 0)
+    lax.fori_loop(0, CH // BAND, backward, 0, unroll=2)
     back = dot(pulled[...], hot[...], NT)
     grad_in = dot(ext[...], back.astype(BF16), NT)
     for d in range(4):

time: 71.2 us -> 71.1 us (level)
  no operation moved by 1% of the time
where the time goes in v9:
time: 71.1 us; the launch traced here: 70.7 us
  blocking collectives  39.9 us (56%)
  starting transfers between devices  13.4 us (19%)
  Pallas kernels  13 us (18%)
  waiting for transfers between devices  2.78 us (4%)
  between operations  1.48 us (2%)
    all_to_all x3, blocking collectives, exchange(): return lax.all_to_all(x, axis, 0, 0)  39.9 us
    pallas_call x7, Pallas kernels, call(): pl.pallas_call(kernel, out_shape=[shape for _, shape in outs], in_specs=[...  13 us
    ppermute x2, starting transfers between devices, shards(): lax.ppermute(halo, 'atom', [*pair, *((j, i) for i, j in pair)])  9.13 us
    all_to_all x1, starting transfers between devices, exchange(): return lax.all_to_all(x, axis, 0, 0)  4.32 us
    all_to_all x1, waiting for transfers between devices, exchange(): return lax.all_to_all(x, axis, 0, 0)  2.77 us
  transfers between devices with their start and end apart: 3, of which 1 were waited for; matrix products, arithmetic and copies ran while one was open for 0% of the time, Pallas kernels for 11%

profile of v9, /device:TPU:1, one launch (start us, length us, event | category | flops | bytes accessed | tf_op | source)
XLA Modules:
  0.0 70.7 jit_solution(8578346471600218969)
XLA Ops:
  1.3 1.7 %shard_map.147 = (bf16[144,128]{1,0:T(8,128)(2,1)}, bf16[16,80,128]{2,1,0:T(8,128)(2,1)}) custom-call(bf16[1,128,128]{2,1,0:T(8,128)(2,1)} %feats_hbm.1, bf16[1,128,128]{2,1,0:T(8,128)(2,1)} %cot.1, f32[3,1,128]{2,1,0:T(1,128)} %bitcast.3, bf16[128,128]{1,0:T(8,128)(2,1)} %in_weight.1, s32[1,1]{1,0:T(1,128)} %bitcast.2.count_hbm), custom_call_target="tpu_custom_call" | custom-call | flops 1000000 | bytes 65536 | tf_op jit(solution)/shard_map/pallas_call | solution.py:56
  3.0 9.1 %collective-permute-start.1 = (bf16[144,128]{1,0:T(8,128)(2,1)}, bf16[144,128]{1,0:T(8,128)(2,1)S(1)}, u32[]{:S(2)}, u32[]{:S(2)}) collective-permute-start(bf16[144,128]{1,0:T(8,128)(2,1)} %get-tuple-element.15.own), channel_id=1, source_target_pairs={{1,2},{3,4},{5,6},{7,8},{9,10},{11,12},{13,14},{15,0},{2,1},{4,3},... | collective-permute-start | bytes 110600 | tf_op jit(solution)/shard_map/ppermute | solution.py:610
  12.1 0.0 collective-permute-start
  12.1 0.0 copy-start.5
  12.2 0.0 copy-start.6
  12.2 0.0 copy-start.7
  12.2 0.0 copy-start.8
  12.2 0.0 copy-start.9
  12.2 4.3 %all-to-all-start = ((bf16[16,80,128]{2,1,0:T(8,128)(2,1)}), bf16[16,80,128]{2,1,0:T(8,128)(2,1)S(1)}, u32[]{:S(2)}, u32[]{:S(2)}) async-start(bf16[16,80,128]{2,1,0:T(8,128)(2,1)} %get-tuple-element.14), calls=%async_computation | async-start | bytes 655360 | tf_op jit(solution)/shard_map/all_to_all | solution.py:563
  16.5 0.0 copy-start
  16.5 0.0 copy-start.4
  16.6 0.0 collective-permute-done.1.second_swap
  16.6 0.0 collective-permute-done.first_swap
  16.6 0.0 copy-done.1
  16.7 6.8 %shard_map.148 = (f32[512,128]{1,0:T(8,128)S(1)}, f32[128,128]{1,0:T(8,128)S(1)}) custom-call(bf16[144,128]{1,0:T(8,128)(2,1)S(1)} %copy-done.1, bf16[144,128]{1,0:T(8,128)(2,1)S(1)} %collective-permute-done.first_swap, bf16[144,128]{1,0:T(8,128)(2,1)S(1)} %collective-permute-done.1.second_swap, s32[1,32,128]{2,1,0:T(8,128)S(1)} %copy-done.6, ...), custom_call_target="tpu_custom_call" | custom-call | flops 10000000000 | bytes 65536 | tf_op jit(solution)/shard_map/pallas_call | solution.py:56
  23.4 0.8 %shard_map.149.folded = f32[64,896]{1,0:T(8,128)S(1)} custom-call(s32[3,2048]{1,0:T(4,128)S(1)} %copy-done.4, f32[2048,128]{1,0:T(8,128)S(1)} %copy-done), custom_call_target="tpu_custom_call" | custom-call | flops 100000000 | bytes 65536 | tf_op jit(solution)/shard_map/pallas_call | solution.py:56
  24.2 2.8 %all-to-all-done.gathered = bf16[16,80,128]{2,1,0:T(8,128)(2,1)S(1)} async-done(((bf16[16,80,128]{2,1,0:T(8,128)(2,1)}), bf16[16,80,128]{2,1,0:T(8,128)(2,1)S(1)}, u32[]{:S(2)}, u32[]{:S(2)}) %all-to-all-start) | async-done | bytes 327712 | tf_op jit(solution)/shard_map/all_to_all | solution.py:563
  27.0 2.6 %shard_map.150 = (bf16[16,48,128]{2,1,0:T(8,128)(2,1)S(1)}, f32[16,8,128]{2,1,0:T(8,128)S(1)}) custom-call(bf16[16,80,128]{2,1,0:T(8,128)(2,1)S(1)} %all-to-all-done.gathered, f32[64,896]{1,0:T(8,128)S(1)} %shard_map.149.folded, s32[3,2048]{1,0:T(4,128)S(1)} %copy-done.4, f32[512,128]{1,0:T(8,128)S(1)} %get-tuple-element.18.early), custom_call_target="tpu_custom_call" | custom-call | flops 10000000000 | bytes 65536 | tf_op jit(solution)/shard_map/pallas_call | solution.py:56
  29.6 14.3 %all_to_all.20.sums = bf16[16,48,128]{2,1,0:T(8,128)(2,1)S(1)} all-to-all(bf16[16,48,128]{2,1,0:T(8,128)(2,1)S(1)} %get-tuple-element.19), channel_id=1, replica_groups=mesh['dp'=16,'atom'=16] {'dp'}, dimensions={0} | all-to-all | bytes 393216 | tf_op jit(solution)/shard_map/all_to_all | solution.py:563
  43.9 0.1 shard_map.151
  44.0 14.2 %all_to_all.21.sums = bf16[16,48,128]{2,1,0:T(8,128)(2,1)S(1)} all-to-all(bf16[16,48,128]{2,1,0:T(8,128)(2,1)S(1)} %shard_map.151), channel_id=1, replica_groups=mesh['dp'=16,'atom'=16] {'atom'}, dimensions={0} | all-to-all | bytes 393216 | tf_op jit(solution)/shard_map/all_to_all | solution.py:563
  58.2 0.2 shard_map.152
  58.4 11.4 %all_to_all.22.sums = bf16[16,48,128]{2,1,0:T(8,128)(2,1)S(1)} all-to-all(bf16[16,48,128]{2,1,0:T(8,128)(2,1)S(1)} %get-tuple-element.22), channel_id=1, replica_groups=mesh['dp'=16,'atom'=16] {'dp'}, dimensions={0} | all-to-all | bytes 393216 | tf_op jit(solution)/shard_map/all_to_all | solution.py:563
  69.8 0.9 %shard_map.153 = (bf16[1,128,128]{2,1,0:T(8,128)(2,1)}, f32[128,128]{1,0:T(8,128)}, f32[128,128]{1,0:T(8,128)}, f32[384,128]{1,0:T(8,128)}) custom-call(bf16[16,48,128]{2,1,0:T(8,128)(2,1)S(1)} %all_to_all.22.sums, f32[128,128]{1,0:T(8,128)S(1)} %get-tuple-element.23.field), custom_call_target="tpu_custom_call" | custom-call | flops 1000000 | bytes 65536 | tf_op jit(solution)/shard_map/pallas_call | solution.py:56
  (12 shorter events, 0.0 us)
Async XLA Ops:
  3.0 13.6 %collective-permute-start.1 = (bf16[144,128]{1,0:T(8,128)(2,1)}, bf16[144,128]{1,0:T(8,128)(2,1)S(1)}, u32[]{:S(2)}, u32[]{:S(2)}) collective-permute-start(bf16[144,128]{1,0:T(8,128)(2,1)} %get-tuple-element.15.own), channel_id=1, source_target_pairs={{1,2},{3,4},{5,6},{7,8},{9,10},{11,12},{13,14},{15,0},{2,1},{4,3},... | collective-permute-start | bytes 110600 | tf_op jit(solution)/shard_map/ppermute | solution.py:610
  12.1 4.4 %collective-permute-start = (bf16[144,128]{1,0:T(8,128)(2,1)}, bf16[144,128]{1,0:T(8,128)(2,1)S(1)}, u32[]{:S(2)}, u32[]{:S(2)}) collective-permute-start(bf16[144,128]{1,0:T(8,128)(2,1)} %get-tuple-element.15.own), channel_id=1, source_target_pairs={{0,1},{2,3},{4,5},{6,7},{8,9},{10,11},{12,13},{14,15},{1,0},{3,2},... | collective-permute-start | bytes 110600 | tf_op jit(solution)/shard_map/ppermute | solution.py:610
  12.1 4.4 %copy-start.1 = (bf16[144,128]{1,0:T(8,128)(2,1)S(1)}, bf16[144,128]{1,0:T(8,128)(2,1)}, u32[]{:S(2)}) copy-start(bf16[144,128]{1,0:T(8,128)(2,1)} %get-tuple-element.15.own) | copy-start | bytes 110596
  12.1 4.5 %copy-start.2 = (bf16[1,128,128]{2,1,0:T(8,128)(2,1)S(1)}, bf16[1,128,128]{2,1,0:T(8,128)(2,1)}, u32[]{:S(2)}) copy-start(bf16[1,128,128]{2,1,0:T(8,128)(2,1)} %cot.1) | copy-start | bytes 98308
  12.1 4.5 %copy-start.3 = (bf16[128,128]{1,0:T(8,128)(2,1)S(1)}, bf16[128,128]{1,0:T(8,128)(2,1)}, u32[]{:S(2)}) copy-start(bf16[128,128]{1,0:T(8,128)(2,1)} %in_weight.1) | copy-start | bytes 98308
  12.1 4.5 %copy-start.5 = (bf16[384,128]{1,0:T(8,128)(2,1)S(1)}, bf16[384,128]{1,0:T(8,128)(2,1)}, u32[]{:S(2)}) copy-start(bf16[384,128]{1,0:T(8,128)(2,1)} %out_weight.1) | copy-start | bytes 294916
  12.2 4.5 %copy-start.6 = (s32[1,32,128]{2,1,0:T(8,128)S(1)}, s32[1,32,128]{2,1,0:T(8,128)}, u32[]{:S(2)}) copy-start(s32[1,32,128]{2,1,0:T(8,128)} %neighbours.1) | copy-start | bytes 49156
  12.2 4.5 %copy-start.7 = (s32[1,32,128]{2,1,0:T(8,128)S(1)}, s32[1,32,128]{2,1,0:T(8,128)}, u32[]{:S(2)}) copy-start(s32[1,32,128]{2,1,0:T(8,128)} %images.1) | copy-start | bytes 49156
  12.2 4.5 %copy-start.8 = (f32[3,8,128]{2,1,0:T(8,128)S(1)}, f32[3,8,128]{2,1,0:T(8,128)}, u32[]{:S(2)}) copy-start(f32[3,8,128]{2,1,0:T(8,128)} %radial_weight.1) | copy-start | bytes 36868
  12.2 4.5 %copy-start.9 = (s32[1,128]{1,0:T(1,128)S(1)}, s32[1,128]{1,0:T(1,128)}, u32[]{:S(2)}) copy-start(s32[1,128]{1,0:T(1,128)} %count.1) | copy-start | bytes 1540
  12.2 14.8 %all-to-all-start = ((bf16[16,80,128]{2,1,0:T(8,128)(2,1)}), bf16[16,80,128]{2,1,0:T(8,128)(2,1)S(1)}, u32[]{:S(2)}, u32[]{:S(2)}) async-start(bf16[16,80,128]{2,1,0:T(8,128)(2,1)} %get-tuple-element.14), calls=%async_computation | async-start | bytes 655360 | tf_op jit(solution)/shard_map/all_to_all | solution.py:563
  16.5 6.9 %copy-start = (f32[2048,128]{1,0:T(8,128)S(1)}, f32[2048,128]{1,0:T(8,128)}, u32[]{:S(2)}) copy-start(f32[2048,128]{1,0:T(8,128)} %filter_weight.1) | copy-start | bytes 3145732
  16.5 6.9 %copy-start.4 = (s32[3,2048]{1,0:T(4,128)S(1)}, s32[3,2048]{1,0:T(4,128)}, u32[]{:S(2)}) copy-start(s32[3,2048]{1,0:T(4,128)} %miller.1) | copy-start | bytes 73732
